TPU v7x, 128 devices: a whole 4x4x4 slice. The times are simulated.
128 devices in a mesh: dp: 1, seg: 16 (over y, x), head: 8 (over z, core).
Axes of the slice: x: 4, y: 4, z: 4, core: 2. Of those that a mesh axis runs over, the one named last changes fastest.
Arguments:
- inputs: bfloat16 [16384, 8192], P(('dp', 'seg', 'head')), may hold values from -6 to 6
- b_rows: bfloat16 [16384, 2048], P(('dp', 'seg', 'head')), may hold values from -0.375 to 0.375
- c_rows: bfloat16 [16384, 2048], P(('dp', 'seg', 'head')), may hold values from -0.375 to 0.375
- dt_rows: bfloat16 [16384, 128], P(('dp', 'seg', 'head')), may hold values from -1.5 to 1
- a_log: float32 [128], replicated, may hold values from -14 to -2, as said below
- d_skip: float32 [128], replicated, may hold values from 0.5 to 1.5
- grad_out: bfloat16 [16384, 8192], P(('dp', 'seg', 'head')), may hold values from -0.29882812 to 0.29882812
Outputs:
- outputs: bfloat16 [16384, 8192], P(('dp', 'seg', 'head'))
- grad_inputs: bfloat16 [16384, 8192], P(('dp', 'seg', 'head'))
- grad_b: bfloat16 [16384, 2048], P(('dp', 'seg', 'head'))
- grad_c: bfloat16 [16384, 2048], P(('dp', 'seg', 'head'))
- grad_dt: bfloat16 [16384, 128], P(('dp', 'seg', 'head'))
- grad_a_log: float32 [128], P(('dp', 'head'))
- grad_d_skip: float32 [128], P(('dp', 'head'))
Inputs may be any that keep to these rules, and one draw needn't show every extreme that they name: a_log lies between log(0.1 / 16384) and log(1 / 12).
All inputs are finite; a program needn't handle non-finite values.
Results may differ from a plain program's by a relative error of at most 0.0014.
Values may be sent and summed in bfloat16 or wider, within the bound.
No kernel may reach another device: no remote copies, remote signals or barrier semaphores. Data moves between devices by JAX's collectives and lax.ppermute only.
A program may use at most 384 MiB of HBM per device.

v0:
```python
import jax
import jax.numpy as jnp
from jax import lax
from jax.sharding import PartitionSpec as P

HEAD_DIM = 64
GSTATE = 256
BLOCK = 256


HIGH_ACCURACY = lax.Precision.HIGHEST


def prefix(value, axis, join, neutral, backward):
    count, mine = (lax.axis_size(axis), lax.axis_index(axis))
    pieces = jax.tree.map(lambda part: lax.all_gather(part, axis), value)
    if backward:
        pieces = jax.tree.map(lambda part: part[::-1], pieces)
        mine = count - 1 - mine
    so_far = jax.tree.map(
        lambda part, zero: jnp.full_like(part, 0) + jnp.asarray(zero, part.dtype), value, neutral
    )

    def hop(position, so_far):
        longer = join(so_far, jax.tree.map(lambda part: part[position], pieces))
        return jax.tree.map(lambda new, old: jnp.where(position < mine, new, old), longer, so_far)

    return lax.fori_loop(0, count - 1, hop, so_far)


def ssd_blocks(inputs, b_rows, c_rows, dt_rows, a_log, d_skip, state_init):
    head_count, head_width, state_width = state_init.shape
    groups = b_rows.shape[1] // state_width
    repeat = head_count // groups
    blocks = inputs.shape[0] // BLOCK
    x_blocks = inputs.reshape(blocks, BLOCK, groups, repeat, head_width)
    b_blocks = b_rows.reshape(blocks, BLOCK, groups, state_width)
    c_blocks = c_rows.reshape(blocks, BLOCK, groups, state_width)
    step_size_blocks = dt_rows.reshape(blocks, BLOCK, groups, repeat)
    decay_rate = jnp.exp(a_log).reshape(groups, repeat)
    skip_gain = d_skip.reshape(groups, repeat)
    causal = jnp.arange(BLOCK)[:, None] >= jnp.arange(BLOCK)[None, :]

    def advance(running, pieces):
        input_block, b_block, c_block, dt_block = pieces
        step_size = jax.nn.softplus(dt_block)
        cumulative = jnp.cumsum(-step_size * decay_rate, axis=0)
        along = jnp.moveaxis(cumulative, 0, -1)
        decay_gap = along[..., :, None] - along[..., None, :]
        mixing_weights = jnp.where(causal, jnp.exp(jnp.where(causal, decay_gap, 0.0)), 0.0)
        scores = jnp.einsum("tgn,sgn->gts", c_block, b_block, precision=HIGH_ACCURACY)
        mixing_weights = (
            mixing_weights * scores[:, None] * jnp.moveaxis(step_size, 0, -1)[..., None, :]
        )
        intra_block_part = jnp.einsum(
            "mlbn,nmlc->bmlc", mixing_weights, input_block, precision=HIGH_ACCURACY
        )
        carried_over = (
            jnp.einsum("tgn,grpn->tgrp", c_block, running, precision=HIGH_ACCURACY)
            * jnp.exp(cumulative)[..., None]
        )
        tail_weight = jnp.exp(cumulative[-1][None] - cumulative) * step_size
        fresh_state = jnp.einsum(
            "sgrp,sgn->grpn", input_block * tail_weight[..., None], b_block, precision=HIGH_ACCURACY
        )
        running = running * jnp.exp(cumulative[-1])[..., None, None] + fresh_state
        return (running, intra_block_part + carried_over + skip_gain[..., None] * input_block)

    running = state_init.reshape(groups, repeat, head_width, state_width)
    final_state, results = lax.scan(
        advance, running, (x_blocks, b_blocks, c_blocks, step_size_blocks)
    )
    return (results.reshape(inputs.shape), final_state.reshape(head_count, head_width, state_width))


def carry_in(c_in, dt_in, log_rate, start_state):
    seg_rows = c_in.shape[0]
    heads_here, head_width, state_width = start_state.shape
    groups_here = c_in.shape[1] // state_width
    repeat = heads_here // groups_here
    running_log = jnp.cumsum(-jax.nn.softplus(dt_in) * jnp.exp(log_rate), axis=0)
    carried_over = jnp.einsum(
        "tgn,grpn->tgrp",
        c_in.reshape(seg_rows, groups_here, state_width),
        start_state.reshape(groups_here, repeat, head_width, state_width),
        precision=HIGH_ACCURACY,
    )
    carried_over = (
        carried_over * jnp.exp(running_log).reshape(seg_rows, groups_here, repeat)[..., None]
    )
    return (
        carried_over.reshape(seg_rows, heads_here * head_width),
        jnp.exp(running_log[-1])[:, None, None] * start_state,
    )


def combine(earlier, later):
    return (earlier[0] * later[0], later[0][:, None, None] * earlier[1] + later[1])


def on_device(inputs, b_rows, c_rows, dt_rows, a_log, d_skip, grad_out):
    heads_here = dt_rows.shape[1] // lax.axis_size("head")
    head_start = lax.axis_index("head") * heads_here
    rate_here = lax.dynamic_slice_in_dim(a_log, head_start, heads_here, 0)
    skip_here = lax.dynamic_slice_in_dim(d_skip, head_start, heads_here, 0)
    x_seg, b_seg, c_seg, dt_seg, grad_seg = (
        lax.all_to_all(inputs, "head", split_axis=1, concat_axis=0, tiled=True),
        lax.all_to_all(b_rows, "head", split_axis=1, concat_axis=0, tiled=True),
        lax.all_to_all(c_rows, "head", split_axis=1, concat_axis=0, tiled=True),
        lax.all_to_all(dt_rows, "head", split_axis=1, concat_axis=0, tiled=True),
        lax.all_to_all(grad_out, "head", split_axis=1, concat_axis=0, tiled=True),
    )
    seg_rows = x_seg.shape[0]
    head_width = HEAD_DIM
    state_width = GSTATE
    groups_here = b_seg.shape[1] // state_width
    repeat = heads_here // groups_here
    x_float = x_seg.astype(jnp.float32)
    b_float = b_seg.astype(jnp.float32)
    c_float = c_seg.astype(jnp.float32)
    dt_float = dt_seg.astype(jnp.float32)
    zero_state = jnp.zeros((heads_here, head_width, state_width), jnp.float32)

    def forward(x_in, b_in, c_in, dt_in, log_rate, skip_gain):
        return ssd_blocks(x_in, b_in, c_in, dt_in, log_rate, skip_gain, zero_state)

    (local_results, block_local_state), pullback = jax.vjp(
        forward, x_float, b_float, c_float, dt_float, rate_here, skip_here
    )
    cumulative = jnp.cumsum(-jax.nn.softplus(dt_float) * jnp.exp(rate_here), axis=0)
    decay_total = jnp.exp(cumulative[-1])
    identity = (jnp.ones_like(decay_total), jnp.zeros_like(block_local_state))
    state_init = prefix((decay_total, block_local_state), "seg", combine, identity, False)[1]

    def correction(c_in, dt_in, log_rate):
        return carry_in(c_in, dt_in, log_rate, state_init)

    (carried_over, carried_state), carry_pullback = jax.vjp(
        correction, c_float, dt_float, rate_here
    )
    results = (local_results + carried_over).astype(jnp.bfloat16)
    grad_float = grad_seg.astype(jnp.float32)
    weighted = grad_float.reshape(seg_rows, heads_here, head_width) * jnp.exp(cumulative)[..., None]
    weighted = weighted.reshape(seg_rows, groups_here, repeat, head_width)
    start_grad = jnp.einsum(
        "tgrp,tgn->grpn",
        weighted,
        c_float.reshape(seg_rows, groups_here, state_width),
        precision=HIGH_ACCURACY,
    )
    start_grad = start_grad.reshape(heads_here, head_width, state_width)
    end_grad = prefix((decay_total, start_grad), "seg", combine, identity, True)[1]
    grads = pullback((grad_float, end_grad))
    carry_grads = carry_pullback((grad_float, end_grad))
    grad_rate, grad_skip = lax.psum((grads[4] + carry_grads[2], grads[5]), "seg")
    grad_x = grads[0].astype(jnp.bfloat16)
    grad_bproj = grads[1].astype(jnp.bfloat16)
    grad_cproj = (grads[2] + carry_grads[0]).astype(jnp.bfloat16)
    grad_step = (grads[3] + carry_grads[1]).astype(jnp.bfloat16)
    results_back, grad_x_back, grad_b_back, grad_c_back, grad_dt_back = (
        lax.all_to_all(results, "head", split_axis=0, concat_axis=1, tiled=True),
        lax.all_to_all(grad_x, "head", split_axis=0, concat_axis=1, tiled=True),
        lax.all_to_all(grad_bproj, "head", split_axis=0, concat_axis=1, tiled=True),
        lax.all_to_all(grad_cproj, "head", split_axis=0, concat_axis=1, tiled=True),
        lax.all_to_all(grad_step, "head", split_axis=0, concat_axis=1, tiled=True),
    )
    return (results_back, grad_x_back, grad_b_back, grad_c_back, grad_dt_back, grad_rate, grad_skip)


def solution(mesh):
    in_specs = (
        P(("dp", "seg", "head"), None),
        P(("dp", "seg", "head"), None),
        P(("dp", "seg", "head"), None),
        P(("dp", "seg", "head"), None),
        P(),
        P(),
        P(("dp", "seg", "head"), None),
    )
    out_specs = (
        P(("dp", "seg", "head"), None),
        P(("dp", "seg", "head"), None),
        P(("dp", "seg", "head"), None),
        P(("dp", "seg", "head"), None),
        P(("dp", "seg", "head"), None),
        P(("dp", "head")),
        P(("dp", "head")),
    )
    return jax.shard_map(
        on_device, mesh=mesh, in_specs=in_specs, out_specs=out_specs, check_vma=False
    )
```

profile of v0, /device:TPU:0, one launch (start us, length us, event | category | flops | bytes accessed | tf_op | source)
XLA Modules:
  0.0 982.9 jit_solution(12921092813921279639)
XLA Ops:
  25.0 8.4 all-to-all-done.3
  39.4 7.8 all-to-all-done.2
  55.4 23.3 %all-to-all-done.1 = bf16[128,8,1024]{0,2,1:T(8,128)(2,1)} async-done(((bf16[128,8,1024]{0,2,1:T(8,128)(2,1)}), bf16[128,8,1024]{0,2,1:T(8,128)(2,1)}, u32[]{:S(2)}, u32[]{:S(2)}) %all-to-all-start.1) | async-done | bytes 2097184 | tf_op jit(solution)/shard_map/all_to_all | solution.py:107
  98.2 233.1 %while.115 = (s32[]{:T(128)}, f32[1,16,64,256]{3,2,1,0:T(8,128)S(1)}, f32[4,256,1,16,64]{1,0,4,3,2:T(4,128)}, f32[4,256,1,16]{1,2,3,0:T(1,128)S(1)}, f32[4,256,1...) while((s32[]{:T(128)}, ...), condition=%wide.region_3.4_spmd.clone.clone.clone, body=%wide.region_0.3_spmd.clone.clone.sunk.clone | while | flops 2631237632 | bytes 38744280 | solution.py:70
  102.2 6.7 multiply_dynamic-update-slice_fusion.6
  120.2 23.4 %dynamic_update_slice.273 = f32[4,256,1,16,64]{1,0,4,3,2:T(4,128)} dynamic-update-slice(f32[4,256,1,16,64]{1,0,4,3,2:T(4,128)} %get-tuple-element.2871, f32[1,256,1,16,64]{1,0,4,3,2:T(1,128)S(1)} %copy.483, s32[]{:T(128)} %get-tuple-element.2869, s32[]{:T(128)} %constant.233.clone.1..sunk.6, s32[]{:T(128)} %constant.233.clone.1..sunk.6, s32[]{:T(128)} %constant.233.clone.1..sunk.6, ...) | dynamic-update-slice | bytes 2097156 | tf_op jit(solution)/shard_map/jvp()/while/body/jit(dynamic_update_index_in_dim)/dynamic_update_slice | solution.py:70
  159.6 6.7 multiply_dynamic-update-slice_fusion.6
  170.0 6.6 fusion.276
  177.6 23.4 %dynamic_update_slice.273 = f32[4,256,1,16,64]{1,0,4,3,2:T(4,128)} dynamic-update-slice(f32[4,256,1,16,64]{1,0,4,3,2:T(4,128)} %get-tuple-element.2871, f32[1,256,1,16,64]{1,0,4,3,2:T(1,128)S(1)} %copy.483, s32[]{:T(128)} %get-tuple-element.2869, s32[]{:T(128)} %constant.233.clone.1..sunk.6, s32[]{:T(128)} %constant.233.clone.1..sunk.6, s32[]{:T(128)} %constant.233.clone.1..sunk.6, ...) | dynamic-update-slice | bytes 2097156 | tf_op jit(solution)/shard_map/jvp()/while/body/jit(dynamic_update_index_in_dim)/dynamic_update_slice | solution.py:70
  218.1 6.7 multiply_dynamic-update-slice_fusion.6
  236.1 23.4 %dynamic_update_slice.273 = f32[4,256,1,16,64]{1,0,4,3,2:T(4,128)} dynamic-update-slice(f32[4,256,1,16,64]{1,0,4,3,2:T(4,128)} %get-tuple-element.2871, f32[1,256,1,16,64]{1,0,4,3,2:T(1,128)S(1)} %copy.483, s32[]{:T(128)} %get-tuple-element.2869, s32[]{:T(128)} %constant.233.clone.1..sunk.6, s32[]{:T(128)} %constant.233.clone.1..sunk.6, s32[]{:T(128)} %constant.233.clone.1..sunk.6, ...) | dynamic-update-slice | bytes 2097156 | tf_op jit(solution)/shard_map/jvp()/while/body/jit(dynamic_update_index_in_dim)/dynamic_update_slice | solution.py:70
  276.6 6.7 multiply_dynamic-update-slice_fusion.6
  294.6 23.4 %dynamic_update_slice.273 = f32[4,256,1,16,64]{1,0,4,3,2:T(4,128)} dynamic-update-slice(f32[4,256,1,16,64]{1,0,4,3,2:T(4,128)} %get-tuple-element.2871, f32[1,256,1,16,64]{1,0,4,3,2:T(1,128)S(1)} %copy.483, s32[]{:T(128)} %get-tuple-element.2869, s32[]{:T(128)} %constant.233.clone.1..sunk.6, s32[]{:T(128)} %constant.233.clone.1..sunk.6, s32[]{:T(128)} %constant.233.clone.1..sunk.6, ...) | dynamic-update-slice | bytes 2097156 | tf_op jit(solution)/shard_map/jvp()/while/body/jit(dynamic_update_index_in_dim)/dynamic_update_slice | solution.py:70
  349.0 18.1 %all-to-all-done.5 = bf16[128,8,1024]{0,2,1:T(8,128)(2,1)S(1)} async-done(((bf16[128,8,1024]{0,2,1:T(8,128)(2,1)}), bf16[128,8,1024]{0,2,1:T(8,128)(2,1)S(1)}, u32[]{:S(2)}, u32[]{:S(2)}) %all-to-all-start.5) | async-done | bytes 2097184 | tf_op jit(solution)/shard_map/all_to_all | solution.py:111
  367.1 7.1 bitcast_multiply_fusion.15
  387.0 21.0 %all-gather.1 = f32[16,1,16]{2,1,0:T(1,128)S(1)} all-gather(f32[1,1,16]{2,1,0:T(1,128)S(1)} %bitcast.1010), channel_id=1, replica_groups=mesh['dp'=1,'seg'=16,'head'=8] {'seg'}, dimensions={0}, use_global_device_ids=true | all-gather | bytes 1088 | tf_op jit(solution)/shard_map/all_gather | solution.py:16
  423.3 19.9 %all-gather.5.cloned.1.call-done = f32[16,16,64,256]{3,2,1,0:T(8,128)} async-done(((f32[1,16,64,256]{3,2,1,0:T(8,128)}), f32[16,16,64,256]{3,2,1,0:T(8,128)}) %all-gather.5.cloned.1.call-update) | async-done | bytes 16777232 | tf_op jit(solution)/shard_map/all_gather | solution.py:16
  443.2 22.8 %while.113 = (s32[]{:T(128)}, f32[16,64,256]{2,1,0:T(8,128)S(1)}, s32[]{:T(128)}, f32[16,16]{1,0:T(8,128)S(1)}, f32[16,16,64,256]{3,2,1,0:T(8,128)}) while((s32[]{:T(128)}, f32[16,64,256]{2,1,0:T(8,128)S(1)}, s32[]{:T(128)}, f32[16,16]{1,0:T(8,128)S(1)}, f32[16,16,64,256]{3,2,1,0:T(8,128)}) %tuple.256), condition=%wide.region_7.8_spmd.clone.clone, body=%wide.region_6.7_spmd.clone.sunk.clone | while | flops 1048580 | bytes 3146009 | solution.py:28
  466.0 90.2 %all-gather.7.cloned.1.call-done = f32[256,64,256]{2,1,0:T(8,128)} async-done(((f32[16,64,256]{2,1,0:T(8,128)}), f32[256,64,256]{2,1,0:T(8,128)}) %all-gather.7.cloned.1.call-update) | async-done | bytes 16777232 | tf_op jit(solution)/shard_map/all_gather | solution.py:16
  556.2 11.7 %rev.7 = f32[16,16,64,256]{3,2,1,0:T(8,128)} reverse(f32[16,16,64,256]{3,2,1,0:T(8,128)} %bitcast.956), dimensions={0} | reverse | bytes 33554432 | tf_op jit(solution)/shard_map/rev | solution.py:18
  567.9 22.5 %while.114 = (s32[]{:T(128)}, f32[16,64,256]{2,1,0:T(8,128)S(1)}, s32[]{:T(128)}, f32[16,16]{1,0:T(8,128)S(1)}, f32[16,16,64,256]{3,2,1,0:T(8,128)}) while((s32[]{:T(128)}, f32[16,64,256]{2,1,0:T(8,128)S(1)}, s32[]{:T(128)}, f32[16,16]{1,0:T(8,128)S(1)}, f32[16,16,64,256]{3,2,1,0:T(8,128)}) %tuple.243), condition=%wide.region_9.10_spmd.clone.clone, body=%wide.region_8.9_spmd.clone.sunk.clone | while | flops 1048580 | bytes 3146009 | solution.py:28
  590.8 7.8 fusion.159
  598.7 19.8 %reduce-window.58 = f32[16,8,128]{2,1,0:T(8,128)S(1)} reduce-window(f32[16,8,128]{2,1,0:T(8,128)S(1)} %bitcast.996, f32[]{:T(128)} %constant.234.clone.1), window={size=1x1x128 pad=0_0x0_0x0_127}, to_apply=%region_26.27 | reduce-window | flops 2080768 | bytes 131076 | tf_op jit(solution)/shard_map/reduce-window.2
  621.2 222.3 %while.116 = (s32[]{:T(128)}, f32[1,16]{1,0:T(1,128)}, f32[1,16]{1,0:T(1,128)}, f32[1,16,64,256]{3,2,1,0:T(8,128)S(1)}, bf16[4,256,1,16,64]{1,4,3,2,0:T(8,128)(2...) while((s32[]{:T(128)}, f32[1,16]{1,0:T(1,128)}, ...), condition=%wide.region_23.24_spmd.clone.clone.clone, body=%wide.region_10.23_spmd.clone.clone.sunk.clone | while | flops 5250875392 | bytes 62415456 | solution.py:70
  636.1 9.5 fusion.290
  691.1 9.5 fusion.290
  746.8 9.5 fusion.290
  802.4 9.5 fusion.290
  850.5 10.1 %fusion.166 = bf16[8,128,256]{2,1,0:T(8,128)(2,1)} fusion(f32[8,128,256]{2,1,0:T(8,128)} %bitcast.965, f32[16,8,8,8,128]{4,3,2,1,0:T(8,128)} %get-tuple-element.2132, f32[16,64,256]{2,1,0:T(8,128)S(1)} %get-tuple-element.1251), kind=kOutput, calls=%fused_computation.236 | convolution fusion | flops 3221749760 | bytes 6815744 | tf_op jit(solution)/shard_map/transpose(jvp(tgn,grpn->tgrp))/dot_general | solution.py:82
  860.6 15.3 %all_to_all.151 = bf16[8,128,256]{2,1,0:T(8,128)(2,1)} all-to-all(bf16[8,128,256]{2,1,0:T(8,128)(2,1)} %fusion.166), channel_id=1, replica_groups=mesh['dp'=1,'seg'=16,'head'=8] {'head'}, dimensions={0} | all-to-all | bytes 1048576 | tf_op jit(solution)/shard_map/all_to_all | solution.py:164
  905.0 16.1 %all-to-all-done.6 = bf16[8,128,1024]{1,2,0:T(8,128)(2,1)S(1)} async-done(((bf16[8,128,1024]{1,2,0:T(8,128)(2,1)}), bf16[8,128,1024]{1,2,0:T(8,128)(2,1)S(1)}, u32[]{:S(2)}, u32[]{:S(2)}) %all-to-all-start.6) | async-done | bytes 2097184 | tf_op jit(solution)/shard_map/all_to_all | solution.py:162
  925.6 38.9 %all-reduce.3 = (f32[16]{0:T(128)}, f32[16]{0:T(128)}) all-reduce(f32[16]{0:T(128)S(1)} %fusion.187, f32[16]{0:T(128)S(1)} %bitcast.1008), channel_id=1, replica_groups=mesh['dp'=1,'seg'=16,'head'=8] {'seg'}, use_global_device_ids=true, to_apply=%region_29.30 | all-reduce | flops 32 | bytes 256 | tf_op jit(solution)/shard_map/psum | solution.py:155
  (502 shorter events, 485.3 us)
Async XLA Ops:
  7.2 44.6 %copy-start = (f32[128]{0:T(128)S(1)}, f32[128]{0:T(128)}, u32[]{:S(2)}) copy-start(f32[128]{0:T(128)} %param.20) | copy-start | bytes 1540
  7.2 29.8 %copy-start.8 = (bf16[128,8192]{1,0:T(8,128)(2,1)S(1)}, bf16[128,8192]{1,0:T(8,128)(2,1)}, u32[]{:S(2)}) copy-start(bf16[128,8192]{1,0:T(8,128)(2,1)} %param.15) | copy-start | bytes 6291460
  8.8 10.8 %all-to-all-start = ((bf16[128,8,16]{0,2,1:T(8,128)(2,1)}), bf16[128,8,16]{0,2,1:T(8,128)(2,1)S(1)}, u32[]{:S(2)}, u32[]{:S(2)}) async-start(bf16[128,8,16]{0,2,1:T(8,128)(2,1)} %bitcast), calls=%async_computation | async-start | bytes 65536 | tf_op jit(solution)/shard_map/all_to_all | solution.py:110
  19.7 13.8 %all-to-all-start.3 = ((bf16[128,8,256]{2,0,1:T(8,128)(2,1)}), bf16[128,8,256]{2,0,1:T(8,128)(2,1)S(1)}, u32[]{:S(2)}, u32[]{:S(2)}) async-start(bf16[128,8,256]{2,0,1:T(8,128)(2,1)} %bitcast.645), calls=%async_computation.3 | async-start | bytes 1048576 | tf_op jit(solution)/shard_map/all_to_all | solution.py:109
  33.4 13.8 %all-to-all-start.2 = ((bf16[128,8,256]{2,0,1:T(8,128)(2,1)}), bf16[128,8,256]{2,0,1:T(8,128)(2,1)S(1)}, u32[]{:S(2)}, u32[]{:S(2)}) async-start(bf16[128,8,256]{2,0,1:T(8,128)(2,1)} %bitcast.974), calls=%async_computation.2 | async-start | bytes 1048576 | tf_op jit(solution)/shard_map/all_to_all | solution.py:108
  36.9 15.5 %copy-start.16 = (f32[128]{0:T(128)S(1)}, f32[128]{0:T(128)}, u32[]{:S(2)}) copy-start(f32[128]{0:T(128)} %param.19) | copy-start | bytes 1540
  47.2 31.5 %all-to-all-start.1 = ((bf16[128,8,1024]{0,2,1:T(8,128)(2,1)}), bf16[128,8,1024]{0,2,1:T(8,128)(2,1)}, u32[]{:S(2)}, u32[]{:S(2)}) async-start(bf16[128,8,1024]{0,2,1:T(8,128)(2,1)} %bitcast.3), calls=%async_computation.1 | async-start | bytes 4194304 | tf_op jit(solution)/shard_map/all_to_all | solution.py:107
  51.5 391.6 %all-gather.5.cloned.1.call-start = ((), (), s32[]{:S(2)}) async-start(), calls=%async_computation.10 | async-start | bytes 17825792 | tf_op jit(solution)/shard_map/all_gather | solution.py:16
  53.1 286.9 %copy-start.10 = (f32[8,2,8,128]{3,2,1,0:T(8,128)}, f32[8,2,8,128]{3,2,1,0:T(8,128)S(1)}, u32[]{:S(2)}) copy-start(f32[8,2,8,128]{3,2,1,0:T(8,128)S(1)} %get-tuple-element.2135) | copy-start | bytes 196612
  336.3 30.8 %all-to-all-start.5 = ((bf16[128,8,1024]{0,2,1:T(8,128)(2,1)}), bf16[128,8,1024]{0,2,1:T(8,128)(2,1)S(1)}, u32[]{:S(2)}, u32[]{:S(2)}) async-start(bf16[128,8,1024]{0,2,1:T(8,128)(2,1)} %bitcast.962), calls=%async_computation.5 | async-start | bytes 4194304 | tf_op jit(solution)/shard_map/all_to_all | solution.py:111
  339.9 216.2 %all-gather.7.cloned.1.call-start = ((), (), s32[]{:S(2)}) async-start(), calls=%async_computation.11 | async-start | bytes 17825792 | tf_op jit(solution)/shard_map/all_gather | solution.py:16
  340.1 5.0 copy-start.15
  367.1 7.1 copy-start.3
  621.3 3.5 copy-start.11
  621.3 7.7 copy-start.5
  668.2 8.1 copy-start.12
  676.4 7.7 copy-start.5
  723.9 8.1 copy-start.12
  732.0 7.7 copy-start.5
  779.6 8.1 copy-start.12
  787.6 7.7 copy-start.5
  835.2 8.1 copy-start.12
  846.0 14.6 %all-to-all-start.9 = ((bf16[8,128,16]{1,2,0:T(8,128)(2,1)}), bf16[8,128,16]{1,2,0:T(8,128)(2,1)S(1)}, u32[]{:S(2)}, u32[]{:S(2)}) async-start(bf16[8,128,16]{1,2,0:T(8,128)(2,1)} %bitcast.649), calls=%async_computation.9 | async-start | bytes 65536 | tf_op jit(solution)/shard_map/all_to_all | solution.py:165
  850.5 29.6 %copy-start.7 = (bf16[4,256,1,16,64]{1,4,3,2,0:T(8,128)(2,1)S(1)}, bf16[4,256,1,16,64]{1,4,3,2,0:T(8,128)(2,1)}, u32[]{:S(2)}) copy-start(bf16[4,256,1,16,64]{1,4,3,2,0:T(8,128)(2,1)} %get-tuple-element.1271) | copy-start | bytes 6291460
  875.9 14.5 %all-to-all-start.7 = ((bf16[8,128,256]{2,1,0:T(8,128)(2,1)}), bf16[8,128,256]{2,1,0:T(8,128)(2,1)}, u32[]{:S(2)}, u32[]{:S(2)}) async-start(bf16[8,128,256]{2,1,0:T(8,128)(2,1)} %bitcast.972), calls=%async_computation.7 | async-start | bytes 1048576 | tf_op jit(solution)/shard_map/all_to_all | solution.py:163
  890.4 30.7 %all-to-all-start.6 = ((bf16[8,128,1024]{1,2,0:T(8,128)(2,1)}), bf16[8,128,1024]{1,2,0:T(8,128)(2,1)S(1)}, u32[]{:S(2)}, u32[]{:S(2)}) async-start(bf16[8,128,1024]{1,2,0:T(8,128)(2,1)} %copy.238), calls=%async_computation.6 | async-start | bytes 4194304 | tf_op jit(solution)/shard_map/all_to_all | solution.py:162
  903.3 22.2 %copy-start.13 = (f32[1,16]{1,0:T(1,128)S(1)}, f32[1,16]{1,0:T(1,128)}, u32[]{:S(2)}) copy-start(f32[1,16]{1,0:T(1,128)} %get-tuple-element.1275) | copy-start | bytes 196
  903.3 22.2 %copy-start.17 = (f32[128]{0:T(128)S(1)}, f32[128]{0:T(128)}, u32[]{:S(2)}) copy-start(f32[128]{0:T(128)} %param.19) | copy-start | bytes 1540
  903.4 22.2 %copy-start.14 = (f32[1,16]{1,0:T(1,128)S(1)}, f32[1,16]{1,0:T(1,128)}, u32[]{:S(2)}) copy-start(f32[1,16]{1,0:T(1,128)} %get-tuple-element.1276) | copy-start | bytes 196
  903.4 61.9 %copy-start.9 = (bf16[8,128,256]{2,1,0:T(8,128)(2,1)S(1)}, bf16[8,128,256]{2,1,0:T(8,128)(2,1)}, u32[]{:S(2)}) copy-start(bf16[8,128,256]{2,1,0:T(8,128)(2,1)} %all_to_all.151) | copy-start | bytes 1572868
  921.1 50.7 %all-to-all-start.4 = ((bf16[8,128,1024]{1,2,0:T(8,128)(2,1)}), bf16[8,128,1024]{1,2,0:T(8,128)(2,1)}, u32[]{:S(2)}, u32[]{:S(2)}) async-start(bf16[8,128,1024]{1,2,0:T(8,128)(2,1)} %copy.223), calls=%async_computation.4 | async-start | bytes 4194304 | tf_op jit(solution)/shard_map/all_to_all | solution.py:161
  968.9 7.0 copy-start.1
  (9 other events, 23.0 us)
Sparse Core Ops, SparseCore 0:
  332.4 110.7 all-gather.4
  445.3 110.8 all-gather.6
where the time goes:
time: 998 us; the launch traced here: 983 us
  local copies, waits for them, and re-layouts  271 us (27%)
  matrix products  205 us (21%)
  waiting for transfers between devices  190 us (19%)
  other arithmetic  188 us (19%)
  blocking collectives  75.2 us (8%)
  starting transfers between devices  36.9 us (4%)
  between operations  14.8 us (1%)
    dynamic_update_slice x28, local copies, waits for them, and re-layouts, ssd_blocks(): lax.scan(advance, running, (x_blocks, b_blocks, c_blocks, step_size_blocks))  121 us
    all_gather x2, waiting for transfers between devices, prefix(): pieces = jax.tree.map(lambda part: lax.all_gather(part, axis), value)  110 us
    dot_general x12, matrix products, advance(): jnp.einsum('mlbn,nmlc->bmlc', mixing_weights, input_block, precision=HIGH...  84.2 us
    dynamic_update_slice x28, other arithmetic, ssd_blocks(): lax.scan(advance, running, (x_blocks, b_blocks, c_blocks, step_size_blocks))  51.3 us
    another operation x43, other arithmetic  46.7 us
    select_n x30, other arithmetic, hop(): jnp.where(position < mine, new, old)  44.2 us
    dot_general x12, matrix products, advance(): jnp.einsum('sgrp,sgn->grpn', input_block * tail_weight[..., None], b_bloc...  40.4 us
    psum x1, blocking collectives, on_device(): lax.psum((grads[4] + carry_grads[2], grads[5]), 'seg')  38.9 us
  transfers between devices with their start and end apart: 11, of which 9 were waited for; matrix products, arithmetic and copies ran while one was open for 12% of the time, Pallas kernels for 0%

commit v1 on v0

v1 whole, which is shorter than its diff:
```python
import jax
import jax.numpy as jnp
from jax import lax
from jax.experimental import pallas as pl
from jax.experimental.pallas import tpu as pltpu
from jax.sharding import PartitionSpec as P

HEAD_DIM = 64
GSTATE = 256
BLOCK = 256
LANES = 128
VMEM_BYTES = 52 * 1024 * 1024

F32 = jnp.float32
BF16 = jnp.bfloat16


def dot(left, right):
    return lax.dot_general(left, right, (((1,), (0,)), ((), ())), preferred_element_type=F32)


def dot_nt(left, right):
    return lax.dot_general(left, right, (((1,), (1,)), ((), ())), preferred_element_type=F32)


def split2(value):
    high = value.astype(BF16)
    return high, (value - high.astype(F32)).astype(BF16)


def split3(value):
    high, rest = value.astype(BF16), None
    rest = value - high.astype(F32)
    middle = rest.astype(BF16)
    return high, middle, (rest - middle.astype(F32)).astype(BF16)


def dot3(ones, value):
    high, middle, low = split3(value)
    return dot(ones, high) + dot(ones, middle) + dot(ones, low)


def iota(shape, dim):
    return lax.broadcasted_iota(jnp.int32, shape, dim)


def step_sizes(dt_ref, rate_ref):
    dt = dt_ref[...].astype(F32)
    step = jnp.log(1.0 + jnp.exp(dt))
    log_decay = -step * rate_ref[...]
    lower = (iota((BLOCK, BLOCK), 0) >= iota((BLOCK, BLOCK), 1)).astype(BF16)
    return dt, step, log_decay, dot3(lower, log_decay)


def spread(value, heads, expand_ref):
    high, middle, low = split3(value)
    lane = iota(value.shape, 1)
    terms = jnp.where(lane < heads, high, jnp.where(lane < 2 * heads, middle, low))
    return dot(terms, expand_ref[...])


def gather_heads(value, collect_ref):
    high, low = split2(value)
    return dot(high, collect_ref[...]) + dot(low, collect_ref[...])


def state_kernel(heads, x_ref, b_ref, dt_ref, rate_ref, expand_ref, out_ref):
    @pl.when(pl.program_id(0) == 0)
    def _():
        out_ref[...] = jnp.zeros_like(out_ref)

    _, step, _, cumulative = step_sizes(dt_ref, rate_ref)
    weight = spread(jnp.exp(-cumulative) * step, heads, expand_ref)
    decay = spread(jnp.exp(cumulative[BLOCK - 8 :]), heads, expand_ref)[7:8]
    x_high, x_low = split2(x_ref[...].astype(F32) * weight)
    b_t = b_ref[...].T
    out_ref[...] = (out_ref[...] + dot(b_t, x_high) + dot(b_t, x_low)) * decay


def grad_state_kernel(heads, dy_ref, c_ref, dt_ref, rate_ref, expand_ref, out_ref):
    @pl.when(pl.program_id(0) == 0)
    def _():
        out_ref[...] = jnp.zeros_like(out_ref)

    _, _, _, cumulative = step_sizes(dt_ref, rate_ref)
    growth = spread(jnp.exp(cumulative), heads, expand_ref)
    dy_high, dy_low = split2(dy_ref[...].astype(F32) * growth)
    c_t = c_ref[...].T
    out_ref[...] = out_ref[...] * growth[BLOCK - 1 :] + dot(c_t, dy_high) + dot(c_t, dy_low)


def forward_kernel(
    heads, x_ref, b_ref, dt_ref, dy_ref, c_ref, start_ref, rate_ref, skip_ref, expand_ref, collect_ref,
    out_ref, states_ref, mixed_ref, dots_ref, skip_grad_ref, running,
):
    @pl.when(pl.program_id(0) == 0)
    def _():
        running[...] = start_ref[...]
        skip_grad_ref[...] = jnp.zeros_like(skip_grad_ref)

    channels = x_ref.shape[1]
    _, step, _, cumulative = step_sizes(dt_ref, rate_ref)
    growth = spread(jnp.exp(cumulative), heads, expand_ref)
    weight = spread(jnp.exp(-cumulative) * step, heads, expand_ref)
    x = x_ref[...].astype(F32)
    dy = dy_ref[...].astype(F32)
    b, c = b_ref[...], c_ref[...]
    state = running[...]
    states_ref[...] = state
    s_high, s_low = split2(state)
    x_high, x_low = split2(x * weight)
    causal = iota((BLOCK, BLOCK), 0) >= iota((BLOCK, BLOCK), 1)
    k_high, k_low = split2(jnp.where(causal, dot_nt(c, b), 0.0))
    inner = dot(k_high, x_high) + dot(k_high, x_low) + dot(k_low, x_high)
    inner = (inner + dot(c, s_high) + dot(c, s_low)) * growth
    out_ref[:, :channels] = (inner + skip_ref[...] * x).astype(BF16)
    dots_ref[...] = gather_heads(dy * inner, collect_ref)
    skip_grad_ref[...] += jnp.sum(dy * x, axis=0, keepdims=True)
    d_high, d_low = split2(dy * growth)
    mixed = dot_nt(d_high, x_high) + dot_nt(d_high, x_low) + dot_nt(d_low, x_high)
    mixed = jnp.where(causal, mixed, 0.0)
    mixed_ref[...] = mixed
    q_high, q_low = split2(mixed)
    grad_c = dot(q_high, b) + dot(q_low, b)
    grad_c = grad_c + dot_nt(d_high, s_high) + dot_nt(d_high, s_low) + dot_nt(d_low, s_high)
    out_ref[:, channels:] = grad_c.astype(BF16)
    b_t = b.T
    running[...] = (state + dot(b_t, x_high) + dot(b_t, x_low)) * growth[BLOCK - 1 :]


def backward_kernel(
    heads, x_ref, b_ref, dt_ref, dy_ref, c_ref, end_ref, states_ref, mixed_ref, dots_ref, rate_ref, skip_ref,
    expand_ref, collect_ref, out_ref, rate_grad_ref, running,
):
    @pl.when(pl.program_id(0) == 0)
    def _():
        running[...] = end_ref[...]
        rate_grad_ref[...] = jnp.zeros_like(rate_grad_ref)

    channels = x_ref.shape[1]
    width = b_ref.shape[1]
    dt, step, log_decay, cumulative = step_sizes(dt_ref, rate_ref)
    growth = spread(jnp.exp(cumulative), heads, expand_ref)
    weight = spread(jnp.exp(-cumulative) * step, heads, expand_ref)
    dy = dy_ref[...].astype(F32)
    b, c = b_ref[...], c_ref[...]
    scaled = x_ref[...].astype(F32) * weight
    x_high, x_low = split2(scaled)
    d_high, d_low = split2(dy * growth)
    later = running[...] * growth[BLOCK - 1 :]
    g_high, g_low = split2(later)
    causal = iota((BLOCK, BLOCK), 0) <= iota((BLOCK, BLOCK), 1)
    k_high, k_low = split2(jnp.where(causal, dot_nt(b, c), 0.0))
    inner = dot(k_high, d_high) + dot(k_high, d_low) + dot(k_low, d_high)
    inner = inner + dot(b, g_high) + dot(b, g_low)
    out_ref[:, :channels] = (inner * weight + skip_ref[...] * dy).astype(BF16)
    q_high, q_low = split2(mixed_ref[...].T)
    grad_b = dot(q_high, c) + dot(q_low, c)
    grad_b = grad_b + dot_nt(x_high, g_high) + dot_nt(x_high, g_low) + dot_nt(x_low, g_high)
    out_ref[:, channels : channels + width] = grad_b.astype(BF16)
    c_t = c.T
    earlier = later + dot(c_t, d_high) + dot(c_t, d_low)
    running[...] = earlier
    through = jnp.sum(earlier * states_ref[...], axis=0, keepdims=True)
    through = gather_heads(jnp.broadcast_to(through, (8, channels)), collect_ref)[:1]
    pulled = gather_heads(scaled * inner, collect_ref)
    below = (iota((BLOCK, BLOCK), 0) > iota((BLOCK, BLOCK), 1)).astype(BF16)
    grad_log_decay = through - dot3(below, dots_ref[...] - pulled)
    rate_grad_ref[...] += jnp.sum(grad_log_decay * log_decay, axis=0, keepdims=True)
    grad_step = pulled / step - rate_ref[...] * grad_log_decay
    out_ref[:, channels + width :] = (grad_step / (1.0 + jnp.exp(-dt))).astype(BF16)


def scan_kernel(backward, pieces_ref, decay_ref, out_ref):
    count = pieces_ref.shape[0]
    total = jnp.zeros(pieces_ref.shape[1:], F32)
    for index in reversed(range(count)) if backward else range(count):
        out_ref[index] = total
        total = total * decay_ref[index : index + 1] + pieces_ref[index]


def params():
    return pltpu.CompilerParams(vmem_limit_bytes=VMEM_BYTES, dimension_semantics=("arbitrary",))


def cost(flops, traffic):
    return pl.CostEstimate(flops=flops, bytes_accessed=traffic, transcendentals=0)


def seg_scan(state, decays, backward):
    count = lax.axis_size("seg")
    rows, channels = state.shape
    pieces = lax.all_to_all(state.reshape(count, rows // count, channels), "seg", 0, 0)
    sums = pl.pallas_call(
        lambda *refs: scan_kernel(backward, *refs),
        out_shape=jax.ShapeDtypeStruct(pieces.shape, F32),
        compiler_params=pltpu.CompilerParams(vmem_limit_bytes=VMEM_BYTES),
        cost_estimate=cost(2 * state.size, 8 * state.size),
    )(pieces, decays)
    return lax.all_to_all(sums, "seg", 0, 0).reshape(rows, channels)


def on_device(inputs, b_rows, c_rows, dt_rows, a_log, d_skip, grad_out):
    shards, segments = lax.axis_size("head"), lax.axis_size("seg")
    rows = inputs.shape[0]
    heads = dt_rows.shape[1] // shards
    channels = inputs.shape[1] // shards
    width = b_rows.shape[1] // shards
    copies = LANES // heads
    first = lax.axis_index("head") * heads
    rate = jnp.exp(a_log)
    rate_here = lax.dynamic_slice_in_dim(rate, first, heads, 0)
    skip_here = lax.dynamic_slice_in_dim(d_skip, first, heads, 0)

    def parts(value):
        return value.reshape(rows, shards, -1).transpose(1, 0, 2)

    def exchange(value):
        return lax.all_to_all(value, "head", 0, 0)

    dt_parts = jnp.tile(parts(dt_rows), (1, 1, copies))
    first_in = exchange(jnp.concatenate([parts(inputs), parts(b_rows), dt_parts], axis=2))
    second_in = exchange(jnp.concatenate([parts(grad_out), parts(c_rows)], axis=2))
    local_total = jnp.sum(-jax.nn.softplus(dt_rows.astype(F32)) * rate, axis=0)
    totals = lax.all_gather(local_total, ("seg", "head")).reshape(segments, shards, -1).sum(axis=1)
    decays = jnp.exp(lax.dynamic_slice_in_dim(totals, first, heads, 1))
    decays = jnp.repeat(decays, HEAD_DIM, axis=1)

    length = rows * shards
    blocks = length // BLOCK
    xbd = first_in.reshape(length, channels + width + LANES)
    dyc = second_in.reshape(length, channels + width)
    rate_row = jnp.tile(rate_here, copies)[None]
    skip_row = jnp.repeat(skip_here, HEAD_DIM)[None]
    lane, channel = jnp.arange(LANES), jnp.arange(channels)
    same = (lane % heads)[:, None] == (channel // HEAD_DIM)[None, :]
    expand = (same & (lane < 3 * heads)[:, None]).astype(BF16)
    collect = same.T.astype(BF16)

    def whole(array):
        return pl.BlockSpec(array.shape, lambda i: (0,) * array.ndim)

    def sections(place):
        return {
            "main": pl.BlockSpec((BLOCK, channels), lambda i: (place(i), 0)),
            "side": pl.BlockSpec((BLOCK, width), lambda i: (place(i), channels // width)),
            "dt": pl.BlockSpec((BLOCK, LANES), lambda i: (place(i), (channels + width) // LANES)),
            "per_head": pl.BlockSpec((BLOCK, LANES), lambda i: (place(i), 0)),
            "mixed": pl.BlockSpec((BLOCK, BLOCK), lambda i: (place(i), 0)),
            "state": pl.BlockSpec((None, width, channels), lambda i: (place(i), 0, 0)),
        }

    onward = sections(lambda i: i)
    back = sections(lambda i: blocks - 1 - i)
    state_shape = jax.ShapeDtypeStruct((width, channels), F32)
    unit = 2 * length * width * channels

    state = pl.pallas_call(
        lambda *refs: state_kernel(heads, *refs),
        grid=(blocks,),
        in_specs=[onward["main"], onward["side"], onward["dt"], whole(rate_row), whole(expand)],
        out_specs=pl.BlockSpec((width, channels), lambda i: (0, 0)),
        out_shape=state_shape,
        compiler_params=params(),
        cost_estimate=cost(2 * unit, 4 * length * channels),
    )(xbd, xbd, xbd, rate_row, expand)
    start = seg_scan(state, decays, False)
    grad_state = pl.pallas_call(
        lambda *refs: grad_state_kernel(heads, *refs),
        grid=(blocks,),
        in_specs=[back["main"], back["side"], back["dt"], whole(rate_row), whole(expand)],
        out_specs=pl.BlockSpec((width, channels), lambda i: (0, 0)),
        out_shape=state_shape,
        compiler_params=params(),
        cost_estimate=cost(2 * unit, 4 * length * channels),
    )(dyc, dyc, xbd, rate_row, expand)
    end = seg_scan(grad_state, decays, True)

    results, states, mixed, dots, skip_grad = pl.pallas_call(
        lambda *refs: forward_kernel(heads, *refs),
        grid=(blocks,),
        in_specs=[
            onward["main"], onward["side"], onward["dt"], onward["main"], onward["side"], whole(start),
            whole(rate_row), whole(skip_row), whole(expand), whole(collect),
        ],
        out_specs=[
            pl.BlockSpec((BLOCK, channels + width), lambda i: (i, 0)),
            onward["state"], onward["mixed"], onward["per_head"],
            pl.BlockSpec((1, channels), lambda i: (0, 0)),
        ],
        out_shape=[
            jax.ShapeDtypeStruct((length, channels + width), BF16),
            jax.ShapeDtypeStruct((blocks, width, channels), F32),
            jax.ShapeDtypeStruct((length, BLOCK), F32),
            jax.ShapeDtypeStruct((length, LANES), F32),
            jax.ShapeDtypeStruct((1, channels), F32),
        ],
        scratch_shapes=[pltpu.VMEM((width, channels), F32)],
        compiler_params=params(),
        cost_estimate=cost(14 * unit, 16 * length * channels),
    )(xbd, xbd, xbd, dyc, dyc, start, rate_row, skip_row, expand, collect)
    first_out = exchange(results.reshape(shards, rows, channels + width))

    grads, rate_grad = pl.pallas_call(
        lambda *refs: backward_kernel(heads, *refs),
        grid=(blocks,),
        in_specs=[
            back["main"], back["side"], back["dt"], back["main"], back["side"], whole(end),
            back["state"], back["mixed"], back["per_head"],
            whole(rate_row), whole(skip_row), whole(expand), whole(collect),
        ],
        out_specs=[
            pl.BlockSpec((BLOCK, channels + width + LANES), lambda i: (blocks - 1 - i, 0)),
            pl.BlockSpec((1, LANES), lambda i: (0, 0)),
        ],
        out_shape=[
            jax.ShapeDtypeStruct((length, channels + width + LANES), BF16),
            jax.ShapeDtypeStruct((1, LANES), F32),
        ],
        scratch_shapes=[pltpu.VMEM((width, channels), F32)],
        compiler_params=params(),
        cost_estimate=cost(12 * unit, 16 * length * channels),
    )(xbd, xbd, xbd, dyc, dyc, end, states, mixed, dots, rate_row, skip_row, expand, collect)
    second_out = exchange(grads.reshape(shards, rows, channels + width + LANES))

    skip_grad = skip_grad.reshape(heads, HEAD_DIM).sum(axis=1)
    sums = jnp.concatenate([rate_grad[0, :heads], skip_grad])
    sums = jnp.pad(sums, (0, LANES - 2 * heads))
    sums = lax.all_to_all(jnp.broadcast_to(sums, (segments, 1, LANES)), "seg", 0, 0).sum(axis=(0, 1))

    def whole_rows(value):
        return value.transpose(1, 0, 2).reshape(rows, -1)

    return (
        whole_rows(first_out[:, :, :channels]),
        whole_rows(second_out[:, :, :channels]),
        whole_rows(second_out[:, :, channels : channels + width]),
        whole_rows(first_out[:, :, channels:]),
        whole_rows(second_out[:, :, channels + width : channels + width + heads]),
        sums[:heads],
        sums[heads : 2 * heads],
    )


def solution(mesh):
    by_rows = P(("dp", "seg", "head"), None)
    in_specs = (by_rows, by_rows, by_rows, by_rows, P(), P(), by_rows)
    out_specs = (by_rows, by_rows, by_rows, by_rows, by_rows, P(("dp", "head")), P(("dp", "head")))
    return jax.shard_map(on_device, mesh=mesh, in_specs=in_specs, out_specs=out_specs, check_vma=False)
```

time: 998 us -> 319 us (0.32); the launches traced: 983 us -> 317 us
  local copies, waits for them, and re-layouts: 271 us -> 29 us
  matrix products: 205 us -> 0 us
  other arithmetic: 188 us -> 4.98 us
  Pallas kernels: 0 us -> 52.5 us
  waiting for transfers between devices: 190 us -> 143 us
  blocking collectives: 75.2 us -> 50.7 us
  between operations: 14.8 us -> 0.93 us
    dot_general x51 -> x0, matrix products: 205 us -> none  [the longest x12 84.2 us: advance(): jnp.einsum('mlbn,nmlc->bmlc', mixing_weights, input_block, precision=HIGH...]
    dynamic_update_slice x28 -> x0, local copies, waits for them, and re-layouts: 121 us -> none  [ssd_blocks(): lax.scan(advance, running, (x_blocks, b_blocks, c_blocks, step_size_blocks))]
    all_gather x2 -> x0, waiting for transfers between devices: 110 us -> none  [prefix(): pieces = jax.tree.map(lambda part: lax.all_gather(part, axis), value)]
    all_to_all x9 -> x8, waiting for transfers between devices: 80.2 us -> 143 us  [the longest x4 116 us: exchange(): return lax.all_to_all(value, 'head', 0, 0)]
    pallas_call x0 -> x6, Pallas kernels: none -> 52.5 us  [the longest x1 19.1 us: on_device(): pl.pallas_call(lambda *refs: forward_kernel(heads, *refs), grid=(blocks,)...]
    dynamic_update_slice x28 -> x0, other arithmetic: 51.3 us -> none  [ssd_blocks(): lax.scan(advance, running, (x_blocks, b_blocks, c_blocks, step_size_blocks))]
    another operation x43 -> x0, other arithmetic: 46.7 us -> none
    select_n x30 -> x2, other arithmetic: 44.2 us -> 0.01 us  [on_device(): same = (lane % heads)[:, None] == (channel // HEAD_DIM)[None, :]]
  transfers between devices with their start and end apart: 11 -> 8, of which waited for: 9 -> 6; matrix products, arithmetic and copies ran while one was open for 12% -> 5% of each run, Pallas kernels for 0% -> 11%
where the time goes in v1:
time: 319 us; the launch traced here: 317 us
  waiting for transfers between devices  143 us (45%)
  Pallas kernels  52.5 us (16%)
  blocking collectives  50.7 us (16%)
  starting transfers between devices  35.7 us (11%)
  local copies, waits for them, and re-layouts  29 us (9%)
  other arithmetic  4.98 us (2%)
    all_to_all x4, waiting for transfers between devices, exchange(): return lax.all_to_all(value, 'head', 0, 0)  116 us
    all_gather x1, blocking collectives, on_device(): lax.all_gather(local_total, ('seg', 'head')).reshape(segments, shards, -1)  36.4 us
    pallas_call x1, Pallas kernels, on_device(): pl.pallas_call(lambda *refs: forward_kernel(heads, *refs), grid=(blocks,)...  19.1 us
    all_to_all x4, starting transfers between devices, exchange(): return lax.all_to_all(value, 'head', 0, 0)  17.1 us
    pallas_call x1, Pallas kernels, on_device(): pl.pallas_call(lambda *refs: backward_kernel(heads, *refs), grid=(blocks,...  16.5 us
    all_to_all x2, waiting for transfers between devices, seg_scan(): return lax.all_to_all(sums, 'seg', 0, 0).reshape(rows, channels)  15.9 us
    all_to_all x1, blocking collectives, on_device(): lax.all_to_all(jnp.broadcast_to(sums, (segments, 1, LANES)), 'seg', 0, 0)  14.3 us
    unnamed x28, local copies, waits for them, and re-layouts  13.9 us
  transfers between devices with their start and end apart: 8, of which 6 were waited for; matrix products, arithmetic and copies ran while one was open for 5% of the time, Pallas kernels for 11%

profile of v1, /device:TPU:0, one launch (start us, length us, event | category | flops | bytes accessed | tf_op | source)
XLA Modules:
  0.0 317.2 jit_solution(15811383470359159300)
XLA Ops:
  0.7 1.9 copy.84
  3.0 1.9 pad_maximum_fusion
  4.8 5.4 %all-to-all-start = ((bf16[8,128,1408]{2,1,0:T(8,128)(2,1)}), bf16[8,128,1408]{2,1,0:T(8,128)(2,1)S(1)}, u32[]{:S(2)}, u32[]{:S(2)}) async-start(bf16[8,128,1408]{2,1,0:T(8,128)(2,1)} %pad_maximum_fusion), calls=%async_computation | async-start | bytes 5767168 | tf_op jit(solution)/shard_map/all_to_all | solution.py:219
  10.2 1.9 copy.83
  12.2 1.8 pad_maximum_fusion.1
  13.9 31.9 %all-to-all-done = bf16[8,128,1408]{2,1,0:T(8,128)(2,1)S(1)} async-done(((bf16[8,128,1408]{2,1,0:T(8,128)(2,1)}), bf16[8,128,1408]{2,1,0:T(8,128)(2,1)S(1)}, u32[]{:S(2)}, u32[]{:S(2)}) %all-to-all-start) | async-done | bytes 2883616 | tf_op jit(solution)/shard_map/all_to_all | solution.py:219
  45.9 1.6 copy-done
  47.5 4.4 %all-to-all-start.1 = ((bf16[8,128,1280]{2,1,0:T(8,128)(2,1)}), bf16[8,128,1280]{2,1,0:T(8,128)(2,1)}, u32[]{:S(2)}, u32[]{:S(2)}) async-start(bf16[8,128,1280]{2,1,0:T(8,128)(2,1)} %pad_maximum_fusion.1), calls=%async_computation.1 | async-start | bytes 5242880 | tf_op jit(solution)/shard_map/all_to_all | solution.py:219
  52.2 6.2 %shard_map.126 = f32[256,1024]{1,0:T(8,128)} custom-call(bf16[1024,1408]{1,0:T(8,128)(2,1)} %bitcast.64, bf16[1024,1408]{1,0:T(8,128)(2,1)} %bitcast.65, bf16[1024,1408]{1,0:T(8,128)(2,1)} %bitcast.66, f32[1,128]{1,0:T(1,128)S(1)} %broadcast_in_dim_tile.3.refs_3_.refs_6_.refs_9_, bf16[128,1024]{1,0:T(8,128)(2,1)S(1)} %and_convert_fusion.refs_4_.refs_8_.refs_11_), custom_call_target="tpu_custom_call" | custom-call | flops 1073741824 | bytes 4194304 | tf_op jit(solution)/shard_map/pallas_call | solution.py:258
  58.4 26.2 %all-to-all-done.1 = bf16[8,128,1280]{2,1,0:T(8,128)(2,1)} async-done(((bf16[8,128,1280]{2,1,0:T(8,128)(2,1)}), bf16[8,128,1280]{2,1,0:T(8,128)(2,1)}, u32[]{:S(2)}, u32[]{:S(2)}) %all-to-all-start.1) | async-done | bytes 2621472 | tf_op jit(solution)/shard_map/all_to_all | solution.py:219
  84.7 7.0 %all-to-all-start.2 = ((f32[16,16,1024]{2,1,0:T(8,128)}), f32[16,16,1024]{2,1,0:T(8,128)S(1)}, u32[]{:S(2)}, u32[]{:S(2)}) async-start(f32[16,16,1024]{2,1,0:T(8,128)} %bitcast.9), calls=%async_computation.2 | async-start | bytes 2097152 | tf_op jit(solution)/shard_map/all_to_all | solution.py:193
  91.7 6.1 %shard_map.129 = f32[256,1024]{1,0:T(8,128)} custom-call(bf16[1024,1280]{1,0:T(8,128)(2,1)} %bitcast.8.refs_3_.refs_4_.refs_0_.refs_1_, bf16[1024,1280]{1,0:T(8,128)(2,1)} %bitcast.8.refs_3_.refs_4_.refs_0_.refs_1_, bf16[1024,1408]{1,0:T(8,128)(2,1)} %bitcast.67, f32[1,128]{1,0:T(1,128)S(1)} %broadcast_in_dim_tile.3.refs_3_.refs_6_.refs_9_, ...), custom_call_target="tpu_custom_call" | custom-call | flops 1073741824 | bytes 4194304 | tf_op jit(solution)/shard_map/pallas_call | solution.py:268
  97.8 11.3 %all-to-all-done.2.refs_0_ = f32[16,16,1024]{2,1,0:T(8,128)S(1)} async-done(((f32[16,16,1024]{2,1,0:T(8,128)}), f32[16,16,1024]{2,1,0:T(8,128)S(1)}, u32[]{:S(2)}, u32[]{:S(2)}) %all-to-all-start.2) | async-done | bytes 1048608 | tf_op jit(solution)/shard_map/all_to_all | solution.py:193
  109.2 3.7 %all-to-all-start.5 = ((f32[16,16,1024]{2,1,0:T(8,128)}), f32[16,16,1024]{2,1,0:T(8,128)S(1)}, u32[]{:S(2)}, u32[]{:S(2)}) async-start(f32[16,16,1024]{2,1,0:T(8,128)} %bitcast.15), calls=%async_computation.5 | async-start | bytes 2097152 | tf_op jit(solution)/shard_map/all_to_all | solution.py:193
  112.9 36.4 %all-gather.1 = f32[128,1,128]{2,1,0:T(1,128)S(1)} all-gather(f32[1,1,128]{2,1,0:T(1,128)S(1)} %bitcast.95), channel_id=2, replica_groups=mesh['dp'=1,'seg'=16,'head'=8] {'seg','head'}, dimensions={0}, use_global_device_ids=true | all-gather | bytes 66048 | tf_op jit(solution)/shard_map/all_gather | solution.py:225
  149.6 2.3 shard_map.127
  151.9 4.1 %all-to-all-start.3 = ((f32[16,16,1024]{2,1,0:T(8,128)}), f32[16,16,1024]{2,1,0:T(8,128)S(1)}, u32[]{:S(2)}, u32[]{:S(2)}) async-start(f32[16,16,1024]{2,1,0:T(8,128)} %shard_map.127), calls=%async_computation.3 | async-start | bytes 2097152 | tf_op jit(solution)/shard_map/all_to_all | solution.py:200
  156.1 2.3 shard_map.130
  158.4 15.9 %all-to-all-done.3 = f32[16,16,1024]{2,1,0:T(8,128)S(1)} async-done(((f32[16,16,1024]{2,1,0:T(8,128)}), f32[16,16,1024]{2,1,0:T(8,128)S(1)}, u32[]{:S(2)}, u32[]{:S(2)}) %all-to-all-start.3) | async-done | bytes 1048608 | tf_op jit(solution)/shard_map/all_to_all | solution.py:200
  174.2 3.8 %all-to-all-start.6 = ((f32[16,16,1024]{2,1,0:T(8,128)}), f32[16,16,1024]{2,1,0:T(8,128)S(1)}, u32[]{:S(2)}, u32[]{:S(2)}) async-start(f32[16,16,1024]{2,1,0:T(8,128)} %shard_map.130), calls=%async_computation.6 | async-start | bytes 2097152 | tf_op jit(solution)/shard_map/all_to_all | solution.py:200
  178.6 19.1 %shard_map.128 = (bf16[1024,1280]{1,0:T(8,128)(2,1)}, f32[4,256,1024]{2,1,0:T(8,128)}, f32[1024,256]{1,0:T(8,128)}, f32[1024,128]{1,0:T(8,128)S(1)}, f32[1,1024]{1,0:T(1,128)S(1)}) custom-call(bf16[1024,1408]{1,0:T(8,128)(2,1)} %bitcast.68, bf16[1024,1408]{1,0:T(8,128)(2,1)} %bitcast.69, bf16[1024,1408]{1,0:T(8,128)(2,1)} %bitcast.70, ...), custom_call_target="tpu_custom_call" | custom-call | flops 7516192768 | bytes 16777216 | tf_op jit(solution)/shard_map/pallas_call | solution.py:279
  198.7 16.5 %shard_map.131 = (bf16[1024,1408]{1,0:T(8,128)(2,1)}, f32[1,128]{1,0:T(1,128)S(1)}) custom-call(bf16[1024,1408]{1,0:T(8,128)(2,1)} %bitcast.71, bf16[1024,1408]{1,0:T(8,128)(2,1)} %bitcast.72, bf16[1024,1408]{1,0:T(8,128)(2,1)} %bitcast.73, bf16[1024,1280]{1,0:T(8,128)(2,1)} %bitcast.8.refs_3_.refs_4_.refs_0_.refs_1_, ...), custom_call_target="tpu_custom_call" | custom-call | flops 6442450944 | bytes 16777216 | tf_op jit(solution)/shard_map/pallas_call | solution.py:304
  216.6 14.3 %all_to_all.45 = f32[16,1,128]{2,1,0:T(1,128)S(1)} all-to-all(f32[16,1,128]{2,1,0:T(1,128)S(1)} %broadcast_in_dim.15), channel_id=1, replica_groups=mesh['dp'=1,'seg'=16,'head'=8] {'seg'}, dimensions={0} | all-to-all | bytes 16384 | tf_op jit(solution)/shard_map/all_to_all | solution.py:329
  230.9 3.6 %all-to-all-start.4 = ((bf16[8,128,1280]{2,1,0:T(8,128)(2,1)}), bf16[8,128,1280]{2,1,0:T(8,128)(2,1)S(1)}, u32[]{:S(2)}, u32[]{:S(2)}) async-start(bf16[8,128,1280]{2,1,0:T(8,128)(2,1)} %bitcast.78), calls=%async_computation.4 | async-start | bytes 5242880 | tf_op jit(solution)/shard_map/all_to_all | solution.py:219
  234.6 4.6 %copy.67 = bf16[8,128,1408]{1,2,0:T(8,128)(2,1)} copy(bf16[8,128,1408]{2,1,0:T(8,128)(2,1)} %bitcast.77) | data formatting | bytes 5767168 | tf_op jit(solution)/shard_map/reshape | solution.py:324
  239.1 28.2 %all-to-all-done.4 = bf16[8,128,1280]{2,1,0:T(8,128)(2,1)S(1)} async-done(((bf16[8,128,1280]{2,1,0:T(8,128)(2,1)}), bf16[8,128,1280]{2,1,0:T(8,128)(2,1)S(1)}, u32[]{:S(2)}, u32[]{:S(2)}) %all-to-all-start.4) | async-done | bytes 2621472 | tf_op jit(solution)/shard_map/all_to_all | solution.py:219
  267.3 1.5 copy-done.1
  268.8 3.6 %all-to-all-start.7 = ((bf16[8,128,1408]{1,2,0:T(8,128)(2,1)}), bf16[8,128,1408]{1,2,0:T(8,128)(2,1)S(1)}, u32[]{:S(2)}, u32[]{:S(2)}) async-start(bf16[8,128,1408]{1,2,0:T(8,128)(2,1)} %copy.67), calls=%async_computation.7 | async-start | bytes 5767168 | tf_op jit(solution)/shard_map/all_to_all | solution.py:219
  273.1 1.8 slice_bitcast_fusion
  278.3 29.8 %all-to-all-done.7 = bf16[8,128,1408]{1,2,0:T(8,128)(2,1)S(1)} async-done(((bf16[8,128,1408]{1,2,0:T(8,128)(2,1)}), bf16[8,128,1408]{1,2,0:T(8,128)(2,1)S(1)}, u32[]{:S(2)}, u32[]{:S(2)}) %all-to-all-start.7) | async-done | bytes 2883616 | tf_op jit(solution)/shard_map/all_to_all | solution.py:219
  309.5 4.1 %copy.70 = bf16[128,8192]{1,0:T(8,128)(2,1)} copy(bf16[128,8192]{0,1:T(8,128)(2,1)} %bitcast.75) | data formatting | bytes 4194304
  314.4 2.0 copy.71
  (60 shorter events, 11.0 us)
Async XLA Ops:
  0.6 1.9 copy-start.8
  0.6 2.3 copy-start.6
  4.8 41.0 %all-to-all-start = ((bf16[8,128,1408]{2,1,0:T(8,128)(2,1)}), bf16[8,128,1408]{2,1,0:T(8,128)(2,1)S(1)}, u32[]{:S(2)}, u32[]{:S(2)}) async-start(bf16[8,128,1408]{2,1,0:T(8,128)(2,1)} %pad_maximum_fusion), calls=%async_computation | async-start | bytes 5767168 | tf_op jit(solution)/shard_map/all_to_all | solution.py:219
  10.2 1.9 copy-start.7
  13.9 37.9 %copy-start.9 = (f32[128]{0:T(128)S(1)}, f32[128]{0:T(128)}, u32[]{:S(2)}) copy-start(f32[128]{0:T(128)} %param.11) | copy-start | bytes 1540
  45.9 1.6 copy-start
  47.5 37.2 %all-to-all-start.1 = ((bf16[8,128,1280]{2,1,0:T(8,128)(2,1)}), bf16[8,128,1280]{2,1,0:T(8,128)(2,1)}, u32[]{:S(2)}, u32[]{:S(2)}) async-start(bf16[8,128,1280]{2,1,0:T(8,128)(2,1)} %pad_maximum_fusion.1), calls=%async_computation.1 | async-start | bytes 5242880 | tf_op jit(solution)/shard_map/all_to_all | solution.py:219
  84.7 24.5 %all-to-all-start.2 = ((f32[16,16,1024]{2,1,0:T(8,128)}), f32[16,16,1024]{2,1,0:T(8,128)S(1)}, u32[]{:S(2)}, u32[]{:S(2)}) async-start(f32[16,16,1024]{2,1,0:T(8,128)} %bitcast.9), calls=%async_computation.2 | async-start | bytes 2097152 | tf_op jit(solution)/shard_map/all_to_all | solution.py:193
  109.2 40.4 %copy-start.3 = (f32[16,16,1024]{2,1,0:T(8,128)}, f32[16,16,1024]{2,1,0:T(8,128)S(1)}, u32[]{:S(2)}) copy-start(f32[16,16,1024]{2,1,0:T(8,128)S(1)} %all-to-all-done.2.refs_0_) | copy-start | bytes 3145732
  109.2 42.7 %all-to-all-start.5 = ((f32[16,16,1024]{2,1,0:T(8,128)}), f32[16,16,1024]{2,1,0:T(8,128)S(1)}, u32[]{:S(2)}, u32[]{:S(2)}) async-start(f32[16,16,1024]{2,1,0:T(8,128)} %bitcast.15), calls=%async_computation.5 | async-start | bytes 2097152 | tf_op jit(solution)/shard_map/all_to_all | solution.py:193
  151.9 4.2 %copy-start.2 = (f32[16,16,1024]{2,1,0:T(8,128)}, f32[16,16,1024]{2,1,0:T(8,128)S(1)}, u32[]{:S(2)}) copy-start(f32[16,16,1024]{2,1,0:T(8,128)S(1)} %all-to-all-done.5.refs_0_) | copy-start | bytes 3145732
  151.9 22.3 %all-to-all-start.3 = ((f32[16,16,1024]{2,1,0:T(8,128)}), f32[16,16,1024]{2,1,0:T(8,128)S(1)}, u32[]{:S(2)}, u32[]{:S(2)}) async-start(f32[16,16,1024]{2,1,0:T(8,128)} %shard_map.127), calls=%async_computation.3 | async-start | bytes 2097152 | tf_op jit(solution)/shard_map/all_to_all | solution.py:200
  156.1 22.0 %copy-start.10 = (f32[128]{0:T(128)S(1)}, f32[128]{0:T(128)}, u32[]{:S(2)}) copy-start(f32[128]{0:T(128)} %param.12) | copy-start | bytes 1540
  174.2 4.3 %copy-start.4 = (f32[16,16,1024]{2,1,0:T(8,128)}, f32[16,16,1024]{2,1,0:T(8,128)S(1)}, u32[]{:S(2)}) copy-start(f32[16,16,1024]{2,1,0:T(8,128)S(1)} %all-to-all-done.3) | copy-start | bytes 3145732
  174.2 23.5 %all-to-all-start.6 = ((f32[16,16,1024]{2,1,0:T(8,128)}), f32[16,16,1024]{2,1,0:T(8,128)S(1)}, u32[]{:S(2)}, u32[]{:S(2)}) async-start(f32[16,16,1024]{2,1,0:T(8,128)} %shard_map.130), calls=%async_computation.6 | async-start | bytes 2097152 | tf_op jit(solution)/shard_map/all_to_all | solution.py:200
  197.7 1.0 copy-start.5
  230.9 36.4 %all-to-all-start.4 = ((bf16[8,128,1280]{2,1,0:T(8,128)(2,1)}), bf16[8,128,1280]{2,1,0:T(8,128)(2,1)S(1)}, u32[]{:S(2)}, u32[]{:S(2)}) async-start(bf16[8,128,1280]{2,1,0:T(8,128)(2,1)} %bitcast.78), calls=%async_computation.4 | async-start | bytes 5242880 | tf_op jit(solution)/shard_map/all_to_all | solution.py:219
  267.3 1.5 copy-start.1
  268.8 39.2 %all-to-all-start.7 = ((bf16[8,128,1408]{1,2,0:T(8,128)(2,1)}), bf16[8,128,1408]{1,2,0:T(8,128)(2,1)S(1)}, u32[]{:S(2)}, u32[]{:S(2)}) async-start(bf16[8,128,1408]{1,2,0:T(8,128)(2,1)} %copy.67), calls=%async_computation.7 | async-start | bytes 5767168 | tf_op jit(solution)/shard_map/all_to_all | solution.py:219

commit v2 on v1

v2 whole, which is shorter than its diff:
```python
import jax
import jax.numpy as jnp
from jax import lax
from jax.experimental import pallas as pl
from jax.experimental.pallas import tpu as pltpu
from jax.sharding import PartitionSpec as P

HEAD_DIM = 64
GSTATE = 256
BLOCK = 256
LANES = 128
CHUNK = 256
VMEM_BYTES = 52 * 1024 * 1024

F32 = jnp.float32
BF16 = jnp.bfloat16


def dot(left, right):
    return lax.dot_general(left, right, (((1,), (0,)), ((), ())), preferred_element_type=F32)


def dot_nt(left, right):
    return lax.dot_general(left, right, (((1,), (1,)), ((), ())), preferred_element_type=F32)


def split2(value):
    high = value.astype(BF16)
    return high, (value - high.astype(F32)).astype(BF16)


def split3(value):
    high, rest = value.astype(BF16), None
    rest = value - high.astype(F32)
    middle = rest.astype(BF16)
    return high, middle, (rest - middle.astype(F32)).astype(BF16)


def dot3(ones, value):
    high, middle, low = split3(value)
    return dot(ones, high) + dot(ones, middle) + dot(ones, low)


def iota(shape, dim):
    return lax.broadcasted_iota(jnp.int32, shape, dim)


def step_sizes(dt, rate):
    step = jnp.log(1.0 + jnp.exp(dt))
    return step, -step * rate


def three_terms(value, heads):
    high, middle, low = split3(value)
    lane = iota(value.shape, 1)
    return jnp.where(lane < heads, high, jnp.where(lane < 2 * heads, middle, low))


def chunks(channels):
    return [slice(at, at + CHUNK) for at in range(0, channels, CHUNK)]


def gather_heads(value, collect):
    high, low = split2(value)
    return dot(high, collect) + dot(low, collect)


def pack_kernel(heads, x_ref, b_ref, dt_ref, out_ref):
    shard, channels, width = pl.program_id(0), x_ref.shape[1], b_ref.shape[1]
    out_ref[:, :channels] = x_ref[...]
    out_ref[:, channels : channels + width] = b_ref[...]
    wanted = shard * heads + lax.rem(iota((LANES, LANES), 1), heads)
    pick = (iota((LANES, LANES), 0) == wanted).astype(BF16)
    out_ref[:, channels + width :] = dot(dt_ref[...], pick).astype(BF16)


def unpack_kernel(heads, in_ref, x_ref, b_ref, dt_ref):
    shard, channels, width = pl.program_id(0), x_ref.shape[1], b_ref.shape[1]
    x_ref[...] = in_ref[:, :channels]
    b_ref[...] = in_ref[:, channels : channels + width]
    mine = iota(dt_ref.shape, 1) // heads == shard
    dt_ref[...] = jnp.where(mine, in_ref[:, channels + width :], dt_ref[...])


def state_kernel(heads, x_ref, b_ref, dt_ref, rate_ref, expand_ref, out_ref, growth_ref, weight_ref):
    block = pl.program_id(0)
    channels = x_ref.shape[1]

    @pl.when(block == 0)
    def _():
        out_ref[...] = jnp.zeros_like(out_ref)
        lower = (iota((BLOCK, BLOCK), 0) >= iota((BLOCK, BLOCK), 1)).astype(BF16)
        log_total = jnp.zeros((1, LANES), F32)
        for at in range(0, dt_ref.shape[0], BLOCK):
            rows = slice(at, at + BLOCK)
            step, log_decay = step_sizes(dt_ref[rows].astype(F32), rate_ref[...])
            cumulative = dot3(lower, log_decay)
            growth_ref[rows] = three_terms(jnp.exp(cumulative), heads)
            weight_ref[rows] = three_terms(jnp.exp(-cumulative) * step, heads)
            log_total = log_total + cumulative[BLOCK - 1 :]
        out_ref[:, channels:] = jnp.broadcast_to(jnp.exp(log_total), (out_ref.shape[0], LANES))

    rows = pl.ds(pl.multiple_of(block * BLOCK, BLOCK), BLOCK)
    ends = pl.ds(pl.multiple_of(block * BLOCK + BLOCK - 16, 16), 16)
    weight, last = weight_ref[rows, :], growth_ref[ends, :]
    b_t = b_ref[...].T
    for part in chunks(channels):
        spread = expand_ref[:, part]
        high, low = split2(x_ref[:, part].astype(F32) * dot(weight, spread))
        decay = dot(last, spread)[15:]
        out_ref[:, part] = (out_ref[:, part] + dot(b_t, high) + dot(b_t, low)) * decay


def grad_state_kernel(pieces, growth_ref, expand_ref, *refs):
    piece_refs, (out_ref, dyc_ref) = refs[:pieces], refs[pieces:]
    channels = out_ref.shape[1]
    me = lax.axis_index("head")
    block = pl.num_programs(0) - 1 - pl.program_id(0)
    hop = lax.rem(me // 2 - block + pieces, pieces)

    @pl.when(pl.program_id(0) == 0)
    def _():
        out_ref[...] = jnp.zeros_like(out_ref)

    for index, piece_ref in enumerate(piece_refs):
        @pl.when(hop == index)
        def _():
            dyc_ref[...] = piece_ref[...]

    growth = growth_ref[...]
    c_t = dyc_ref[:, channels:].T
    for part in chunks(channels):
        grow = dot(growth, expand_ref[:, part])
        high, low = split2(dyc_ref[:, part].astype(F32) * grow)
        out_ref[:, part] = out_ref[:, part] * grow[BLOCK - 1 :] + dot(c_t, high) + dot(c_t, low)


def forward_kernel(
    x_ref, b_ref, dy_ref, c_ref, growth_ref, weight_ref, start_ref, skip_ref, expand_ref, collect_ref,
    out_ref, states_ref, mixed_ref, dots_ref, skip_grad_ref, running,
):
    @pl.when(pl.program_id(0) == 0)
    def _():
        running[...] = start_ref[...]
        skip_grad_ref[...] = jnp.zeros_like(skip_grad_ref)

    channels = x_ref.shape[1]
    b, c, growth, weight = b_ref[...], c_ref[...], growth_ref[...], weight_ref[...]
    b_t = b.T
    causal = iota((BLOCK, BLOCK), 0) >= iota((BLOCK, BLOCK), 1)
    k_high, k_low = split2(jnp.where(causal, dot_nt(c, b), 0.0))
    mixed = jnp.zeros((BLOCK, BLOCK), F32)
    grad_c = jnp.zeros(b.shape, F32)
    dots = jnp.zeros((BLOCK, LANES), F32)
    for part in chunks(channels):
        spread = expand_ref[:, part]
        grow = dot(growth, spread)
        x = x_ref[:, part].astype(F32)
        dy = dy_ref[:, part].astype(F32)
        x_high, x_low = split2(x * dot(weight, spread))
        d_high, d_low = split2(dy * grow)
        state = running[:, part]
        states_ref[:, part] = state
        s_high, s_low = split2(state)
        inner = dot(k_high, x_high) + dot(k_high, x_low) + dot(k_low, x_high) + dot(c, s_high) + dot(c, s_low)
        inner = inner * grow
        out_ref[:, part] = (inner + skip_ref[:, part] * x).astype(BF16)
        dots += gather_heads(dy * inner, collect_ref[part])
        skip_grad_ref[:, part] += jnp.sum(dy * x, axis=0, keepdims=True)
        mixed += dot_nt(d_high, x_high) + dot_nt(d_high, x_low) + dot_nt(d_low, x_high)
        grad_c += dot_nt(d_high, s_high) + dot_nt(d_high, s_low) + dot_nt(d_low, s_high)
        running[:, part] = (state + dot(b_t, x_high) + dot(b_t, x_low)) * grow[BLOCK - 1 :]
    dots_ref[...] = dots
    mixed = jnp.where(causal, mixed, 0.0)
    mixed_ref[...] = mixed
    q_high, q_low = split2(mixed)
    out_ref[:, channels:] = (grad_c + dot(q_high, b) + dot(q_low, b)).astype(BF16)


def backward_kernel(
    x_ref, b_ref, dt_ref, dy_ref, c_ref, growth_ref, weight_ref, end_ref, states_ref, mixed_ref, dots_ref, rate_ref,
    skip_ref, expand_ref, collect_ref, out_ref, rate_grad_ref, running,
):
    @pl.when(pl.program_id(0) == 0)
    def _():
        running[...] = end_ref[...]
        rate_grad_ref[...] = jnp.zeros_like(rate_grad_ref)

    channels, width = x_ref.shape[1], b_ref.shape[1]
    b, c, growth, weight = b_ref[...], c_ref[...], growth_ref[...], weight_ref[...]
    c_t = c.T
    anticausal = iota((BLOCK, BLOCK), 0) <= iota((BLOCK, BLOCK), 1)
    k_high, k_low = split2(jnp.where(anticausal, dot_nt(b, c), 0.0))
    q_high, q_low = split2(mixed_ref[...].T)
    grad_b = dot(q_high, c) + dot(q_low, c)
    pulled = jnp.zeros((BLOCK, LANES), F32)
    through = jnp.zeros((8, LANES), F32)
    for part in chunks(channels):
        spread, collect = expand_ref[:, part], collect_ref[part]
        grow, weigh = dot(growth, spread), dot(weight, spread)
        dy = dy_ref[:, part].astype(F32)
        scaled = x_ref[:, part].astype(F32) * weigh
        x_high, x_low = split2(scaled)
        d_high, d_low = split2(dy * grow)
        later = running[:, part] * grow[BLOCK - 1 :]
        g_high, g_low = split2(later)
        inner = dot(k_high, d_high) + dot(k_high, d_low) + dot(k_low, d_high) + dot(b, g_high) + dot(b, g_low)
        out_ref[:, part] = (inner * weigh + skip_ref[:, part] * dy).astype(BF16)
        grad_b += dot_nt(x_high, g_high) + dot_nt(x_high, g_low) + dot_nt(x_low, g_high)
        earlier = later + dot(c_t, d_high) + dot(c_t, d_low)
        running[:, part] = earlier
        meet = jnp.sum(earlier * states_ref[:, part], axis=0, keepdims=True)
        through += gather_heads(jnp.broadcast_to(meet, (8, CHUNK)), collect)
        pulled += gather_heads(scaled * inner, collect)
    out_ref[:, channels : channels + width] = grad_b.astype(BF16)
    dt = dt_ref[...].astype(F32)
    step, log_decay = step_sizes(dt, rate_ref[...])
    below = (iota((BLOCK, BLOCK), 0) > iota((BLOCK, BLOCK), 1)).astype(BF16)
    grad_log_decay = through[:1] - dot3(below, dots_ref[...] - pulled)
    rate_grad_ref[...] += jnp.sum(grad_log_decay * log_decay, axis=0, keepdims=True)
    grad_step = pulled / step - rate_ref[...] * grad_log_decay
    out_ref[:, channels + width :] = (grad_step / (1.0 + jnp.exp(-dt))).astype(BF16)


def scan_kernel(heads, pieces_ref, expand_ref, out_ref, decay_ref):
    count, channels = out_ref.shape[0], out_ref.shape[2]
    decay_ref[...] = dot(three_terms(pieces_ref[:, 0, channels:], heads), expand_ref[...])
    total = jnp.zeros(out_ref.shape[1:], F32)
    for index in range(count):
        out_ref[index] = total
        total = total * decay_ref[index : index + 1] + pieces_ref[index, :, :channels]


def back_scan_kernel(pieces_ref, decay_ref, out_ref):
    total = jnp.zeros(out_ref.shape[1:], F32)
    for index in reversed(range(out_ref.shape[0])):
        out_ref[index] = total
        total = total * decay_ref[index : index + 1] + pieces_ref[index]


def params():
    return pltpu.CompilerParams(vmem_limit_bytes=VMEM_BYTES, dimension_semantics=("arbitrary",))


def cost(flops, traffic):
    return pl.CostEstimate(flops=flops, bytes_accessed=traffic, transcendentals=0)


def seg_exchange(state):
    count = lax.axis_size("seg")
    return lax.all_to_all(state.reshape(count, -1, state.shape[-1]), "seg", 0, 0)


def seg_sum(value):
    count, hop = lax.axis_size("seg"), 1
    while hop < count:
        value = value + lax.ppermute(value, "seg", [(i, i ^ hop) for i in range(count)])
        hop *= 2
    return value


def exchange(value):
    return lax.all_to_all(value, "head", 0, 0)


def swap_cores(own, other):
    count, core = lax.axis_size("head"), lax.axis_index("head") % 2
    swapped = lax.ppermute(other, "head", [(i, i ^ 1) for i in range(count)])
    return jnp.stack([jnp.where(core == 0, own, swapped), jnp.where(core == 0, swapped, own)], axis=1)


def by_core(value):
    pairs, core = value.reshape(-1, 2, *value.shape[1:]), lax.axis_index("head") % 2
    pick = lambda place: lax.dynamic_index_in_dim(pairs, place, 1, keepdims=False)
    return pick(core), pick(1 - core)


def swap_chips(pairs, after):
    count, chip = lax.axis_size("head"), lax.axis_index("head") // 2
    chips = count // 2
    sent = [lax.dynamic_index_in_dim(pairs, (chip + hop) % chips, 0, keepdims=False) for hop in range(chips)]
    sent = [part.reshape(-1, part.shape[-1]) for part in sent]
    if after is not None:
        sent, _ = lax.optimization_barrier((sent, after))
    return sent[:1] + [
        lax.ppermute(sent[hop], "head", [(i, (i + 2 * hop) % count) for i in range(count)]) for hop in range(1, chips)
    ]


def on_device(inputs, b_rows, c_rows, dt_rows, a_log, d_skip, grad_out):
    shards, segments = lax.axis_size("head"), lax.axis_size("seg")
    rows = inputs.shape[0]
    heads = dt_rows.shape[1] // shards
    channels = inputs.shape[1] // shards
    width = b_rows.shape[1] // shards
    copies = LANES // heads
    first = lax.axis_index("head") * heads
    rate = jnp.exp(a_log)
    rate_here = lax.dynamic_slice_in_dim(rate, first, heads, 0)
    skip_here = lax.dynamic_slice_in_dim(d_skip, first, heads, 0)

    def parts(value):
        return value.reshape(rows, shards, -1).transpose(1, 0, 2)

    packed_width = channels + width + LANES
    packed = pl.pallas_call(
        lambda *refs: pack_kernel(heads, *refs),
        grid=(shards,),
        in_specs=[
            pl.BlockSpec((rows, channels), lambda i: (0, i)),
            pl.BlockSpec((rows, width), lambda i: (0, i)),
            pl.BlockSpec((rows, LANES), lambda i: (0, 0)),
        ],
        out_specs=pl.BlockSpec((None, rows, packed_width), lambda i: (i, 0, 0)),
        out_shape=jax.ShapeDtypeStruct((shards, rows, packed_width), BF16),
        compiler_params=params(),
        cost_estimate=cost(rows, 4 * shards * rows * packed_width),
    )(inputs, b_rows, dt_rows)
    first_in = exchange(packed)
    second_parts = jnp.concatenate([parts(grad_out), parts(c_rows)], axis=2)
    second_in = swap_chips(swap_cores(*by_core(second_parts)), first_in)

    length = rows * shards
    blocks = length // BLOCK
    xbd = first_in.reshape(length, packed_width)
    rate_row = jnp.tile(rate_here, copies)[None]
    skip_row = jnp.repeat(skip_here, HEAD_DIM)[None]
    lane, channel = jnp.arange(LANES), jnp.arange(channels)
    same = (lane % heads)[:, None] == (channel // HEAD_DIM)[None, :]
    expand = (same & (lane < 3 * heads)[:, None]).astype(BF16)
    collect = same.T.astype(BF16)

    def whole(array):
        return pl.BlockSpec(array.shape, lambda i: (0,) * array.ndim)

    def sections(place):
        return {
            "main": pl.BlockSpec((BLOCK, channels), lambda i: (place(i), 0)),
            "side": pl.BlockSpec((BLOCK, width), lambda i: (place(i), channels // width)),
            "dt": pl.BlockSpec((BLOCK, LANES), lambda i: (place(i), (channels + width) // LANES)),
            "per_head": pl.BlockSpec((BLOCK, LANES), lambda i: (place(i), 0)),
            "mixed": pl.BlockSpec((BLOCK, BLOCK), lambda i: (place(i), 0)),
            "state": pl.BlockSpec((None, width, channels), lambda i: (place(i), 0, 0)),
        }

    onward = sections(lambda i: i)
    back = sections(lambda i: blocks - 1 - i)
    state_shape = jax.ShapeDtypeStruct((width, channels), F32)
    unit = 2 * length * width * channels

    terms_shape = jax.ShapeDtypeStruct((length, LANES), BF16)
    state, growth, weight = pl.pallas_call(
        lambda *refs: state_kernel(heads, *refs),
        grid=(blocks,),
        in_specs=[
            onward["main"], onward["side"],
            pl.BlockSpec((length, LANES), lambda i: (0, (channels + width) // LANES)),
            whole(rate_row), whole(expand),
        ],
        out_specs=[
            pl.BlockSpec((width, channels + LANES), lambda i: (0, 0)),
            pl.BlockSpec((length, LANES), lambda i: (0, 0)),
            pl.BlockSpec((length, LANES), lambda i: (0, 0)),
        ],
        out_shape=[jax.ShapeDtypeStruct((width, channels + LANES), F32), terms_shape, terms_shape],
        compiler_params=params(),
        cost_estimate=cost(8 * unit, 4 * length * channels),
    )(xbd, xbd, xbd, rate_row, expand)
    piece = (segments, width // segments, channels)
    starts, decays = pl.pallas_call(
        lambda *refs: scan_kernel(heads, *refs),
        out_shape=[jax.ShapeDtypeStruct(piece, F32), jax.ShapeDtypeStruct((segments, channels), F32)],
        compiler_params=pltpu.CompilerParams(vmem_limit_bytes=VMEM_BYTES),
        cost_estimate=cost(unit, 8 * width * channels),
    )(seg_exchange(state), expand)
    start = seg_exchange(starts).reshape(width, channels)
    second_in, _ = lax.optimization_barrier((second_in, starts))
    piece_spec = pl.BlockSpec((BLOCK, channels + width), lambda i: (0, 0))
    grad_state, dyc = pl.pallas_call(
        lambda *refs: grad_state_kernel(len(second_in), *refs),
        grid=(blocks,),
        in_specs=[back["per_head"], whole(expand)] + [piece_spec] * len(second_in),
        out_specs=[
            pl.BlockSpec((width, channels), lambda i: (0, 0)),
            pl.BlockSpec((BLOCK, channels + width), lambda i: (blocks - 1 - i, 0)),
        ],
        out_shape=[state_shape, jax.ShapeDtypeStruct((length, channels + width), BF16)],
        compiler_params=params(),
        cost_estimate=cost(8 * unit, 4 * length * channels),
    )(growth, expand, *second_in)
    grad_state, _ = lax.optimization_barrier((grad_state, start))
    ends = pl.pallas_call(
        back_scan_kernel,
        out_shape=jax.ShapeDtypeStruct(piece, F32),
        compiler_params=pltpu.CompilerParams(vmem_limit_bytes=VMEM_BYTES),
        cost_estimate=cost(unit, 8 * width * channels),
    )(seg_exchange(grad_state), decays)
    end = seg_exchange(ends).reshape(width, channels)

    results, states, mixed, dots, skip_grad = pl.pallas_call(
        forward_kernel,
        grid=(blocks,),
        in_specs=[
            onward["main"], onward["side"], onward["main"], onward["side"], onward["per_head"], onward["per_head"],
            whole(start), whole(skip_row), whole(expand), whole(collect),
        ],
        out_specs=[
            pl.BlockSpec((BLOCK, channels + width), lambda i: (i, 0)),
            onward["state"], onward["mixed"], onward["per_head"],
            pl.BlockSpec((1, channels), lambda i: (0, 0)),
        ],
        out_shape=[
            jax.ShapeDtypeStruct((length, channels + width), BF16),
            jax.ShapeDtypeStruct((blocks, width, channels), F32),
            jax.ShapeDtypeStruct((length, BLOCK), F32),
            jax.ShapeDtypeStruct((length, LANES), F32),
            jax.ShapeDtypeStruct((1, channels), F32),
        ],
        scratch_shapes=[pltpu.VMEM((width, channels), F32)],
        compiler_params=params(),
        cost_estimate=cost(40 * unit, 16 * length * channels),
    )(xbd, xbd, dyc, dyc, growth, weight, start, skip_row, expand, collect)
    results, _ = lax.optimization_barrier((results, ends))
    first_out = swap_chips(swap_cores(*by_core(results.reshape(shards, rows, channels + width))), None)

    grads, rate_grad = pl.pallas_call(
        backward_kernel,
        grid=(blocks,),
        in_specs=[
            back["main"], back["side"], back["dt"], back["main"], back["side"], back["per_head"], back["per_head"],
            whole(end), back["state"], back["mixed"], back["per_head"],
            whole(rate_row), whole(skip_row), whole(expand), whole(collect),
        ],
        out_specs=[
            pl.BlockSpec((BLOCK, channels + width + LANES), lambda i: (blocks - 1 - i, 0)),
            pl.BlockSpec((1, LANES), lambda i: (0, 0)),
        ],
        out_shape=[
            jax.ShapeDtypeStruct((length, channels + width + LANES), BF16),
            jax.ShapeDtypeStruct((1, LANES), F32),
        ],
        scratch_shapes=[pltpu.VMEM((width, channels), F32)],
        compiler_params=params(),
        cost_estimate=cost(34 * unit, 16 * length * channels),
    )(xbd, xbd, xbd, dyc, dyc, growth, weight, end, states, mixed, dots, rate_row, skip_row, expand, collect)
    grads, _ = lax.optimization_barrier((grads, first_out[1:]))
    second_out = exchange(grads.reshape(shards, rows, channels + width + LANES))

    skip_grad = skip_grad.reshape(heads, HEAD_DIM).sum(axis=1)
    sums = jnp.concatenate([rate_grad[0, :heads], skip_grad])
    sums = seg_sum(jnp.pad(sums, (0, LANES - 2 * heads))[None])[0]

    grad_x, grad_b, grad_dt = pl.pallas_call(
        lambda *refs: unpack_kernel(heads, *refs),
        grid=(shards,),
        in_specs=[pl.BlockSpec((None, rows, packed_width), lambda i: (i, 0, 0))],
        out_specs=[
            pl.BlockSpec((rows, channels), lambda i: (0, i)),
            pl.BlockSpec((rows, width), lambda i: (0, i)),
            pl.BlockSpec((rows, LANES), lambda i: (0, 0)),
        ],
        out_shape=[jax.ShapeDtypeStruct(like.shape, BF16) for like in (inputs, b_rows, dt_rows)],
        compiler_params=params(),
        cost_estimate=cost(rows, 4 * shards * rows * packed_width),
    )(second_out)

    chip = lax.axis_index("head") // 2
    outputs = jnp.stack(first_out).reshape(len(first_out), 2, rows, channels + width)
    outputs = outputs[(chip - jnp.arange(len(first_out))) % len(first_out)]
    outputs = outputs.transpose(2, 0, 1, 3)
    return (
        outputs[..., :channels].reshape(rows, -1),
        grad_x,
        grad_b,
        outputs[..., channels:].reshape(rows, -1),
        grad_dt,
        sums[:heads],
        sums[heads : 2 * heads],
    )


def solution(mesh):
    by_rows = P(("dp", "seg", "head"), None)
    in_specs = (by_rows, by_rows, by_rows, by_rows, P(), P(), by_rows)
    out_specs = (by_rows, by_rows, by_rows, by_rows, by_rows, P(("dp", "head")), P(("dp", "head")))
    return jax.shard_map(on_device, mesh=mesh, in_specs=in_specs, out_specs=out_specs, check_vma=False)
```

time: 319 us -> 233 us (0.73)
  waiting for transfers between devices: 143 us -> 69.6 us
  blocking collectives: 50.7 us -> 0 us
  Pallas kernels: 52.5 us -> 69.6 us
  starting transfers between devices: 35.7 us -> 44.3 us
  other arithmetic: 4.98 us -> 11.5 us
  local copies, waits for them, and re-layouts: 29 us -> 34.9 us
    all_to_all x4 -> x2, waiting for transfers between devices: 116 us -> 20.6 us  [exchange(): return lax.all_to_all(value, 'head', 0, 0)]
    all_gather x1 -> x0, blocking collectives: 36.4 us -> none  [on_device(): lax.all_gather(local_total, ('seg', 'head')).reshape(segments, shards, -1)]
    ppermute x0 -> x12, waiting for transfers between devices: none -> 25 us  [the longest x4 15.2 us: seg_sum(): lax.ppermute(value, 'seg', [(i, i ^ hop) for i in range(count)])]
    pallas_call x5 -> x7, Pallas kernels: 46.3 us -> 62.7 us  [the longest x1 20 us: on_device(): pl.pallas_call(forward_kernel, grid=(blocks,), in_specs=[onward['main'],...]
    all_to_all x1 -> x0, blocking collectives: 14.3 us -> none  [on_device(): lax.all_to_all(jnp.broadcast_to(sums, (segments, 1, LANES)), 'seg', 0, 0)]
    ppermute x0 -> x12, starting transfers between devices: none -> 9.55 us  [the longest x6 7.05 us: swap_chips(): lax.ppermute(sent[hop], 'head', [(i, (i + 2 * hop) % count) for i in rang...]
    another operation x0 -> x5, other arithmetic: none -> 8.41 us  [the longest x4 6.6 us: swap_cores(): jnp.stack([jnp.where(core == 0, own, swapped), jnp.where(core == 0, swapp...]
    all_to_all x4 -> x2, starting transfers between devices: 17.1 us -> 9.95 us  [exchange(): return lax.all_to_all(value, 'head', 0, 0)]
  transfers between devices with their start and end apart: 8 -> 18, of which waited for: 6 -> 10; matrix products, arithmetic and copies ran while one was open for 5% -> 17% of each run, Pallas kernels for 11% -> 24%
where the time goes in v2:
time: 233 us; the launch traced here: 231 us
  Pallas kernels  69.6 us (30%)
  waiting for transfers between devices  69.6 us (30%)
  starting transfers between devices  44.3 us (19%)
  local copies, waits for them, and re-layouts  34.9 us (15%)
  other arithmetic  11.5 us (5%)
    all_to_all x4, starting transfers between devices, seg_exchange(): lax.all_to_all(state.reshape(count, -1, state.shape[-1]), 'seg', 0, 0)  24.8 us
    all_to_all x4, waiting for transfers between devices, seg_exchange(): lax.all_to_all(state.reshape(count, -1, state.shape[-1]), 'seg', 0, 0)  24 us
    all_to_all x2, waiting for transfers between devices, exchange(): return lax.all_to_all(value, 'head', 0, 0)  20.6 us
    pallas_call x1, Pallas kernels, on_device(): pl.pallas_call(forward_kernel, grid=(blocks,), in_specs=[onward['main'],...  20 us
    pallas_call x1, Pallas kernels, on_device(): pl.pallas_call(backward_kernel, grid=(blocks,), in_specs=[back['main'], b...  19.6 us
    ppermute x4, waiting for transfers between devices, seg_sum(): lax.ppermute(value, 'seg', [(i, i ^ hop) for i in range(count)])  15.2 us
    all_to_all x2, starting transfers between devices, exchange(): return lax.all_to_all(value, 'head', 0, 0)  9.95 us
    ppermute x6, waiting for transfers between devices, swap_chips(): lax.ppermute(sent[hop], 'head', [(i, (i + 2 * hop) % count) for i in rang...  9.76 us
  transfers between devices with their start and end apart: 18, of which 10 were waited for; matrix products, arithmetic and copies ran while one was open for 17% of the time, Pallas kernels for 24%

profile of v2, /device:TPU:0, one launch (start us, length us, event | category | flops | bytes accessed | tf_op | source)
XLA Modules:
  0.0 230.8 jit_solution(14897476821941319392)
XLA Ops:
  2.4 6.2 %shard_map.126 = bf16[8,128,1408]{2,1,0:T(8,128)(2,1)} custom-call(bf16[128,8192]{1,0:T(8,128)(2,1)} %refs_0_.1, bf16[128,2048]{1,0:T(8,128)(2,1)S(1)} %copy-done, bf16[128,128]{1,0:T(8,128)(2,1)S(1)} %copy-done.1), custom_call_target="tpu_custom_call" | custom-call | flops 128 | bytes 5767168 | tf_op jit(solution)/shard_map/pallas_call | solution.py:306
  8.6 5.5 %all-to-all-start = ((bf16[8,128,1408]{2,1,0:T(8,128)(2,1)}), bf16[8,128,1408]{2,1,0:T(8,128)(2,1)}, u32[]{:S(2)}, u32[]{:S(2)}) async-start(bf16[8,128,1408]{2,1,0:T(8,128)(2,1)} %shard_map.126), calls=%async_computation | async-start | bytes 5767168 | tf_op jit(solution)/shard_map/all_to_all | solution.py:263
  17.5 5.3 %reshape.169 = bf16[4,2,128,1280]{3,1,0,2:T(2,128)(2,1)S(1)} reshape(bf16[8,128,1280]{2,0,1:T(8,128)(2,1)} %pad_maximum_fusion) | data formatting | bytes 5242880 | tf_op jit(solution)/shard_map/reshape | solution.py:273
  22.8 6.9 %constant_dynamic-slice_fusion.1 = (bf16[4,1,128,1280]{3,1,0,2:T(2,128)(2,1)}, bf16[4,1,128,1280]{3,1,0,2:T(2,128)(2,1)S(1)}) fusion(bf16[4,2,128,1280]{3,1,0,2:T(2,128)(2,1)S(1)} %reshape.169, s32[]{:T(128)S(6)} %select_n.164, s32[]{:T(128)S(6)} %select_n.165), kind=kLoop, calls=%fused_computation.43 | loop fusion | bytes 5242888 | tf_op jit(solution)/shard_map/jit(dynamic_index_in_dim)/dynamic_slice | solution.py:274
  32.0 17.9 %all-to-all-done = bf16[8,128,1408]{2,1,0:T(8,128)(2,1)} async-done(((bf16[8,128,1408]{2,1,0:T(8,128)(2,1)}), bf16[8,128,1408]{2,1,0:T(8,128)(2,1)}, u32[]{:S(2)}, u32[]{:S(2)}) %all-to-all-start) | async-done | bytes 2883616 | tf_op jit(solution)/shard_map/all_to_all | solution.py:263
  49.9 6.9 %shard_map.127 = (f32[256,1152]{1,0:T(8,128)}, bf16[1024,128]{1,0:T(8,128)(2,1)S(1)}, bf16[1024,128]{1,0:T(8,128)(2,1)S(1)}) custom-call(bf16[1024,1408]{1,0:T(8,128)(2,1)} %bitcast.refs_0_.refs_1_.refs_2_.x_ref.b_ref.dt_ref, bf16[1024,1408]{1,0:T(8,128)(2,1)} %bitcast.refs_0_.refs_1_.refs_2_.x_ref.b_ref.dt_ref, ...), custom_call_target="tpu_custom_call" | custom-call | flops 4294967296 | bytes 4194304 | tf_op jit(solution)/shard_map/pallas_call | solution.py:352
  56.8 7.1 %all-to-all-start.1 = ((f32[16,16,1152]{2,1,0:T(8,128)}), f32[16,16,1152]{2,1,0:T(8,128)}, u32[]{:S(2)}, u32[]{:S(2)}) async-start(f32[16,16,1152]{2,1,0:T(8,128)} %bitcast.12), calls=%async_computation.1 | async-start | bytes 2359296 | tf_op jit(solution)/shard_map/all_to_all | solution.py:251
  67.7 2.1 collective-permute-start.2
  70.4 12.6 %all-to-all-done.1.refs_0_ = f32[16,16,1152]{2,1,0:T(8,128)} async-done(((f32[16,16,1152]{2,1,0:T(8,128)}), f32[16,16,1152]{2,1,0:T(8,128)}, u32[]{:S(2)}, u32[]{:S(2)}) %all-to-all-start.1) | async-done | bytes 1179680 | tf_op jit(solution)/shard_map/all_to_all | solution.py:251
  83.0 2.5 %shard_map.128 = (f32[16,16,1024]{2,1,0:T(8,128)}, f32[16,1024]{1,0:T(8,128)S(1)}) custom-call(f32[16,16,1152]{2,1,0:T(8,128)} %all-to-all-done.1.refs_0_, bf16[128,1024]{1,0:T(8,128)(2,1)S(1)} %and_convert_fusion.refs_4_.refs_1_.expand_ref), custom_call_target="tpu_custom_call" | custom-call | flops 536870912 | bytes 2097152 | tf_op jit(solution)/shard_map/pallas_call | solution.py:370
  85.5 3.7 %all-to-all-start.2 = ((f32[16,16,1024]{2,1,0:T(8,128)}), f32[16,16,1024]{2,1,0:T(8,128)S(1)}, u32[]{:S(2)}, u32[]{:S(2)}) async-start(f32[16,16,1024]{2,1,0:T(8,128)} %get-tuple-element.41), calls=%async_computation.2 | async-start | bytes 2097152 | tf_op jit(solution)/shard_map/all_to_all | solution.py:251
  89.6 9.0 %collective-permute-done.1.refs_3_ = bf16[256,1280]{1,0:T(8,128)(2,1)S(1)} collective-permute-done((bf16[256,1280]{1,0:T(8,128)(2,1)}, bf16[256,1280]{1,0:T(8,128)(2,1)S(1)}, u32[]{:S(2)}, u32[]{:S(2)}) %collective-permute-start.1) | collective-permute-done | bytes 655392 | tf_op jit(solution)/shard_map/ppermute | solution.py:286
  99.4 6.1 %shard_map.129 = (f32[256,1024]{1,0:T(8,128)}, bf16[1024,1280]{1,0:T(8,128)(2,1)}) custom-call(bf16[1024,128]{1,0:T(8,128)(2,1)S(1)} %get-tuple-element.35.refs_0_.growth_ref, bf16[128,1024]{1,0:T(8,128)(2,1)S(1)} %and_convert_fusion.refs_4_.refs_1_.expand_ref, bf16[256,1280]{1,0:T(8,128)(2,1)S(1)} %bitcast.68, ...), custom_call_target="tpu_custom_call" | custom-call | flops 4294967296 | bytes 4194304 | tf_op jit(solution)/shard_map/pallas_call | solution.py:379
  106.4 6.8 %all-to-all-start.3 = ((f32[16,16,1024]{2,1,0:T(8,128)}), f32[16,16,1024]{2,1,0:T(8,128)S(1)}, u32[]{:S(2)}, u32[]{:S(2)}) async-start(f32[16,16,1024]{2,1,0:T(8,128)} %bitcast.78), calls=%async_computation.3 | async-start | bytes 2097152 | tf_op jit(solution)/shard_map/all_to_all | solution.py:251
  113.2 20.0 %shard_map.130 = (bf16[1024,1280]{1,0:T(8,128)(2,1)}, f32[4,256,1024]{2,1,0:T(8,128)}, f32[1024,256]{1,0:T(8,128)}, f32[1024,128]{1,0:T(8,128)S(1)}, f32[1,1024]{1,0:T(1,128)S(1)}) custom-call(bf16[1024,1408]{1,0:T(8,128)(2,1)} %bitcast.refs_0_.refs_1_.refs_2_.x_ref.b_ref.dt_ref, bf16[1024,1408]{1,0:T(8,128)(2,1)} %bitcast.refs_0_.refs_1_.refs_2_.x_ref.b_ref.dt_ref, ...), custom_call_target="tpu_custom_call" | custom-call | flops 21474836480 | bytes 16777216 | tf_op jit(solution)/shard_map/pallas_call | solution.py:400
  134.2 2.3 shard_map.131
  138.0 7.3 %all-to-all-start.4 = ((f32[16,16,1024]{2,1,0:T(8,128)}), f32[16,16,1024]{2,1,0:T(8,128)}, u32[]{:S(2)}, u32[]{:S(2)}) async-start(f32[16,16,1024]{2,1,0:T(8,128)} %shard_map.131), calls=%async_computation.4 | async-start | bytes 2097152 | tf_op jit(solution)/shard_map/all_to_all | solution.py:251
  145.3 1.9 fusion.1
  149.0 3.6 %collective-permute-start.6 = (bf16[256,1280]{1,0:T(8,128)(2,1)}, bf16[256,1280]{1,0:T(8,128)(2,1)S(1)}, u32[]{:S(2)}, u32[]{:S(2)}) collective-permute-start(bf16[256,1280]{1,0:T(8,128)(2,1)} %bitcast.22), channel_id=1, source_target_pairs={{0,4},{1,5},{2,6},{3,7},{4,0},{5,1},{6,2},{7,3},{8,12},{9,13},{10,... | collective-permute-start | bytes 1966088 | tf_op jit(solution)/shard_map/ppermute | solution.py:286
  152.6 11.4 %all-to-all-done.4 = f32[16,16,1024]{2,1,0:T(8,128)} async-done(((f32[16,16,1024]{2,1,0:T(8,128)}), f32[16,16,1024]{2,1,0:T(8,128)}, u32[]{:S(2)}, u32[]{:S(2)}) %all-to-all-start.4) | async-done | bytes 1048608 | tf_op jit(solution)/shard_map/all_to_all | solution.py:251
  164.0 19.6 %shard_map.132 = (bf16[1024,1408]{1,0:T(8,128)(2,1)}, f32[1,128]{1,0:T(1,128)S(1)}) custom-call(bf16[1024,1408]{1,0:T(8,128)(2,1)} %bitcast.refs_0_.refs_1_.refs_2_.x_ref.b_ref.dt_ref, bf16[1024,1408]{1,0:T(8,128)(2,1)} %bitcast.refs_0_.refs_1_.refs_2_.x_ref.b_ref.dt_ref, bf16[1024,1408]{1,0:T(8,128)(2,1)} %bitcast.refs_0_.refs_1_.refs_2_.x_ref.b_ref.dt_ref, ...), custom_call_target="tpu_custom_call" | custom-call | flops 18253611008 | bytes 16777216 | tf_op jit(solution)/shard_map/pallas_call | solution.py:426
  184.8 4.4 %all-to-all-start.5 = ((bf16[8,128,1408]{2,1,0:T(8,128)(2,1)}), bf16[8,128,1408]{2,1,0:T(8,128)(2,1)}, u32[]{:S(2)}, u32[]{:S(2)}) async-start(bf16[8,128,1408]{2,1,0:T(8,128)(2,1)} %bitcast.72), calls=%async_computation.5 | async-start | bytes 5767168 | tf_op jit(solution)/shard_map/all_to_all | solution.py:263
  190.8 3.5 %collective-permute-done.8 = f32[1,128]{1,0:T(1,128)S(1)} collective-permute-done((f32[1,128]{1,0:T(1,128)S(1)}, f32[1,128]{1,0:T(1,128)S(1)}, u32[]{:S(2)}, u32[]{:S(2)}) %collective-permute-start.8) | collective-permute-done | bytes 544 | tf_op jit(solution)/shard_map/ppermute | solution.py:257
  195.3 4.1 %collective-permute-done.9 = f32[1,128]{1,0:T(1,128)S(1)} collective-permute-done((f32[1,128]{1,0:T(1,128)S(1)}, f32[1,128]{1,0:T(1,128)S(1)}, u32[]{:S(2)}, u32[]{:S(2)}) %collective-permute-start.9) | collective-permute-done | bytes 544 | tf_op jit(solution)/shard_map/ppermute | solution.py:257
  199.5 3.5 %collective-permute-done.10 = f32[1,128]{1,0:T(1,128)S(1)} collective-permute-done((f32[1,128]{1,0:T(1,128)S(1)}, f32[1,128]{1,0:T(1,128)S(1)}, u32[]{:S(2)}, u32[]{:S(2)}) %collective-permute-start.10) | collective-permute-done | bytes 544 | tf_op jit(solution)/shard_map/ppermute | solution.py:257
  203.9 4.1 %collective-permute-done.11 = f32[1,128]{1,0:T(1,128)S(1)} collective-permute-done((f32[1,128]{1,0:T(1,128)S(1)}, f32[1,128]{1,0:T(1,128)S(1)}, u32[]{:S(2)}, u32[]{:S(2)}) %collective-permute-start.11) | collective-permute-done | bytes 544 | tf_op jit(solution)/shard_map/ppermute | solution.py:257
  208.6 1.8 pad_maximum_fusion.1
  210.4 2.2 gather_fusion
  215.5 2.2 copy.17
  217.7 2.8 %reshape.180 = bf16[128,8192]{1,0:T(8,128)(2,1)} reshape(bf16[128,4,2,1024]{3,2,1,0:T(2,128)(2,1)S(1)} %copy.17) | data formatting | bytes 4194304 | tf_op jit(solution)/shard_map/reshape | solution.py:472
  222.2 2.7 %all-to-all-done.5.refs_0_ = bf16[8,128,1408]{2,1,0:T(8,128)(2,1)} async-done(((bf16[8,128,1408]{2,1,0:T(8,128)(2,1)}), bf16[8,128,1408]{2,1,0:T(8,128)(2,1)}, u32[]{:S(2)}, u32[]{:S(2)}) %all-to-all-start.5) | async-done | bytes 2883616 | tf_op jit(solution)/shard_map/all_to_all | solution.py:263
  224.9 5.9 %shard_map.133 = (bf16[128,8192]{1,0:T(8,128)(2,1)}, bf16[128,2048]{1,0:T(8,128)(2,1)}, bf16[128,128]{1,0:T(8,128)(2,1)}) custom-call(bf16[8,128,1408]{2,1,0:T(8,128)(2,1)} %all-to-all-done.5.refs_0_), custom_call_target="tpu_custom_call" | custom-call | flops 128 | bytes 5767168 | tf_op jit(solution)/shard_map/pallas_call | solution.py:453
  (82 shorter events, 27.9 us)
Async XLA Ops:
  0.6 1.0 copy-start
  1.7 0.8 copy-start.1
  8.6 5.6 %copy-start.5 = (bf16[128,8192]{1,0:T(8,128)(2,1)S(1)}, bf16[128,8192]{1,0:T(8,128)(2,1)}, u32[]{:S(2)}) copy-start(bf16[128,8192]{1,0:T(8,128)(2,1)} %param.13) | copy-start | bytes 6291460
  8.6 41.3 %all-to-all-start = ((bf16[8,128,1408]{2,1,0:T(8,128)(2,1)}), bf16[8,128,1408]{2,1,0:T(8,128)(2,1)}, u32[]{:S(2)}, u32[]{:S(2)}) async-start(bf16[8,128,1408]{2,1,0:T(8,128)(2,1)} %shard_map.126), calls=%async_computation | async-start | bytes 5767168 | tf_op jit(solution)/shard_map/all_to_all | solution.py:263
  14.2 1.5 copy-start.10
  29.7 1.9 copy-start.11
  31.2 32.9 %collective-permute-start = (bf16[4,128,1280]{2,1,0:T(8,128)(2,1)}, bf16[4,128,1280]{2,1,0:T(8,128)(2,1)}, u32[]{:S(2)}, u32[]{:S(2)}) collective-permute-start(bf16[4,128,1280]{2,1,0:T(8,128)(2,1)} %bitcast.67), channel_id=1, source_target_pairs={{0,1},{1,0},{2,3},{3,2},{4,5},{5,4},{6,7},{7,6},{8,9},{9,8},{10,11... | collective-permute-start | bytes 3932168 | tf_op jit(solution)/shard_map/ppermute | solution.py:268
  49.9 14.1 %copy-start.2 = (bf16[4,1,128,1280]{3,1,0,2:T(2,128)(2,1)S(1)}, bf16[4,1,128,1280]{3,1,0,2:T(2,128)(2,1)}, u32[]{:S(2)}) copy-start(bf16[4,1,128,1280]{3,1,0,2:T(2,128)(2,1)} %get-tuple-element.75) | copy-start | bytes 3932164
  56.8 26.2 %all-to-all-start.1 = ((f32[16,16,1152]{2,1,0:T(8,128)}), f32[16,16,1152]{2,1,0:T(8,128)}, u32[]{:S(2)}, u32[]{:S(2)}) async-start(f32[16,16,1152]{2,1,0:T(8,128)} %bitcast.12), calls=%async_computation.1 | async-start | bytes 2359296 | tf_op jit(solution)/shard_map/all_to_all | solution.py:251
  67.2 22.0 %copy-start.12 = (f32[128]{0:T(128)S(1)}, f32[128]{0:T(128)}, u32[]{:S(2)}) copy-start(f32[128]{0:T(128)} %param.12) | copy-start | bytes 1540
  67.2 31.5 %collective-permute-start.1 = (bf16[256,1280]{1,0:T(8,128)(2,1)}, bf16[256,1280]{1,0:T(8,128)(2,1)S(1)}, u32[]{:S(2)}, u32[]{:S(2)}) collective-permute-start(bf16[256,1280]{1,0:T(8,128)(2,1)} %bitcast.9), channel_id=1, source_target_pairs={{0,2},{1,3},{2,4},{3,5},{4,6},{5,7},{6,0},{7,1},{8,10},{9,11},{10,... | collective-permute-start | bytes 1966088 | tf_op jit(solution)/shard_map/ppermute | solution.py:286
  67.7 30.9 %collective-permute-start.2 = (bf16[256,1280]{1,0:T(8,128)(2,1)}, bf16[256,1280]{1,0:T(8,128)(2,1)}, u32[]{:S(2)}, u32[]{:S(2)}) collective-permute-start(bf16[256,1280]{1,0:T(8,128)(2,1)} %bitcast.10), channel_id=1, source_target_pairs={{0,4},{1,5},{2,6},{3,7},{4,0},{5,1},{6,2},{7,3},{8,12},{9,13},{10,... | collective-permute-start | bytes 1966088 | tf_op jit(solution)/shard_map/ppermute | solution.py:286
  69.8 29.6 %collective-permute-start.3 = (bf16[256,1280]{1,0:T(8,128)(2,1)}, bf16[256,1280]{1,0:T(8,128)(2,1)}, u32[]{:S(2)}, u32[]{:S(2)}) collective-permute-start(bf16[256,1280]{1,0:T(8,128)(2,1)} %bitcast.11), channel_id=1, source_target_pairs={{0,6},{1,7},{2,0},{3,1},{4,2},{5,3},{6,4},{7,5},{8,14},{9,15},{10,... | collective-permute-start | bytes 1966088 | tf_op jit(solution)/shard_map/ppermute | solution.py:286
  85.5 20.0 %all-to-all-start.2 = ((f32[16,16,1024]{2,1,0:T(8,128)}), f32[16,16,1024]{2,1,0:T(8,128)S(1)}, u32[]{:S(2)}, u32[]{:S(2)}) async-start(f32[16,16,1024]{2,1,0:T(8,128)} %get-tuple-element.41), calls=%async_computation.2 | async-start | bytes 2097152 | tf_op jit(solution)/shard_map/all_to_all | solution.py:251
  105.5 1.0 copy-start.6
  106.4 26.8 %all-to-all-start.3 = ((f32[16,16,1024]{2,1,0:T(8,128)}), f32[16,16,1024]{2,1,0:T(8,128)S(1)}, u32[]{:S(2)}, u32[]{:S(2)}) async-start(f32[16,16,1024]{2,1,0:T(8,128)} %bitcast.78), calls=%async_computation.3 | async-start | bytes 2097152 | tf_op jit(solution)/shard_map/all_to_all | solution.py:251
  133.3 1.0 copy-start.3
  137.9 7.4 %collective-permute-start.4 = (bf16[4,128,1280]{2,1,0:T(8,128)(2,1)S(1)}, bf16[4,128,1280]{2,1,0:T(8,128)(2,1)}, u32[]{:S(2)}, u32[]{:S(2)}) collective-permute-start(bf16[4,128,1280]{2,1,0:T(8,128)(2,1)S(1)} %dynamic-slice_bitcast_fusion), channel_id=1, source_target_pairs={{0,1},{1,0},{2,3},{3,2},{4,5},{5,4},{6,7},{7,6},{8,9},{9,8},{10,11... | collective-permute-start | bytes 3932168 | tf_op jit(solution)/shard_map/ppermute | solution.py:268
  138.0 25.9 %all-to-all-start.4 = ((f32[16,16,1024]{2,1,0:T(8,128)}), f32[16,16,1024]{2,1,0:T(8,128)}, u32[]{:S(2)}, u32[]{:S(2)}) async-start(f32[16,16,1024]{2,1,0:T(8,128)} %shard_map.131), calls=%async_computation.4 | async-start | bytes 2097152 | tf_op jit(solution)/shard_map/all_to_all | solution.py:251
  148.8 34.8 %collective-permute-start.5 = (bf16[256,1280]{1,0:T(8,128)(2,1)}, bf16[256,1280]{1,0:T(8,128)(2,1)S(1)}, u32[]{:S(2)}, u32[]{:S(2)}) collective-permute-start(bf16[256,1280]{1,0:T(8,128)(2,1)} %bitcast.20), channel_id=1, source_target_pairs={{0,2},{1,3},{2,4},{3,5},{4,6},{5,7},{6,0},{7,1},{8,10},{9,11},{10,... | collective-permute-start | bytes 1966088 | tf_op jit(solution)/shard_map/ppermute | solution.py:286
  149.0 34.6 %collective-permute-start.6 = (bf16[256,1280]{1,0:T(8,128)(2,1)}, bf16[256,1280]{1,0:T(8,128)(2,1)S(1)}, u32[]{:S(2)}, u32[]{:S(2)}) collective-permute-start(bf16[256,1280]{1,0:T(8,128)(2,1)} %bitcast.22), channel_id=1, source_target_pairs={{0,4},{1,5},{2,6},{3,7},{4,0},{5,1},{6,2},{7,3},{8,12},{9,13},{10,... | collective-permute-start | bytes 1966088 | tf_op jit(solution)/shard_map/ppermute | solution.py:286
  152.6 31.0 %collective-permute-start.7 = (bf16[256,1280]{1,0:T(8,128)(2,1)}, bf16[256,1280]{1,0:T(8,128)(2,1)S(1)}, u32[]{:S(2)}, u32[]{:S(2)}) collective-permute-start(bf16[256,1280]{1,0:T(8,128)(2,1)} %bitcast.24), channel_id=1, source_target_pairs={{0,6},{1,7},{2,0},{3,1},{4,2},{5,3},{6,4},{7,5},{8,14},{9,15},{10,... | collective-permute-start | bytes 1966088 | tf_op jit(solution)/shard_map/ppermute | solution.py:286
  183.6 0.8 copy-start.7
  183.6 1.1 copy-start.8
  183.6 1.2 copy-start.9
  183.6 25.0 %copy-start.4 = (bf16[1,2,128,1280]{3,2,0,1:T(8,128)(2,1)S(1)}, bf16[1,2,128,1280]{3,2,0,1:T(8,128)(2,1)}, u32[]{:S(2)}) copy-start(bf16[1,2,128,1280]{3,2,0,1:T(8,128)(2,1)} %get-tuple-element.67) | copy-start | bytes 1966084
  184.8 40.1 %all-to-all-start.5 = ((bf16[8,128,1408]{2,1,0:T(8,128)(2,1)}), bf16[8,128,1408]{2,1,0:T(8,128)(2,1)}, u32[]{:S(2)}, u32[]{:S(2)}) async-start(bf16[8,128,1408]{2,1,0:T(8,128)(2,1)} %bitcast.72), calls=%async_computation.5 | async-start | bytes 5767168 | tf_op jit(solution)/shard_map/all_to_all | solution.py:263
  190.7 3.6 %collective-permute-start.8 = (f32[1,128]{1,0:T(1,128)S(1)}, f32[1,128]{1,0:T(1,128)S(1)}, u32[]{:S(2)}, u32[]{:S(2)}) collective-permute-start(f32[1,128]{1,0:T(1,128)S(1)} %fusion.16), channel_id=1, source_target_pairs={{0,8},{8,0},{16,24},{24,16},{32,40},{40,32},{48,56},{56,48},{64,72... | collective-permute-start | bytes 1544 | tf_op jit(solution)/shard_map/ppermute | solution.py:257
  194.4 5.1 %collective-permute-start.9 = (f32[1,128]{1,0:T(1,128)S(1)}, f32[1,128]{1,0:T(1,128)S(1)}, u32[]{:S(2)}, u32[]{:S(2)}) collective-permute-start(f32[1,128]{1,0:T(1,128)S(1)} %fusion.17), channel_id=1, source_target_pairs={{0,16},{8,24},{16,0},{24,8},{32,48},{40,56},{48,32},{56,40},{64,80... | collective-permute-start | bytes 1544 | tf_op jit(solution)/shard_map/ppermute | solution.py:257
  199.4 3.5 %collective-permute-start.10 = (f32[1,128]{1,0:T(1,128)S(1)}, f32[1,128]{1,0:T(1,128)S(1)}, u32[]{:S(2)}, u32[]{:S(2)}) collective-permute-start(f32[1,128]{1,0:T(1,128)S(1)} %add.150), channel_id=1, source_target_pairs={{0,32},{8,40},{16,48},{24,56},{32,0},{40,8},{48,16},{56,24},{64,96... | collective-permute-start | bytes 1544 | tf_op jit(solution)/shard_map/ppermute | solution.py:257
  203.0 5.0 %collective-permute-start.11 = (f32[1,128]{1,0:T(1,128)S(1)}, f32[1,128]{1,0:T(1,128)S(1)}, u32[]{:S(2)}, u32[]{:S(2)}) collective-permute-start(f32[1,128]{1,0:T(1,128)S(1)} %add.151), channel_id=1, source_target_pairs={{0,64},{8,72},{16,80},{24,88},{32,96},{40,104},{48,112},{56,120},{... | collective-permute-start | bytes 1544 | tf_op jit(solution)/shard_map/ppermute | solution.py:257

commit v3 on v2

v3 whole, which is shorter than its diff:
```python
import jax
import jax.numpy as jnp
from jax import lax
from jax.experimental import pallas as pl
from jax.experimental.pallas import tpu as pltpu
from jax.sharding import PartitionSpec as P

HEAD_DIM = 64
GSTATE = 256
BLOCK = 256
LANES = 128
CHANNELS = 1024
VMEM_BYTES = 50 * 1024 * 1024

F32 = jnp.float32
BF16 = jnp.bfloat16


def dot(left, right):
    return lax.dot_general(left, right, (((1,), (0,)), ((), ())), preferred_element_type=F32)


def dot_nt(left, right):
    return lax.dot_general(left, right, (((1,), (1,)), ((), ())), preferred_element_type=F32)


def split2(value):
    high = value.astype(BF16)
    return high, (value - high.astype(F32)).astype(BF16)


def split3(value):
    high, rest = value.astype(BF16), None
    rest = value - high.astype(F32)
    middle = rest.astype(BF16)
    return high, middle, (rest - middle.astype(F32)).astype(BF16)


def dot3(ones, value):
    high, middle, low = split3(value)
    return dot(ones, high) + dot(ones, middle) + dot(ones, low)


def iota(shape, dim):
    return lax.broadcasted_iota(jnp.int32, shape, dim)


def step_sizes(dt, rate):
    step = jnp.log(1.0 + jnp.exp(dt))
    return step, -step * rate


def three_terms(value, heads):
    high, middle, low = split3(value)
    lane = iota(value.shape, 1)
    return jnp.where(lane < heads, high, jnp.where(lane < 2 * heads, middle, low))


def gather_heads(value, collect):
    high, low = split2(value)
    return dot(high, collect) + dot(low, collect)


def pack_kernel(heads, x_ref, b_ref, dt_ref, out_ref):
    here, channels, width = out_ref.shape[0], CHANNELS, GSTATE
    for index in range(here):
        shard = pl.program_id(0) * here + index
        out_ref[index, :, :channels] = x_ref[:, index * channels : (index + 1) * channels]
        out_ref[index, :, channels : channels + width] = b_ref[:, index * width : (index + 1) * width]
        wanted = shard * heads + lax.rem(iota((LANES, LANES), 1), heads)
        pick = (iota((LANES, LANES), 0) == wanted).astype(BF16)
        out_ref[index, :, channels + width :] = dot(dt_ref[...], pick).astype(BF16)


def unpack_kernel(heads, in_ref, x_ref, b_ref, dt_ref):
    here, channels, width = in_ref.shape[0], CHANNELS, GSTATE
    for index in range(here):
        shard = pl.program_id(0) * here + index
        x_ref[:, index * channels : (index + 1) * channels] = in_ref[index, :, :channels]
        b_ref[:, index * width : (index + 1) * width] = in_ref[index, :, channels : channels + width]
        mine = iota(dt_ref.shape, 1) // heads == shard
        dt_ref[...] = jnp.where(mine, in_ref[index, :, channels + width :], dt_ref[...])


def core_halves(first, second, own_ref, other_ref):
    core = lax.rem(lax.axis_index("head"), 2)

    @pl.when(core == 0)
    def _():
        own_ref[...], other_ref[...] = first, second

    @pl.when(core == 1)
    def _():
        own_ref[...], other_ref[...] = second, first


def pack_pair_kernel(dy_ref, c_ref, own_ref, other_ref):
    channels, width = CHANNELS, GSTATE
    first = jnp.concatenate([dy_ref[:, :channels], c_ref[:, :width]], axis=1)
    second = jnp.concatenate([dy_ref[:, channels:], c_ref[:, width:]], axis=1)
    core_halves(first, second, own_ref, other_ref)


def merge_kernel(own_ref, swapped_ref, *out_refs):
    me, chips, rows = lax.axis_index("head"), own_ref.shape[0], own_ref.shape[1]
    core = lax.rem(me, 2)
    for hop, out_ref in enumerate(out_refs):
        chip = lax.rem(me // 2 + hop, chips)
        out_ref[pl.ds(pl.multiple_of(core * rows, rows), rows), :] = own_ref[chip]
        out_ref[pl.ds(pl.multiple_of((1 - core) * rows, rows), rows), :] = swapped_ref[chip]


def unpack_pairs_kernel(pieces, *refs):
    piece_refs, (y_ref, c_ref) = refs[:pieces], refs[pieces:]
    me, rows, channels, width = lax.axis_index("head"), y_ref.shape[0], CHANNELS, GSTATE
    for hop, piece_ref in enumerate(piece_refs):
        chip = lax.rem(me // 2 - hop + pieces, pieces)
        for core in range(2):
            part = slice(core * rows, (core + 1) * rows)
            at = pl.multiple_of((2 * chip + core) * channels, channels)
            y_ref[:, pl.ds(at, channels)] = piece_ref[part, :channels]
            at = pl.multiple_of((2 * chip + core) * width, width)
            c_ref[:, pl.ds(at, width)] = piece_ref[part, channels:]


def state_kernel(
    heads, x_ref, b_ref, dt_ref, rate_ref, expand_ref,
    out_ref, growth_ref, weight_ref, before_ref, decay_ref, so_far,
):
    block = pl.program_id(0)
    channels = x_ref.shape[1]

    @pl.when(block == 0)
    def _():
        out_ref[...] = jnp.zeros_like(out_ref)
        so_far[...] = jnp.ones_like(so_far)
        lower = (iota((BLOCK, BLOCK), 0) >= iota((BLOCK, BLOCK), 1)).astype(BF16)
        log_total = jnp.zeros((1, LANES), F32)
        for at in range(0, dt_ref.shape[0], BLOCK):
            rows = slice(at, at + BLOCK)
            step, log_decay = step_sizes(dt_ref[rows].astype(F32), rate_ref[...])
            cumulative = dot3(lower, log_decay)
            growth_ref[rows] = three_terms(jnp.exp(cumulative), heads)
            weight_ref[rows] = three_terms(jnp.exp(-cumulative) * step, heads)
            log_total = log_total + cumulative[BLOCK - 1 :]
        out_ref[:, channels:] = jnp.broadcast_to(jnp.exp(log_total), (out_ref.shape[0], LANES))

    rows = pl.ds(pl.multiple_of(block * BLOCK, BLOCK), BLOCK)
    ends = pl.ds(pl.multiple_of(block * BLOCK + BLOCK - 16, 16), 16)
    spread = expand_ref[...]
    high, low = split2(x_ref[...].astype(F32) * dot(weight_ref[rows, :], spread))
    decay = dot(growth_ref[ends, :], spread)[15:]
    b_t = b_ref[...].T
    state = out_ref[:, :channels]
    before_ref[...] = state
    decay_ref[...] = so_far[...]
    so_far[...] = so_far[...] * decay
    out_ref[:, :channels] = (state + dot(b_t, high) + dot(b_t, low)) * decay


def grad_state_kernel(pieces, growth_ref, expand_ref, *refs):
    piece_refs, (out_ref, dyc_ref, later_ref, decay_ref, so_far) = refs[:pieces], refs[pieces:]
    channels = out_ref.shape[1]
    block = pl.num_programs(0) - 1 - pl.program_id(0)
    hop = lax.rem(lax.axis_index("head") // 2 - block + pieces, pieces)

    @pl.when(pl.program_id(0) == 0)
    def _():
        out_ref[...] = jnp.zeros_like(out_ref)
        so_far[...] = jnp.ones_like(so_far)

    for index, piece_ref in enumerate(piece_refs):
        @pl.when(hop == index)
        def _():
            dyc_ref[...] = piece_ref[...]

    grow = dot(growth_ref[...], expand_ref[...])
    decay = grow[BLOCK - 1 :]
    high, low = split2(dyc_ref[:, :channels].astype(F32) * grow)
    c_t = dyc_ref[:, channels:].T
    later = out_ref[...] * decay
    later_ref[...] = later
    so_far[...] = so_far[...] * decay
    decay_ref[...] = so_far[...]
    out_ref[...] = later + dot(c_t, high) + dot(c_t, low)


def inside_kernel(
    x_ref, b_ref, dy_ref, c_ref, growth_ref, weight_ref, expand_ref,
    inner_ref, grad_inner_ref, grad_b_ref, grad_c_ref, skip_grad_ref,
):
    @pl.when(pl.program_id(0) == 0)
    def _():
        skip_grad_ref[...] = jnp.zeros_like(skip_grad_ref)

    b, c = b_ref[...], c_ref[...]
    x, dy = x_ref[...].astype(F32), dy_ref[...].astype(F32)
    skip_grad_ref[...] += jnp.sum(dy * x, axis=0, keepdims=True)
    x_high, x_low = split2(x * dot(weight_ref[...], expand_ref[...]))
    d_high, d_low = split2(dy * dot(growth_ref[...], expand_ref[...]))
    causal = iota((BLOCK, BLOCK), 0) >= iota((BLOCK, BLOCK), 1)
    anticausal = iota((BLOCK, BLOCK), 0) <= iota((BLOCK, BLOCK), 1)
    k_high, k_low = split2(jnp.where(causal, dot_nt(c, b), 0.0))
    inner_ref[...] = dot(k_high, x_high) + dot(k_high, x_low) + dot(k_low, x_high)
    k_high, k_low = split2(jnp.where(anticausal, dot_nt(b, c), 0.0))
    grad_inner_ref[...] = dot(k_high, d_high) + dot(k_high, d_low) + dot(k_low, d_high)
    mixed = dot_nt(d_high, x_high) + dot_nt(d_high, x_low) + dot_nt(d_low, x_high)
    mixed = jnp.where(causal, mixed, 0.0)
    q_high, q_low = split2(mixed)
    grad_c_ref[...] = dot(q_high, b) + dot(q_low, b)
    q_high, q_low = split2(mixed.T)
    grad_b_ref[...] = dot(q_high, c) + dot(q_low, c)


def forward_kernel(
    x_ref, c_ref, dy_ref, growth_ref, inner_ref, grad_c_ref, before_ref, decay_ref, start_ref,
    skip_ref, expand_ref, collect_ref, own_ref, other_ref, dots_ref,
):
    grow, c = dot(growth_ref[...], expand_ref[...]), c_ref[...]
    grown = dy_ref[...].astype(F32) * grow
    d_high, d_low = split2(grown)
    s_high, s_low = split2(before_ref[...] + decay_ref[...] * start_ref[...])
    inner = inner_ref[...] + dot(c, s_high) + dot(c, s_low)
    grad_c = grad_c_ref[...] + dot_nt(d_high, s_high) + dot_nt(d_high, s_low) + dot_nt(d_low, s_high)
    dots_ref[...] = gather_heads(grown * inner, collect_ref[...])
    y = inner * grow + skip_ref[...] * x_ref[...].astype(F32)
    y, grad_c = y.astype(BF16), grad_c.astype(BF16)
    result = jnp.concatenate([y, grad_c], axis=1)
    core_halves(result[: BLOCK // 2], result[BLOCK // 2 :], own_ref, other_ref)


def backward_kernel(
    x_ref, b_ref, dt_ref, dy_ref, weight_ref, inner_ref, grad_b_ref, later_ref, decay_ref, end_ref,
    state_ref, start_ref, total_ref, dots_ref, rate_ref, skip_ref, expand_ref, collect_ref,
    out_ref, rate_grad_ref, after,
):
    channels, width = x_ref.shape[1], b_ref.shape[1]

    @pl.when(pl.program_id(0) == 0)
    def _():
        final = state_ref[...] + total_ref[...] * start_ref[...]
        meet = jnp.sum(final * end_ref[...], axis=0, keepdims=True)
        after[...] = gather_heads(jnp.broadcast_to(meet, (8, channels)), collect_ref[...])
        rate_grad_ref[...] = jnp.zeros_like(rate_grad_ref)

    b, weigh = b_ref[...], dot(weight_ref[...], expand_ref[...])
    scaled = x_ref[...].astype(F32) * weigh
    x_high, x_low = split2(scaled)
    g_high, g_low = split2(later_ref[...] + decay_ref[...] * end_ref[...])
    inner = inner_ref[...] + dot(b, g_high) + dot(b, g_low)
    pulled = gather_heads(scaled * inner, collect_ref[...])
    out_ref[:, :channels] = (inner * weigh + skip_ref[...] * dy_ref[...].astype(F32)).astype(BF16)
    grad_b = grad_b_ref[...] + dot_nt(x_high, g_high) + dot_nt(x_high, g_low) + dot_nt(x_low, g_high)
    out_ref[:, channels : channels + width] = grad_b.astype(BF16)
    dt = dt_ref[...].astype(F32)
    step, log_decay = step_sizes(dt, rate_ref[...])
    change = dots_ref[...] - pulled
    onward = (iota((BLOCK, BLOCK), 0) <= iota((BLOCK, BLOCK), 1)).astype(BF16)
    grad_log_decay = dot3(onward, change) + after[:1]
    after[...] = after[...] + jnp.sum(change, axis=0, keepdims=True)
    rate_grad_ref[...] += jnp.sum(grad_log_decay * log_decay, axis=0, keepdims=True)
    grad_step = pulled / step - rate_ref[...] * grad_log_decay
    out_ref[:, channels + width :] = (grad_step / (1.0 + jnp.exp(-dt))).astype(BF16)


def scan_kernel(heads, pieces_ref, expand_ref, out_ref, decay_ref):
    count, channels = out_ref.shape[0], out_ref.shape[2]
    decay_ref[...] = dot(three_terms(pieces_ref[:, 0, channels:], heads), expand_ref[...])
    total = jnp.zeros(out_ref.shape[1:], F32)
    for index in range(count):
        out_ref[index] = total
        total = total * decay_ref[index : index + 1] + pieces_ref[index, :, :channels]


def back_scan_kernel(pieces_ref, decay_ref, out_ref):
    total = jnp.zeros(out_ref.shape[1:], F32)
    for index in reversed(range(out_ref.shape[0])):
        out_ref[index] = total
        total = total * decay_ref[index : index + 1] + pieces_ref[index]


def params():
    return pltpu.CompilerParams(vmem_limit_bytes=VMEM_BYTES, dimension_semantics=("arbitrary",))


def cost(flops, traffic):
    return pl.CostEstimate(flops=flops, bytes_accessed=traffic, transcendentals=0)


def seg_exchange(state):
    count = lax.axis_size("seg")
    return lax.all_to_all(state.reshape(count, -1, state.shape[-1]), "seg", 0, 0)


def seg_sum(value):
    count, hop = lax.axis_size("seg"), 1
    while hop < count:
        value = value + lax.ppermute(value, "seg", [(i, i ^ hop) for i in range(count)])
        hop *= 2
    return value


def exchange(value):
    return lax.all_to_all(value, "head", 0, 0)


def swap_cores(own, other):
    count = lax.axis_size("head")
    chips, rows, columns = own.shape
    swapped = lax.ppermute(other, "head", [(i, i ^ 1) for i in range(count)])
    return pl.pallas_call(
        merge_kernel,
        out_shape=[jax.ShapeDtypeStruct((2 * rows, columns), BF16)] * chips,
        compiler_params=pltpu.CompilerParams(vmem_limit_bytes=VMEM_BYTES),
        cost_estimate=cost(rows, 16 * own.size),
    )(own, swapped)


def swap_chips(sent):
    count = lax.axis_size("head")

    def permute(hop, value):
        return lax.ppermute(value, "head", [(i, (i + 2 * hop) % count) for i in range(count)])

    came = {0: sent[0], 1: permute(1, sent[1]), len(sent) - 1: permute(len(sent) - 1, sent[-1])}
    for hop in range(2, len(sent) - 1):
        value, _ = lax.optimization_barrier((sent[hop], list(came.values())[1:]))
        came[hop] = permute(hop, value)
    return [came[hop] for hop in range(len(sent))]


def on_device(inputs, b_rows, c_rows, dt_rows, a_log, d_skip, grad_out):
    shards, segments = lax.axis_size("head"), lax.axis_size("seg")
    rows = inputs.shape[0]
    heads = dt_rows.shape[1] // shards
    channels = inputs.shape[1] // shards
    width = b_rows.shape[1] // shards
    copies = LANES // heads
    first = lax.axis_index("head") * heads
    rate = jnp.exp(a_log)
    rate_here = lax.dynamic_slice_in_dim(rate, first, heads, 0)
    skip_here = lax.dynamic_slice_in_dim(d_skip, first, heads, 0)

    packed_width, pair_width = channels + width + LANES, channels + width
    packed = pl.pallas_call(
        lambda *refs: pack_kernel(heads, *refs),
        grid=(shards // 2,),
        in_specs=[
            pl.BlockSpec((rows, 2 * channels), lambda i: (0, i)),
            pl.BlockSpec((rows, 2 * width), lambda i: (0, i)),
            pl.BlockSpec((rows, LANES), lambda i: (0, 0)),
        ],
        out_specs=pl.BlockSpec((2, rows, packed_width), lambda i: (i, 0, 0)),
        out_shape=jax.ShapeDtypeStruct((shards, rows, packed_width), BF16),
        compiler_params=params(),
        cost_estimate=cost(rows, 4 * shards * rows * packed_width),
    )(inputs, b_rows, dt_rows)
    first_in = exchange(packed)
    half_spec = pl.BlockSpec((None, rows, pair_width), lambda i: (i, 0, 0))
    half_shape = jax.ShapeDtypeStruct((shards // 2, rows, pair_width), BF16)
    own, other = pl.pallas_call(
        pack_pair_kernel,
        grid=(shards // 2,),
        in_specs=[
            pl.BlockSpec((rows, 2 * channels), lambda i: (0, i)),
            pl.BlockSpec((rows, 2 * width), lambda i: (0, i)),
        ],
        out_specs=[half_spec, half_spec],
        out_shape=[half_shape, half_shape],
        compiler_params=params(),
        cost_estimate=cost(rows, 4 * shards * rows * pair_width),
    )(grad_out, c_rows)
    first_in, sent = lax.optimization_barrier((first_in, swap_cores(own, other)))
    second_in = swap_chips(sent)

    length = rows * shards
    blocks = length // BLOCK
    xbd = first_in.reshape(length, packed_width)
    rate_row = jnp.tile(rate_here, copies)[None]
    skip_row = jnp.repeat(skip_here, HEAD_DIM)[None]
    lane, channel = jnp.arange(LANES), jnp.arange(channels)
    same = (lane % heads)[:, None] == (channel // HEAD_DIM)[None, :]
    expand = (same & (lane < 3 * heads)[:, None]).astype(BF16)
    collect = same.T.astype(BF16)

    def whole(array):
        return pl.BlockSpec(array.shape, lambda i: (0,) * array.ndim)

    def sections(place):
        return {
            "main": pl.BlockSpec((BLOCK, channels), lambda i: (place(i), 0)),
            "side": pl.BlockSpec((BLOCK, width), lambda i: (place(i), channels // width)),
            "dt": pl.BlockSpec((BLOCK, LANES), lambda i: (place(i), (channels + width) // LANES)),
            "per_head": pl.BlockSpec((BLOCK, LANES), lambda i: (place(i), 0)),
            "mixed": pl.BlockSpec((BLOCK, BLOCK), lambda i: (place(i), 0)),
            "decay": pl.BlockSpec((None, 1, channels), lambda i: (place(i), 0, 0)),
            "state": pl.BlockSpec((None, width, channels), lambda i: (place(i), 0, 0)),
        }

    onward = sections(lambda i: i)
    back = sections(lambda i: blocks - 1 - i)
    state_shape = jax.ShapeDtypeStruct((width, channels), F32)
    states_shape = jax.ShapeDtypeStruct((blocks, width, channels), F32)
    terms_shape = jax.ShapeDtypeStruct((length, LANES), BF16)
    decays_shape = jax.ShapeDtypeStruct((blocks, 1, channels), F32)
    row_scratch = pltpu.VMEM((1, channels), F32)
    unit = 2 * length * width * channels

    state, growth, weight, before, decay_before = pl.pallas_call(
        lambda *refs: state_kernel(heads, *refs),
        grid=(blocks,),
        in_specs=[
            onward["main"], onward["side"],
            pl.BlockSpec((length, LANES), lambda i: (0, (channels + width) // LANES)),
            whole(rate_row), whole(expand),
        ],
        out_specs=[
            pl.BlockSpec((width, channels + LANES), lambda i: (0, 0)),
            pl.BlockSpec((length, LANES), lambda i: (0, 0)),
            pl.BlockSpec((length, LANES), lambda i: (0, 0)),
            onward["state"], onward["decay"],
        ],
        out_shape=[
            jax.ShapeDtypeStruct((width, channels + LANES), F32),
            terms_shape, terms_shape, states_shape, decays_shape,
        ],
        scratch_shapes=[row_scratch],
        compiler_params=params(),
        cost_estimate=cost(6 * unit, 4 * length * channels),
    )(xbd, xbd, xbd, rate_row, expand)
    piece = (segments, width // segments, channels)
    starts, decays = pl.pallas_call(
        lambda *refs: scan_kernel(heads, *refs),
        out_shape=[jax.ShapeDtypeStruct(piece, F32), jax.ShapeDtypeStruct((segments, channels), F32)],
        compiler_params=pltpu.CompilerParams(vmem_limit_bytes=VMEM_BYTES),
        cost_estimate=cost(unit, 8 * width * channels),
    )(seg_exchange(state), expand)
    starts, _ = lax.optimization_barrier((starts, second_in[1:]))
    start = seg_exchange(starts).reshape(width, channels)

    grad_state, dyc, later, decay_after = pl.pallas_call(
        lambda *refs: grad_state_kernel(len(second_in), *refs),
        grid=(blocks,),
        in_specs=[back["per_head"], whole(expand)] + [whole(part) for part in second_in],
        out_specs=[
            pl.BlockSpec((width, channels), lambda i: (0, 0)),
            pl.BlockSpec((BLOCK, pair_width), lambda i: (blocks - 1 - i, 0)),
            back["state"], back["decay"],
        ],
        out_shape=[
            state_shape, jax.ShapeDtypeStruct((length, pair_width), BF16),
            states_shape, decays_shape,
        ],
        scratch_shapes=[row_scratch],
        compiler_params=params(),
        cost_estimate=cost(6 * unit, 4 * length * channels),
    )(growth, expand, *second_in)
    inner, grad_inner, inside_b, inside_c, skip_grad = pl.pallas_call(
        inside_kernel,
        grid=(blocks,),
        in_specs=[onward[name] for name in ("main", "side", "main", "side", "per_head", "per_head")] + [whole(expand)],
        out_specs=[
            onward["main"], onward["main"], onward["mixed"], onward["mixed"],
            pl.BlockSpec((1, channels), lambda i: (0, 0)),
        ],
        out_shape=[
            jax.ShapeDtypeStruct((length, channels), F32), jax.ShapeDtypeStruct((length, channels), F32),
            jax.ShapeDtypeStruct((length, width), F32), jax.ShapeDtypeStruct((length, width), F32),
            jax.ShapeDtypeStruct((1, channels), F32),
        ],
        compiler_params=params(),
        cost_estimate=cost(12 * unit, 16 * length * channels),
    )(xbd, xbd, dyc, dyc, growth, weight, expand)

    grad_state, _ = lax.optimization_barrier((grad_state, (start, inner)))
    pieces = seg_exchange(grad_state)
    own, other, dots = pl.pallas_call(
        forward_kernel,
        grid=(blocks,),
        in_specs=[
            onward["main"], onward["side"], onward["main"], onward["per_head"],
            onward["main"], onward["mixed"], onward["state"], onward["decay"],
            whole(start), whole(skip_row), whole(expand), whole(collect),
        ],
        out_specs=[half_spec, half_spec, onward["per_head"]],
        out_shape=[half_shape, half_shape, jax.ShapeDtypeStruct((length, LANES), F32)],
        compiler_params=params(),
        cost_estimate=cost(8 * unit, 16 * length * channels),
    )(xbd, dyc, dyc, growth, inner, inside_c, before, decay_before, start, skip_row, expand, collect)
    ends = pl.pallas_call(
        back_scan_kernel,
        out_shape=jax.ShapeDtypeStruct(piece, F32),
        compiler_params=pltpu.CompilerParams(vmem_limit_bytes=VMEM_BYTES),
        cost_estimate=cost(unit, 8 * width * channels),
    )(pieces, decays)
    own, other, _ = lax.optimization_barrier((own, other, pieces))
    first_out = swap_chips(swap_cores(own, other))
    end = seg_exchange(ends).reshape(width, channels)


    total = lax.dynamic_slice_in_dim(decays, lax.axis_index("seg"), 1, 0)
    grads, rate_grad = pl.pallas_call(
        backward_kernel,
        grid=(blocks,),
        in_specs=[
            back["main"], back["side"], back["dt"], back["main"], back["per_head"],
            back["main"], back["mixed"], back["state"], back["decay"],
            whole(end), pl.BlockSpec((width, channels), lambda i: (0, 0)), whole(start), whole(total),
            back["per_head"], whole(rate_row), whole(skip_row), whole(expand), whole(collect),
        ],
        out_specs=[
            pl.BlockSpec((BLOCK, packed_width), lambda i: (blocks - 1 - i, 0)),
            pl.BlockSpec((1, LANES), lambda i: (0, 0)),
        ],
        out_shape=[
            jax.ShapeDtypeStruct((length, packed_width), BF16),
            jax.ShapeDtypeStruct((1, LANES), F32),
        ],
        scratch_shapes=[pltpu.VMEM((8, LANES), F32)],
        compiler_params=params(),
        cost_estimate=cost(8 * unit, 16 * length * channels),
    )(
        xbd, xbd, xbd, dyc, weight, grad_inner, inside_b, later, decay_after,
        end, state, start, total, dots, rate_row, skip_row, expand, collect,
    )
    grads, _ = lax.optimization_barrier((grads, first_out[1:]))
    second_out = exchange(grads.reshape(shards, rows, packed_width))

    skip_grad = skip_grad.reshape(heads, HEAD_DIM).sum(axis=1)
    sums = jnp.concatenate([rate_grad[0, :heads], skip_grad])
    sums = seg_sum(jnp.pad(sums, (0, LANES - 2 * heads))[None])[0]

    grad_x, grad_b, grad_dt = pl.pallas_call(
        lambda *refs: unpack_kernel(heads, *refs),
        grid=(shards // 2,),
        in_specs=[pl.BlockSpec((2, rows, packed_width), lambda i: (i, 0, 0))],
        out_specs=[
            pl.BlockSpec((rows, 2 * channels), lambda i: (0, i)),
            pl.BlockSpec((rows, 2 * width), lambda i: (0, i)),
            pl.BlockSpec((rows, LANES), lambda i: (0, 0)),
        ],
        out_shape=[jax.ShapeDtypeStruct(like.shape, BF16) for like in (inputs, b_rows, dt_rows)],
        compiler_params=params(),
        cost_estimate=cost(rows, 4 * shards * rows * packed_width),
    )(second_out)
    outputs, grad_c = pl.pallas_call(
        lambda *refs: unpack_pairs_kernel(len(first_out), *refs),
        out_shape=[jax.ShapeDtypeStruct(like.shape, BF16) for like in (inputs, c_rows)],
        compiler_params=pltpu.CompilerParams(vmem_limit_bytes=VMEM_BYTES),
        cost_estimate=cost(rows, 4 * shards * rows * pair_width),
    )(*first_out)
    return outputs, grad_x, grad_b, grad_c, grad_dt, sums[:heads], sums[heads : 2 * heads]


def solution(mesh):
    by_rows = P(("dp", "seg", "head"), None)
    in_specs = (by_rows, by_rows, by_rows, by_rows, P(), P(), by_rows)
    out_specs = (by_rows, by_rows, by_rows, by_rows, by_rows, P(("dp", "head")), P(("dp", "head")))
    return jax.shard_map(on_device, mesh=mesh, in_specs=in_specs, out_specs=out_specs, check_vma=False)
```

time: 233 us -> 224 us (0.961)
  local copies, waits for them, and re-layouts: 34.9 us -> 18 us
  waiting for transfers between devices: 69.6 us -> 83.2 us
  other arithmetic: 11.5 us -> 1.3 us
  starting transfers between devices: 44.3 us -> 52 us
  Pallas kernels: 69.6 us -> 66.4 us
    pallas_call x2 -> x7, Pallas kernels: 12.1 us -> 29.2 us  [the longest x1 13.4 us: on_device(): pl.pallas_call(inside_kernel, grid=(blocks,), in_specs=[onward[name] for...]
    all_to_all x2, waiting for transfers between devices: 20.6 us -> 36.4 us  [exchange(): return lax.all_to_all(value, 'head', 0, 0)]
    pallas_call x1, Pallas kernels: 20 us -> 9.64 us  [on_device(): pl.pallas_call(forward_kernel, grid=(blocks,), in_specs=[onward['main'],...]
    reshape x3 -> x0, local copies, waits for them, and re-layouts: 9.25 us -> none  [the longest x1 5.27 us: by_core(): value.reshape(-1, 2, *value.shape[1:])]
    another operation x5 -> x0, other arithmetic: 8.41 us -> none  [the longest x4 6.6 us: swap_cores(): jnp.stack([jnp.where(core == 0, own, swapped), jnp.where(core == 0, swapp...]
    unnamed x29 -> x48, local copies, waits for them, and re-layouts: 7.92 us -> 15.7 us
    pallas_call x1, Pallas kernels: 19.6 us -> 12.2 us  [on_device(): pl.pallas_call(backward_kernel, grid=(blocks,), in_specs=[back['main'], b...]
    ppermute x6, waiting for transfers between devices: 9.76 us -> 16.2 us  [permute(): lax.ppermute(value, 'head', [(i, (i + 2 * hop) % count) for i in range(co...]
  transfers between devices with their start and end apart: 18 -> 18, of which waited for: 10 -> 12; matrix products, arithmetic and copies ran while one was open for 17% -> 2% of each run, Pallas kernels for 24% -> 28%
where the time goes in v3:
time: 224 us; the launch traced here: 222 us
  waiting for transfers between devices  83.2 us (37%)
  Pallas kernels  66.4 us (30%)
  starting transfers between devices  52 us (23%)
  local copies, waits for them, and re-layouts  18 us (8%)
    all_to_all x2, waiting for transfers between devices, exchange(): return lax.all_to_all(value, 'head', 0, 0)  36.4 us
    all_to_all x4, starting transfers between devices, seg_exchange(): lax.all_to_all(state.reshape(count, -1, state.shape[-1]), 'seg', 0, 0)  24.2 us
    all_to_all x4, waiting for transfers between devices, seg_exchange(): lax.all_to_all(state.reshape(count, -1, state.shape[-1]), 'seg', 0, 0)  19.1 us
    ppermute x6, waiting for transfers between devices, permute(): lax.ppermute(value, 'head', [(i, (i + 2 * hop) % count) for i in range(co...  16.2 us
    unnamed x48, local copies, waits for them, and re-layouts  15.7 us
    pallas_call x1, Pallas kernels, on_device(): pl.pallas_call(inside_kernel, grid=(blocks,), in_specs=[onward[name] for...  13.4 us
    pallas_call x1, Pallas kernels, on_device(): pl.pallas_call(backward_kernel, grid=(blocks,), in_specs=[back['main'], b...  12.2 us
    ppermute x6, starting transfers between devices, permute(): lax.ppermute(value, 'head', [(i, (i + 2 * hop) % count) for i in range(co...  9.72 us
  transfers between devices with their start and end apart: 18, of which 12 were waited for; matrix products, arithmetic and copies ran while one was open for 2% of the time, Pallas kernels for 28%

profile of v3, /device:TPU:0, one launch (start us, length us, event | category | flops | bytes accessed | tf_op | source)
XLA Modules:
  0.0 221.9 jit_solution(5241402435912754549)
XLA Ops:
  4.0 2.5 %shard_map.126 = bf16[8,128,1408]{2,1,0:T(8,128)(2,1)} custom-call(bf16[128,8192]{1,0:T(8,128)(2,1)S(1)} %copy-done.1, bf16[128,2048]{1,0:T(8,128)(2,1)S(1)} %copy-done.14, bf16[128,128]{1,0:T(8,128)(2,1)S(1)} %copy-done.16), custom_call_target="tpu_custom_call" | custom-call | flops 128 | bytes 5767168 | tf_op jit(solution)/shard_map/pallas_call | solution.py:345
  6.5 5.5 %all-to-all-start = ((bf16[8,128,1408]{2,1,0:T(8,128)(2,1)}), bf16[8,128,1408]{2,1,0:T(8,128)(2,1)}, u32[]{:S(2)}, u32[]{:S(2)}) async-start(bf16[8,128,1408]{2,1,0:T(8,128)(2,1)} %shard_map.126), calls=%async_computation | async-start | bytes 5767168 | tf_op jit(solution)/shard_map/all_to_all | solution.py:304
  12.0 3.7 %shard_map.127 = (bf16[4,128,1280]{2,1,0:T(8,128)(2,1)S(1)}, bf16[4,128,1280]{2,1,0:T(8,128)(2,1)}) custom-call(bf16[128,8192]{1,0:T(8,128)(2,1)} %dy_ref.1, bf16[128,2048]{1,0:T(8,128)(2,1)S(1)} %copy-done.11), custom_call_target="tpu_custom_call" | custom-call | flops 128 | bytes 5242880 | tf_op jit(solution)/shard_map/pallas_call | solution.py:361
  16.6 2.7 %collective-permute-done.swapped_ref = bf16[4,128,1280]{2,1,0:T(8,128)(2,1)} collective-permute-done((bf16[4,128,1280]{2,1,0:T(8,128)(2,1)}, bf16[4,128,1280]{2,1,0:T(8,128)(2,1)}, u32[]{:S(2)}, u32[]{:S(2)}) %collective-permute-start) | collective-permute-done | bytes 1310752 | tf_op jit(solution)/shard_map/ppermute | solution.py:310
  19.3 2.5 %shard_map.128 = (bf16[256,1280]{1,0:T(8,128)(2,1)S(1)}, bf16[256,1280]{1,0:T(8,128)(2,1)}, bf16[256,1280]{1,0:T(8,128)(2,1)S(1)}, bf16[256,1280]{1,0:T(8,128)(2,1)}) custom-call(bf16[4,128,1280]{2,1,0:T(8,128)(2,1)S(1)} %get-tuple-element.55.own_ref, bf16[4,128,1280]{2,1,0:T(8,128)(2,1)} %collective-permute-done.swapped_ref), custom_call_target="tpu_custom_call" | custom-call | flops 128 | bytes 10485760 | tf_op jit(solution)/shard_map/pallas_call | solution.py:311
  22.6 25.1 %all-to-all-done = bf16[8,128,1408]{2,1,0:T(8,128)(2,1)} async-done(((bf16[8,128,1408]{2,1,0:T(8,128)(2,1)}), bf16[8,128,1408]{2,1,0:T(8,128)(2,1)}, u32[]{:S(2)}, u32[]{:S(2)}) %all-to-all-start) | async-done | bytes 2883616 | tf_op jit(solution)/shard_map/all_to_all | solution.py:304
  48.3 2.7 %collective-permute-start.2 = (bf16[256,1280]{1,0:T(8,128)(2,1)}, bf16[256,1280]{1,0:T(8,128)(2,1)}, u32[]{:S(2)}, u32[]{:S(2)}) collective-permute-start(bf16[256,1280]{1,0:T(8,128)(2,1)} %get-tuple-element.66), channel_id=1, source_target_pairs={{0,6},{1,7},{2,0},{3,1},{4,2},{5,3},{6,4},{7,5},{8,14},{9,15},{10,... | collective-permute-start | bytes 1966088 | tf_op jit(solution)/shard_map/ppermute | solution.py:323
  51.0 6.9 %shard_map.129 = (f32[256,1152]{1,0:T(8,128)}, bf16[1024,128]{1,0:T(8,128)(2,1)S(1)}, bf16[1024,128]{1,0:T(8,128)(2,1)S(1)}, f32[4,256,1024]{2,1,0:T(8,128)}, f32[4,1,1024]{2,1,0:T(1,128)S(1)}) custom-call(bf16[1024,1408]{1,0:T(8,128)(2,1)} %bitcast.refs_0_.refs_1_.refs_2_.x_ref.b_ref.dt_ref, ...), custom_call_target="tpu_custom_call" | custom-call | flops 3221225472 | bytes 4194304 | tf_op jit(solution)/shard_map/pallas_call | solution.py:409
  57.9 7.0 %all-to-all-start.1 = ((f32[16,16,1152]{2,1,0:T(8,128)}), f32[16,16,1152]{2,1,0:T(8,128)S(1)}, u32[]{:S(2)}, u32[]{:S(2)}) async-start(f32[16,16,1152]{2,1,0:T(8,128)} %bitcast.1), calls=%async_computation.1 | async-start | bytes 2359296 | tf_op jit(solution)/shard_map/all_to_all | solution.py:292
  67.0 16.1 %all-to-all-done.1.refs_0_ = f32[16,16,1152]{2,1,0:T(8,128)S(1)} async-done(((f32[16,16,1152]{2,1,0:T(8,128)}), f32[16,16,1152]{2,1,0:T(8,128)S(1)}, u32[]{:S(2)}, u32[]{:S(2)}) %all-to-all-start.1) | async-done | bytes 1179680 | tf_op jit(solution)/shard_map/all_to_all | solution.py:292
  84.4 5.4 %all-to-all-start.2 = ((f32[16,16,1024]{2,1,0:T(8,128)}), f32[16,16,1024]{2,1,0:T(8,128)S(1)}, u32[]{:S(2)}, u32[]{:S(2)}) async-start(f32[16,16,1024]{2,1,0:T(8,128)} %get-tuple-element.76), calls=%async_computation.2 | async-start | bytes 2097152 | tf_op jit(solution)/shard_map/all_to_all | solution.py:292
  89.8 6.1 %shard_map.130 = (f32[256,1024]{1,0:T(8,128)}, bf16[1024,1280]{1,0:T(8,128)(2,1)}, f32[4,256,1024]{2,1,0:T(8,128)}, f32[4,1,1024]{2,1,0:T(1,128)S(1)}) custom-call(bf16[1024,128]{1,0:T(8,128)(2,1)S(1)} %get-tuple-element.62.refs_0_.growth_ref, bf16[128,1024]{1,0:T(8,128)(2,1)S(1)} %and_convert_fusion.refs_4_.refs_1_.expand_ref, ...), custom_call_target="tpu_custom_call" | custom-call | flops 3221225472 | bytes 4194304 | tf_op jit(solution)/shard_map/pallas_call | solution.py:441
  95.9 13.4 %shard_map.131 = (f32[1024,1024]{1,0:T(8,128)}, f32[1024,1024]{1,0:T(8,128)}, f32[1024,256]{1,0:T(8,128)S(1)}, f32[1024,256]{1,0:T(8,128)S(1)}, f32[1,1024]{1,0:T(1,128)S(1)}) custom-call(bf16[1024,1408]{1,0:T(8,128)(2,1)} %bitcast.refs_0_.refs_1_.refs_2_.x_ref.b_ref.dt_ref, bf16[1024,1408]{1,0:T(8,128)(2,1)} %bitcast.refs_0_.refs_1_.refs_2_.x_ref.b_ref.dt_ref, ...), custom_call_target="tpu_custom_call" | custom-call | flops 6442450944 | bytes 16777216 | tf_op jit(solution)/shard_map/pallas_call | solution.py:458
  111.2 7.3 %all-to-all-start.3 = ((f32[16,16,1024]{2,1,0:T(8,128)}), f32[16,16,1024]{2,1,0:T(8,128)S(1)}, u32[]{:S(2)}, u32[]{:S(2)}) async-start(f32[16,16,1024]{2,1,0:T(8,128)} %bitcast.20), calls=%async_computation.3 | async-start | bytes 2097152 | tf_op jit(solution)/shard_map/all_to_all | solution.py:292
  120.3 9.6 %shard_map.133 = (bf16[4,128,1280]{2,1,0:T(8,128)(2,1)}, bf16[4,128,1280]{2,1,0:T(8,128)(2,1)}, f32[1024,128]{1,0:T(8,128)S(1)}) custom-call(bf16[1024,1408]{1,0:T(8,128)(2,1)} %bitcast.refs_0_.refs_1_.refs_2_.x_ref.b_ref.dt_ref, bf16[1024,1280]{1,0:T(8,128)(2,1)} %get-tuple-element.68.dy_ref.c_ref, bf16[1024,1280]{1,0:T(8,128)(2,1)} %get-tuple-element.68.dy_ref.c_ref, ...), custom_call_target="tpu_custom_call" | custom-call | flops 4294967296 | bytes 16777216 | tf_op jit(solution)/shard_map/pallas_call | solution.py:477
  130.7 2.9 %all-to-all-done.3.pieces_ref = f32[16,16,1024]{2,1,0:T(8,128)S(1)} async-done(((f32[16,16,1024]{2,1,0:T(8,128)}), f32[16,16,1024]{2,1,0:T(8,128)S(1)}, u32[]{:S(2)}, u32[]{:S(2)}) %all-to-all-start.3) | async-done | bytes 1048608 | tf_op jit(solution)/shard_map/all_to_all | solution.py:292
  134.8 4.4 %all-to-all-start.4 = ((f32[16,16,1024]{2,1,0:T(8,128)}), f32[16,16,1024]{2,1,0:T(8,128)S(1)}, u32[]{:S(2)}, u32[]{:S(2)}) async-start(f32[16,16,1024]{2,1,0:T(8,128)} %shard_map.136), calls=%async_computation.4 | async-start | bytes 2097152 | tf_op jit(solution)/shard_map/all_to_all | solution.py:292
  140.5 2.3 %shard_map.134 = (bf16[256,1280]{1,0:T(8,128)(2,1)S(1)}, bf16[256,1280]{1,0:T(8,128)(2,1)S(1)}, bf16[256,1280]{1,0:T(8,128)(2,1)}, bf16[256,1280]{1,0:T(8,128)(2,1)S(1)}) custom-call(bf16[4,128,1280]{2,1,0:T(8,128)(2,1)S(1)} %copy-done.2, bf16[4,128,1280]{2,1,0:T(8,128)(2,1)} %collective-permute-done.4.swapped_ref), custom_call_target="tpu_custom_call" | custom-call | flops 128 | bytes 10485760 | tf_op jit(solution)/shard_map/pallas_call | solution.py:311
  143.1 3.0 %collective-permute-start.6 = (bf16[256,1280]{1,0:T(8,128)(2,1)S(1)}, bf16[256,1280]{1,0:T(8,128)(2,1)S(1)}, u32[]{:S(2)}, u32[]{:S(2)}) collective-permute-start(bf16[256,1280]{1,0:T(8,128)(2,1)S(1)} %get-tuple-element.86), channel_id=1, source_target_pairs={{0,6},{1,7},{2,0},{3,1},{4,2},{5,3},{6,4},{7,5},{8,14},{9,15},{10,... | collective-permute-start | bytes 1966088 | tf_op jit(solution)/shard_map/ppermute | solution.py:323
  146.1 14.8 %collective-permute-done.5.refs_1_ = bf16[256,1280]{1,0:T(8,128)(2,1)S(1)} collective-permute-done((bf16[256,1280]{1,0:T(8,128)(2,1)S(1)}, bf16[256,1280]{1,0:T(8,128)(2,1)S(1)}, u32[]{:S(2)}, u32[]{:S(2)}) %collective-permute-start.5) | collective-permute-done | bytes 655392 | tf_op jit(solution)/shard_map/ppermute | solution.py:323
  162.7 1.8 collective-permute-start.7
  167.0 12.2 %shard_map.137 = (bf16[1024,1408]{1,0:T(8,128)(2,1)}, f32[1,128]{1,0:T(1,128)S(1)}) custom-call(bf16[1024,1408]{1,0:T(8,128)(2,1)} %bitcast.refs_0_.refs_1_.refs_2_.x_ref.b_ref.dt_ref, bf16[1024,1408]{1,0:T(8,128)(2,1)} %bitcast.refs_0_.refs_1_.refs_2_.x_ref.b_ref.dt_ref, bf16[1024,1408]{1,0:T(8,128)(2,1)} %bitcast.refs_0_.refs_1_.refs_2_.x_ref.b_ref.dt_ref, ...), custom_call_target="tpu_custom_call" | custom-call | flops 4294967296 | bytes 16777216 | tf_op jit(solution)/shard_map/pallas_call | solution.py:502
  180.6 3.8 %all-to-all-start.5 = ((bf16[8,128,1408]{2,1,0:T(8,128)(2,1)}), bf16[8,128,1408]{2,1,0:T(8,128)(2,1)S(1)}, u32[]{:S(2)}, u32[]{:S(2)}) async-start(bf16[8,128,1408]{2,1,0:T(8,128)(2,1)} %bitcast.19), calls=%async_computation.5 | async-start | bytes 5767168 | tf_op jit(solution)/shard_map/all_to_all | solution.py:304
  187.1 2.2 collective-permute-done.8
  189.4 2.8 %collective-permute-start.9 = (f32[1,128]{1,0:T(1,128)S(1)}, f32[1,128]{1,0:T(1,128)S(1)}, u32[]{:S(2)}, u32[]{:S(2)}) collective-permute-start(f32[1,128]{1,0:T(1,128)S(1)} %fusion.5), channel_id=1, source_target_pairs={{0,16},{8,24},{16,0},{24,8},{32,48},{40,56},{48,32},{56,40},{64,80... | collective-permute-start | bytes 1544 | tf_op jit(solution)/shard_map/ppermute | solution.py:298
  192.3 2.2 collective-permute-done.9
  195.8 2.2 collective-permute-done.10
  198.0 2.8 %collective-permute-start.11 = (f32[1,128]{1,0:T(1,128)S(1)}, f32[1,128]{1,0:T(1,128)S(1)}, u32[]{:S(2)}, u32[]{:S(2)}) collective-permute-start(f32[1,128]{1,0:T(1,128)S(1)} %add.55), channel_id=1, source_target_pairs={{0,64},{8,72},{16,80},{24,88},{32,96},{40,104},{48,112},{56,120},{... | collective-permute-start | bytes 1544 | tf_op jit(solution)/shard_map/ppermute | solution.py:298
  200.9 2.2 collective-permute-done.11
  205.8 2.8 %shard_map.135 = (bf16[128,8192]{1,0:T(8,128)(2,1)}, bf16[128,2048]{1,0:T(8,128)(2,1)}) custom-call(bf16[256,1280]{1,0:T(8,128)(2,1)S(1)} %get-tuple-element.83.refs_0_, bf16[256,1280]{1,0:T(8,128)(2,1)S(1)} %copy-done.8, bf16[256,1280]{1,0:T(8,128)(2,1)} %collective-permute-done.7.refs_2_, bf16[256,1280]{1,0:T(8,128)(2,1)S(1)} %copy-done.10), custom_call_target="tpu_custom_call" | custom-call | flops 128 | bytes 5242880 | tf_op jit(solution)/shard_map/pallas_call | solution.py:546
  208.6 11.3 %all-to-all-done.5.refs_0_ = bf16[8,128,1408]{2,1,0:T(8,128)(2,1)S(1)} async-done(((bf16[8,128,1408]{2,1,0:T(8,128)(2,1)}), bf16[8,128,1408]{2,1,0:T(8,128)(2,1)S(1)}, u32[]{:S(2)}, u32[]{:S(2)}) %all-to-all-start.5) | async-done | bytes 2883616 | tf_op jit(solution)/shard_map/all_to_all | solution.py:304
  219.9 2.0 shard_map.138
  (89 shorter events, 28.5 us)
Async XLA Ops:
  0.6 1.6 copy-start.1
  6.5 5.5 %copy-start.11 = (bf16[128,2048]{1,0:T(8,128)(2,1)S(1)}, bf16[128,2048]{1,0:T(8,128)(2,1)}, u32[]{:S(2)}) copy-start(bf16[128,2048]{1,0:T(8,128)(2,1)} %c_ref.1) | copy-start | bytes 1572868
  6.5 41.3 %all-to-all-start = ((bf16[8,128,1408]{2,1,0:T(8,128)(2,1)}), bf16[8,128,1408]{2,1,0:T(8,128)(2,1)}, u32[]{:S(2)}, u32[]{:S(2)}) async-start(bf16[8,128,1408]{2,1,0:T(8,128)(2,1)} %shard_map.126), calls=%async_computation | async-start | bytes 5767168 | tf_op jit(solution)/shard_map/all_to_all | solution.py:304
  12.0 4.3 %copy-start.22 = (f32[128]{0:T(128)S(1)}, f32[128]{0:T(128)}, u32[]{:S(2)}) copy-start(f32[128]{0:T(128)} %param.11) | copy-start | bytes 1540
  15.8 3.5 %collective-permute-start = (bf16[4,128,1280]{2,1,0:T(8,128)(2,1)}, bf16[4,128,1280]{2,1,0:T(8,128)(2,1)}, u32[]{:S(2)}, u32[]{:S(2)}) collective-permute-start(bf16[4,128,1280]{2,1,0:T(8,128)(2,1)} %get-tuple-element.56), channel_id=1, source_target_pairs={{0,1},{1,0},{2,3},{3,2},{4,5},{5,4},{6,7},{7,6},{8,9},{9,8},{10,11... | collective-permute-start | bytes 3932168 | tf_op jit(solution)/shard_map/ppermute | solution.py:310
  47.8 17.8 %collective-permute-start.1 = (bf16[256,1280]{1,0:T(8,128)(2,1)}, bf16[256,1280]{1,0:T(8,128)(2,1)}, u32[]{:S(2)}, u32[]{:S(2)}) collective-permute-start(bf16[256,1280]{1,0:T(8,128)(2,1)} %get-tuple-element.64), channel_id=1, source_target_pairs={{0,2},{1,3},{2,4},{3,5},{4,6},{5,7},{6,0},{7,1},{8,10},{9,11},{10,... | collective-permute-start | bytes 1966088 | tf_op jit(solution)/shard_map/ppermute | solution.py:323
  48.3 17.2 %collective-permute-start.2 = (bf16[256,1280]{1,0:T(8,128)(2,1)}, bf16[256,1280]{1,0:T(8,128)(2,1)}, u32[]{:S(2)}, u32[]{:S(2)}) collective-permute-start(bf16[256,1280]{1,0:T(8,128)(2,1)} %get-tuple-element.66), channel_id=1, source_target_pairs={{0,6},{1,7},{2,0},{3,1},{4,2},{5,3},{6,4},{7,5},{8,14},{9,15},{10,... | collective-permute-start | bytes 1966088 | tf_op jit(solution)/shard_map/ppermute | solution.py:323
  57.9 25.3 %all-to-all-start.1 = ((f32[16,16,1152]{2,1,0:T(8,128)}), f32[16,16,1152]{2,1,0:T(8,128)S(1)}, u32[]{:S(2)}, u32[]{:S(2)}) async-start(f32[16,16,1152]{2,1,0:T(8,128)} %bitcast.1), calls=%async_computation.1 | async-start | bytes 2359296 | tf_op jit(solution)/shard_map/all_to_all | solution.py:292
  65.6 18.9 %collective-permute-start.3 = (bf16[256,1280]{1,0:T(8,128)(2,1)}, bf16[256,1280]{1,0:T(8,128)(2,1)}, u32[]{:S(2)}, u32[]{:S(2)}) collective-permute-start(bf16[256,1280]{1,0:T(8,128)(2,1)} %copy-done.19), channel_id=1, source_target_pairs={{0,4},{1,5},{2,6},{3,7},{4,0},{5,1},{6,2},{7,3},{8,12},{9,13},{10,... | collective-permute-start | bytes 1966088 | tf_op jit(solution)/shard_map/ppermute | solution.py:323
  84.4 49.2 %copy-start.15 = (f32[16,1024]{1,0:T(8,128)}, f32[16,1024]{1,0:T(8,128)S(1)}, u32[]{:S(2)}) copy-start(f32[16,1024]{1,0:T(8,128)S(1)} %get-tuple-element.93.decay_ref) | copy-start | bytes 196612
  84.4 26.8 %all-to-all-start.2 = ((f32[16,16,1024]{2,1,0:T(8,128)}), f32[16,16,1024]{2,1,0:T(8,128)S(1)}, u32[]{:S(2)}, u32[]{:S(2)}) async-start(f32[16,16,1024]{2,1,0:T(8,128)} %get-tuple-element.76), calls=%async_computation.2 | async-start | bytes 2097152 | tf_op jit(solution)/shard_map/all_to_all | solution.py:292
  95.9 13.4 %copy-start.17 = (f32[4,1,1024]{2,1,0:T(1,128)}, f32[4,1,1024]{2,1,0:T(1,128)S(1)}, u32[]{:S(2)}) copy-start(f32[4,1,1024]{2,1,0:T(1,128)S(1)} %get-tuple-element.92.decay_ref) | copy-start | bytes 49156
  111.2 7.4 %copy-start.23 = (f32[128]{0:T(128)S(1)}, f32[128]{0:T(128)}, u32[]{:S(2)}) copy-start(f32[128]{0:T(128)} %param.12) | copy-start | bytes 1540
  111.2 18.7 %copy-start = (f32[16,16,1024]{2,1,0:T(8,128)}, f32[16,16,1024]{2,1,0:T(8,128)S(1)}, u32[]{:S(2)}) copy-start(f32[16,16,1024]{2,1,0:T(8,128)S(1)} %all-to-all-done.2) | copy-start | bytes 3145732
  111.2 22.4 %all-to-all-start.3 = ((f32[16,16,1024]{2,1,0:T(8,128)}), f32[16,16,1024]{2,1,0:T(8,128)S(1)}, u32[]{:S(2)}, u32[]{:S(2)}) async-start(f32[16,16,1024]{2,1,0:T(8,128)} %bitcast.20), calls=%async_computation.3 | async-start | bytes 2097152 | tf_op jit(solution)/shard_map/all_to_all | solution.py:292
  119.0 1.2 copy-start.6
  133.6 5.6 %collective-permute-start.4 = (bf16[4,128,1280]{2,1,0:T(8,128)(2,1)}, bf16[4,128,1280]{2,1,0:T(8,128)(2,1)}, u32[]{:S(2)}, u32[]{:S(2)}) collective-permute-start(bf16[4,128,1280]{2,1,0:T(8,128)(2,1)} %get-tuple-element.82), channel_id=1, source_target_pairs={{0,1},{1,0},{2,3},{3,2},{4,5},{5,4},{6,7},{7,6},{8,9},{9,8},{10,11... | collective-permute-start | bytes 3932168 | tf_op jit(solution)/shard_map/ppermute | solution.py:310
  134.8 30.5 %copy-start.4 = (f32[1024,256]{1,0:T(8,128)S(1)}, f32[1024,256]{1,0:T(8,128)}, u32[]{:S(2)}) copy-start(f32[1024,256]{1,0:T(8,128)} %copy-done.3) | copy-start | bytes 3145732
  134.8 30.4 %all-to-all-start.4 = ((f32[16,16,1024]{2,1,0:T(8,128)}), f32[16,16,1024]{2,1,0:T(8,128)S(1)}, u32[]{:S(2)}, u32[]{:S(2)}) async-start(f32[16,16,1024]{2,1,0:T(8,128)} %shard_map.136), calls=%async_computation.4 | async-start | bytes 2097152 | tf_op jit(solution)/shard_map/all_to_all | solution.py:292
  139.2 1.3 copy-start.2
  142.9 18.1 %collective-permute-start.5 = (bf16[256,1280]{1,0:T(8,128)(2,1)S(1)}, bf16[256,1280]{1,0:T(8,128)(2,1)S(1)}, u32[]{:S(2)}, u32[]{:S(2)}) collective-permute-start(bf16[256,1280]{1,0:T(8,128)(2,1)S(1)} %get-tuple-element.84), channel_id=1, source_target_pairs={{0,2},{1,3},{2,4},{3,5},{4,6},{5,7},{6,0},{7,1},{8,10},{9,11},{10,... | collective-permute-start | bytes 1966088 | tf_op jit(solution)/shard_map/ppermute | solution.py:323
  143.1 18.7 %collective-permute-start.6 = (bf16[256,1280]{1,0:T(8,128)(2,1)S(1)}, bf16[256,1280]{1,0:T(8,128)(2,1)S(1)}, u32[]{:S(2)}, u32[]{:S(2)}) collective-permute-start(bf16[256,1280]{1,0:T(8,128)(2,1)S(1)} %get-tuple-element.86), channel_id=1, source_target_pairs={{0,6},{1,7},{2,0},{3,1},{4,2},{5,3},{6,4},{7,5},{8,14},{9,15},{10,... | collective-permute-start | bytes 1966088 | tf_op jit(solution)/shard_map/ppermute | solution.py:323
  162.7 17.9 %collective-permute-start.7 = (bf16[256,1280]{1,0:T(8,128)(2,1)}, bf16[256,1280]{1,0:T(8,128)(2,1)}, u32[]{:S(2)}, u32[]{:S(2)}) collective-permute-start(bf16[256,1280]{1,0:T(8,128)(2,1)} %get-tuple-element.87), channel_id=1, source_target_pairs={{0,4},{1,5},{2,6},{3,7},{4,0},{5,1},{6,2},{7,3},{8,12},{9,13},{10,... | collective-permute-start | bytes 1966088 | tf_op jit(solution)/shard_map/ppermute | solution.py:323
  165.3 1.0 copy-start.13
  180.6 5.2 %copy-start.21 = (f32[1,128]{1,0:T(1,128)S(1)}, f32[1,128]{1,0:T(1,128)}, u32[]{:S(2)}) copy-start(f32[1,128]{1,0:T(1,128)} %copy-done.20) | copy-start | bytes 1540
  180.6 39.3 %all-to-all-start.5 = ((bf16[8,128,1408]{2,1,0:T(8,128)(2,1)}), bf16[8,128,1408]{2,1,0:T(8,128)(2,1)S(1)}, u32[]{:S(2)}, u32[]{:S(2)}) async-start(bf16[8,128,1408]{2,1,0:T(8,128)(2,1)} %bitcast.19), calls=%async_computation.5 | async-start | bytes 5767168 | tf_op jit(solution)/shard_map/all_to_all | solution.py:304
  185.8 3.6 %collective-permute-start.8 = (f32[1,128]{1,0:T(1,128)S(1)}, f32[1,128]{1,0:T(1,128)S(1)}, u32[]{:S(2)}, u32[]{:S(2)}) collective-permute-start(f32[1,128]{1,0:T(1,128)S(1)} %fusion.4), channel_id=1, source_target_pairs={{0,8},{8,0},{16,24},{24,16},{32,40},{40,32},{48,56},{56,48},{64,72... | collective-permute-start | bytes 1544 | tf_op jit(solution)/shard_map/ppermute | solution.py:298
  189.4 5.1 %collective-permute-start.9 = (f32[1,128]{1,0:T(1,128)S(1)}, f32[1,128]{1,0:T(1,128)S(1)}, u32[]{:S(2)}, u32[]{:S(2)}) collective-permute-start(f32[1,128]{1,0:T(1,128)S(1)} %fusion.5), channel_id=1, source_target_pairs={{0,16},{8,24},{16,0},{24,8},{32,48},{40,56},{48,32},{56,40},{64,80... | collective-permute-start | bytes 1544 | tf_op jit(solution)/shard_map/ppermute | solution.py:298
  194.5 3.5 %collective-permute-start.10 = (f32[1,128]{1,0:T(1,128)S(1)}, f32[1,128]{1,0:T(1,128)S(1)}, u32[]{:S(2)}, u32[]{:S(2)}) collective-permute-start(f32[1,128]{1,0:T(1,128)S(1)} %add.54), channel_id=1, source_target_pairs={{0,32},{8,40},{16,48},{24,56},{32,0},{40,8},{48,16},{56,24},{64,96... | collective-permute-start | bytes 1544 | tf_op jit(solution)/shard_map/ppermute | solution.py:298
  198.0 5.0 %collective-permute-start.11 = (f32[1,128]{1,0:T(1,128)S(1)}, f32[1,128]{1,0:T(1,128)S(1)}, u32[]{:S(2)}, u32[]{:S(2)}) collective-permute-start(f32[1,128]{1,0:T(1,128)S(1)} %add.55), channel_id=1, source_target_pairs={{0,64},{8,72},{16,80},{24,88},{32,96},{40,104},{48,112},{56,120},{... | collective-permute-start | bytes 1544 | tf_op jit(solution)/shard_map/ppermute | solution.py:298
  203.7 1.1 copy-start.8
  204.8 1.1 copy-start.10
  (10 other events, 8.3 us)

commit v4 on v3

--- a/solution.py
+++ b/solution.py
@@ -125,7 +125,7 @@
 
 def state_kernel(
     heads, x_ref, b_ref, dt_ref, rate_ref, expand_ref,
-    out_ref, growth_ref, weight_ref, before_ref, decay_ref, so_far,
+    out_ref, growth_ref, weight_ref, high_ref, low_ref, before_ref, decay_ref, so_far,
 ):
     block = pl.program_id(0)
     channels = x_ref.shape[1]
@@ -149,6 +149,7 @@
     ends = pl.ds(pl.multiple_of(block * BLOCK + BLOCK - 16, 16), 16)
     spread = expand_ref[...]
     high, low = split2(x_ref[...].astype(F32) * dot(weight_ref[rows, :], spread))
+    high_ref[...], low_ref[...] = high, low
     decay = dot(growth_ref[ends, :], spread)[15:]
     b_t = b_ref[...].T
     state = out_ref[:, :channels]
@@ -159,7 +160,7 @@
 
 
 def grad_state_kernel(pieces, growth_ref, expand_ref, *refs):
-    piece_refs, (out_ref, dyc_ref, later_ref, decay_ref, so_far) = refs[:pieces], refs[pieces:]
+    piece_refs, (out_ref, dyc_ref, high_ref, low_ref, later_ref, decay_ref, so_far) = refs[:pieces], refs[pieces:]
     channels = out_ref.shape[1]
     block = pl.num_programs(0) - 1 - pl.program_id(0)
     hop = lax.rem(lax.axis_index("head") // 2 - block + pieces, pieces)
@@ -177,6 +178,7 @@
     grow = dot(growth_ref[...], expand_ref[...])
     decay = grow[BLOCK - 1 :]
     high, low = split2(dyc_ref[:, :channels].astype(F32) * grow)
+    high_ref[...], low_ref[...] = high, low
     c_t = dyc_ref[:, channels:].T
     later = out_ref[...] * decay
     later_ref[...] = later
@@ -186,30 +188,33 @@
 
 
 def inside_kernel(
-    x_ref, b_ref, dy_ref, c_ref, growth_ref, weight_ref, expand_ref,
-    inner_ref, grad_inner_ref, grad_b_ref, grad_c_ref, skip_grad_ref,
+    x_ref, x_high_ref, x_low_ref, b_ref, dy_ref, d_high_ref, d_low_ref, c_ref,
+    inner_ref, grad_b_ref, grad_c_ref, skip_grad_ref,
 ):
     @pl.when(pl.program_id(0) == 0)
     def _():
         skip_grad_ref[...] = jnp.zeros_like(skip_grad_ref)
 
     b, c = b_ref[...], c_ref[...]
-    x, dy = x_ref[...].astype(F32), dy_ref[...].astype(F32)
-    skip_grad_ref[...] += jnp.sum(dy * x, axis=0, keepdims=True)
-    x_high, x_low = split2(x * dot(weight_ref[...], expand_ref[...]))
-    d_high, d_low = split2(dy * dot(growth_ref[...], expand_ref[...]))
+    skip_grad_ref[...] += jnp.sum(dy_ref[...].astype(F32) * x_ref[...].astype(F32), axis=0, keepdims=True)
+    x_high, x_low, d_high, d_low = x_high_ref[...], x_low_ref[...], d_high_ref[...], d_low_ref[...]
     causal = iota((BLOCK, BLOCK), 0) >= iota((BLOCK, BLOCK), 1)
-    anticausal = iota((BLOCK, BLOCK), 0) <= iota((BLOCK, BLOCK), 1)
     k_high, k_low = split2(jnp.where(causal, dot_nt(c, b), 0.0))
     inner_ref[...] = dot(k_high, x_high) + dot(k_high, x_low) + dot(k_low, x_high)
-    k_high, k_low = split2(jnp.where(anticausal, dot_nt(b, c), 0.0))
-    grad_inner_ref[...] = dot(k_high, d_high) + dot(k_high, d_low) + dot(k_low, d_high)
     mixed = dot_nt(d_high, x_high) + dot_nt(d_high, x_low) + dot_nt(d_low, x_high)
     mixed = jnp.where(causal, mixed, 0.0)
     q_high, q_low = split2(mixed)
     grad_c_ref[...] = dot(q_high, b) + dot(q_low, b)
     q_high, q_low = split2(mixed.T)
     grad_b_ref[...] = dot(q_high, c) + dot(q_low, c)
+
+
+def inside_grad_kernel(b_ref, d_high_ref, d_low_ref, c_ref, state_ref, start_ref, total_ref, out_ref, final_ref):
+    final_ref[...] = state_ref[...] + total_ref[...] * start_ref[...]
+    d_high, d_low = d_high_ref[...], d_low_ref[...]
+    anticausal = iota((BLOCK, BLOCK), 0) <= iota((BLOCK, BLOCK), 1)
+    k_high, k_low = split2(jnp.where(anticausal, dot_nt(b_ref[...], c_ref[...]), 0.0))
+    out_ref[...] = dot(k_high, d_high) + dot(k_high, d_low) + dot(k_low, d_high)
 
 
 def forward_kernel(
@@ -231,15 +236,14 @@
 
 def backward_kernel(
     x_ref, b_ref, dt_ref, dy_ref, weight_ref, inner_ref, grad_b_ref, later_ref, decay_ref, end_ref,
-    state_ref, start_ref, total_ref, dots_ref, rate_ref, skip_ref, expand_ref, collect_ref,
+    final_ref, dots_ref, rate_ref, skip_ref, expand_ref, collect_ref,
     out_ref, rate_grad_ref, after,
 ):
     channels, width = x_ref.shape[1], b_ref.shape[1]
 
     @pl.when(pl.program_id(0) == 0)
     def _():
-        final = state_ref[...] + total_ref[...] * start_ref[...]
-        meet = jnp.sum(final * end_ref[...], axis=0, keepdims=True)
+        meet = jnp.sum(final_ref[...] * end_ref[...], axis=0, keepdims=True)
         after[...] = gather_heads(jnp.broadcast_to(meet, (8, channels)), collect_ref[...])
         rate_grad_ref[...] = jnp.zeros_like(rate_grad_ref)
 
@@ -279,8 +283,8 @@
         total = total * decay_ref[index : index + 1] + pieces_ref[index]
 
 
-def params():
-    return pltpu.CompilerParams(vmem_limit_bytes=VMEM_BYTES, dimension_semantics=("arbitrary",))
+def params(mebibytes=VMEM_BYTES >> 20):
+    return pltpu.CompilerParams(vmem_limit_bytes=mebibytes << 20, dimension_semantics=("arbitrary",))
 
 
 def cost(flops, traffic):
@@ -316,7 +320,7 @@
     )(own, swapped)
 
 
-def swap_chips(sent):
+def swap_chips(sent, between):
     count = lax.axis_size("head")
 
     def permute(hop, value):
@@ -324,7 +328,7 @@
 
     came = {0: sent[0], 1: permute(1, sent[1]), len(sent) - 1: permute(len(sent) - 1, sent[-1])}
     for hop in range(2, len(sent) - 1):
-        value, _ = lax.optimization_barrier((sent[hop], list(came.values())[1:]))
+        value, *_ = lax.optimization_barrier((sent[hop], list(came.values())[1:], between))
         came[hop] = permute(hop, value)
     return [came[hop] for hop in range(len(sent))]
 
@@ -344,15 +348,15 @@
     packed_width, pair_width = channels + width + LANES, channels + width
     packed = pl.pallas_call(
         lambda *refs: pack_kernel(heads, *refs),
-        grid=(shards // 2,),
+        grid=(shards // 4,),
         in_specs=[
-            pl.BlockSpec((rows, 2 * channels), lambda i: (0, i)),
-            pl.BlockSpec((rows, 2 * width), lambda i: (0, i)),
+            pl.BlockSpec((rows, 4 * channels), lambda i: (0, i)),
+            pl.BlockSpec((rows, 4 * width), lambda i: (0, i)),
             pl.BlockSpec((rows, LANES), lambda i: (0, 0)),
         ],
-        out_specs=pl.BlockSpec((2, rows, packed_width), lambda i: (i, 0, 0)),
+        out_specs=pl.BlockSpec((4, rows, packed_width), lambda i: (i, 0, 0)),
         out_shape=jax.ShapeDtypeStruct((shards, rows, packed_width), BF16),
-        compiler_params=params(),
+        compiler_params=params(61),
         cost_estimate=cost(rows, 4 * shards * rows * packed_width),
     )(inputs, b_rows, dt_rows)
     first_in = exchange(packed)
@@ -371,7 +375,7 @@
         cost_estimate=cost(rows, 4 * shards * rows * pair_width),
     )(grad_out, c_rows)
     first_in, sent = lax.optimization_barrier((first_in, swap_cores(own, other)))
-    second_in = swap_chips(sent)
+    second_in = swap_chips(sent, None)
 
     length = rows * shards
     blocks = length // BLOCK
@@ -402,11 +406,12 @@
     state_shape = jax.ShapeDtypeStruct((width, channels), F32)
     states_shape = jax.ShapeDtypeStruct((blocks, width, channels), F32)
     terms_shape = jax.ShapeDtypeStruct((length, LANES), BF16)
+    main_shape = jax.ShapeDtypeStruct((length, channels), BF16)
     decays_shape = jax.ShapeDtypeStruct((blocks, 1, channels), F32)
     row_scratch = pltpu.VMEM((1, channels), F32)
     unit = 2 * length * width * channels
 
-    state, growth, weight, before, decay_before = pl.pallas_call(
+    state, growth, weight, x_high, x_low, before, decay_before = pl.pallas_call(
         lambda *refs: state_kernel(heads, *refs),
         grid=(blocks,),
         in_specs=[
@@ -418,11 +423,11 @@
             pl.BlockSpec((width, channels + LANES), lambda i: (0, 0)),
             pl.BlockSpec((length, LANES), lambda i: (0, 0)),
             pl.BlockSpec((length, LANES), lambda i: (0, 0)),
-            onward["state"], onward["decay"],
+            onward["main"], onward["main"], onward["state"], onward["decay"],
         ],
         out_shape=[
             jax.ShapeDtypeStruct((width, channels + LANES), F32),
-            terms_shape, terms_shape, states_shape, decays_shape,
+            terms_shape, terms_shape, main_shape, main_shape, states_shape, decays_shape,
         ],
         scratch_shapes=[row_scratch],
         compiler_params=params(),
@@ -438,39 +443,39 @@
     starts, _ = lax.optimization_barrier((starts, second_in[1:]))
     start = seg_exchange(starts).reshape(width, channels)
 
-    grad_state, dyc, later, decay_after = pl.pallas_call(
+    grad_state, dyc, d_high, d_low, later, decay_after = pl.pallas_call(
         lambda *refs: grad_state_kernel(len(second_in), *refs),
         grid=(blocks,),
         in_specs=[back["per_head"], whole(expand)] + [whole(part) for part in second_in],
         out_specs=[
             pl.BlockSpec((width, channels), lambda i: (0, 0)),
             pl.BlockSpec((BLOCK, pair_width), lambda i: (blocks - 1 - i, 0)),
-            back["state"], back["decay"],
+            back["main"], back["main"], back["state"], back["decay"],
         ],
         out_shape=[
             state_shape, jax.ShapeDtypeStruct((length, pair_width), BF16),
-            states_shape, decays_shape,
+            main_shape, main_shape, states_shape, decays_shape,
         ],
         scratch_shapes=[row_scratch],
         compiler_params=params(),
         cost_estimate=cost(6 * unit, 4 * length * channels),
     )(growth, expand, *second_in)
-    inner, grad_inner, inside_b, inside_c, skip_grad = pl.pallas_call(
+    inner, inside_b, inside_c, skip_grad = pl.pallas_call(
         inside_kernel,
         grid=(blocks,),
-        in_specs=[onward[name] for name in ("main", "side", "main", "side", "per_head", "per_head")] + [whole(expand)],
+        in_specs=[onward[name] for name in ("main", "main", "main", "side", "main", "main", "main", "side")],
         out_specs=[
-            onward["main"], onward["main"], onward["mixed"], onward["mixed"],
+            onward["main"], onward["mixed"], onward["mixed"],
             pl.BlockSpec((1, channels), lambda i: (0, 0)),
         ],
         out_shape=[
-            jax.ShapeDtypeStruct((length, channels), F32), jax.ShapeDtypeStruct((length, channels), F32),
+            jax.ShapeDtypeStruct((length, channels), F32),
             jax.ShapeDtypeStruct((length, width), F32), jax.ShapeDtypeStruct((length, width), F32),
             jax.ShapeDtypeStruct((1, channels), F32),
         ],
         compiler_params=params(),
-        cost_estimate=cost(12 * unit, 16 * length * channels),
-    )(xbd, xbd, dyc, dyc, growth, weight, expand)
+        cost_estimate=cost(8 * unit, 16 * length * channels),
+    )(xbd, x_high, x_low, xbd, dyc, d_high, d_low, dyc)
 
     grad_state, _ = lax.optimization_barrier((grad_state, (start, inner)))
     pieces = seg_exchange(grad_state)
@@ -494,18 +499,29 @@
         cost_estimate=cost(unit, 8 * width * channels),
     )(pieces, decays)
     own, other, _ = lax.optimization_barrier((own, other, pieces))
-    first_out = swap_chips(swap_cores(own, other))
+    d_high, _ = lax.optimization_barrier((d_high, pieces))
+    total = lax.dynamic_slice_in_dim(decays, lax.axis_index("seg"), 1, 0)
+    slab = pl.BlockSpec((width // blocks, channels), lambda i: (i, 0))
+    grad_inner, final = pl.pallas_call(
+        inside_grad_kernel,
+        grid=(blocks,),
+        in_specs=[onward[name] for name in ("side", "main", "main", "side")] + [slab, slab, whole(total)],
+        out_specs=[onward["main"], slab],
+        out_shape=[jax.ShapeDtypeStruct((length, channels), F32), state_shape],
+        compiler_params=params(),
+        cost_estimate=cost(4 * unit, 8 * length * channels),
+    )(xbd, d_high, d_low, dyc, state, start, total)
+    first_out = swap_chips(swap_cores(own, other), grad_inner)
     end = seg_exchange(ends).reshape(width, channels)
 
 
-    total = lax.dynamic_slice_in_dim(decays, lax.axis_index("seg"), 1, 0)
     grads, rate_grad = pl.pallas_call(
         backward_kernel,
         grid=(blocks,),
         in_specs=[
             back["main"], back["side"], back["dt"], back["main"], back["per_head"],
             back["main"], back["mixed"], back["state"], back["decay"],
-            whole(end), pl.BlockSpec((width, channels), lambda i: (0, 0)), whole(start), whole(total),
+            whole(end), whole(final),
             back["per_head"], whole(rate_row), whole(skip_row), whole(expand), whole(collect),
         ],
         out_specs=[
@@ -521,7 +537,7 @@
         cost_estimate=cost(8 * unit, 16 * length * channels),
     )(
         xbd, xbd, xbd, dyc, weight, grad_inner, inside_b, later, decay_after,
-        end, state, start, total, dots, rate_row, skip_row, expand, collect,
+        end, final, dots, rate_row, skip_row, expand, collect,
     )
     grads, _ = lax.optimization_barrier((grads, first_out[1:]))
     second_out = exchange(grads.reshape(shards, rows, packed_width))

time: 224 us -> 218 us (0.973)
  waiting for transfers between devices: 83.2 us -> 76.9 us
  Pallas kernels: 66.4 us -> 71 us
  local copies, waits for them, and re-layouts: 18 us -> 15.7 us
    ppermute x6, waiting for transfers between devices: 16.2 us -> 7.69 us  [permute(): lax.ppermute(value, 'head', [(i, (i + 2 * hop) % count) for i in range(co...]
    pallas_call x1 -> x2, Pallas kernels: 2.46 us -> 9.72 us  [the longest x1 6.71 us: on_device(): pl.pallas_call(inside_grad_kernel, grid=(blocks,), in_specs=[onward[name]...]
    pallas_call x1, Pallas kernels: 13.4 us -> 9.49 us  [on_device(): pl.pallas_call(inside_kernel, grid=(blocks,), in_specs=[onward[name] for...]
    unnamed x48 -> x36, local copies, waits for them, and re-layouts: 15.7 us -> 13.3 us
  transfers between devices with their start and end apart: 18 -> 18, of which waited for: 12 -> 11; matrix products, arithmetic and copies ran while one was open for 2% -> 2% of each run, Pallas kernels for 28% -> 30%
where the time goes in v4:
time: 218 us; the launch traced here: 216 us
  waiting for transfers between devices  76.9 us (35%)
  Pallas kernels  71 us (33%)
  starting transfers between devices  50.8 us (23%)
  local copies, waits for them, and re-layouts  15.7 us (7%)
    all_to_all x2, waiting for transfers between devices, exchange(): return lax.all_to_all(value, 'head', 0, 0)  37.4 us
    all_to_all x4, starting transfers between devices, seg_exchange(): lax.all_to_all(state.reshape(count, -1, state.shape[-1]), 'seg', 0, 0)  23.8 us
    all_to_all x4, waiting for transfers between devices, seg_exchange(): lax.all_to_all(state.reshape(count, -1, state.shape[-1]), 'seg', 0, 0)  20.3 us
    unnamed x36, local copies, waits for them, and re-layouts  13.3 us
    pallas_call x1, Pallas kernels, on_device(): pl.pallas_call(backward_kernel, grid=(blocks,), in_specs=[back['main'], b...  12.1 us
    pallas_call x1, Pallas kernels, on_device(): pl.pallas_call(forward_kernel, grid=(blocks,), in_specs=[onward['main'],...  9.66 us
    pallas_call x1, Pallas kernels, on_device(): pl.pallas_call(inside_kernel, grid=(blocks,), in_specs=[onward[name] for...  9.49 us
    all_to_all x2, starting transfers between devices, exchange(): return lax.all_to_all(value, 'head', 0, 0)  9.44 us
  transfers between devices with their start and end apart: 18, of which 11 were waited for; matrix products, arithmetic and copies ran while one was open for 2% of the time, Pallas kernels for 30%

profile of v4, /device:TPU:0, one launch (start us, length us, event | category | flops | bytes accessed | tf_op | source)
XLA Modules:
  0.0 216.5 jit_solution(12047149422159640910)
XLA Ops:
  0.6 3.0 %shard_map.126 = bf16[8,128,1408]{2,1,0:T(8,128)(2,1)} custom-call(bf16[128,8192]{1,0:T(8,128)(2,1)} %refs_0_.1, bf16[128,2048]{1,0:T(8,128)(2,1)} %refs_1_.1, bf16[128,128]{1,0:T(8,128)(2,1)} %refs_2_.1), custom_call_target="tpu_custom_call" | custom-call | flops 128 | bytes 5767168 | tf_op jit(solution)/shard_map/pallas_call | solution.py:349
  3.6 5.5 %all-to-all-start = ((bf16[8,128,1408]{2,1,0:T(8,128)(2,1)}), bf16[8,128,1408]{2,1,0:T(8,128)(2,1)}, u32[]{:S(2)}, u32[]{:S(2)}) async-start(bf16[8,128,1408]{2,1,0:T(8,128)(2,1)} %shard_map.126), calls=%async_computation | async-start | bytes 5767168 | tf_op jit(solution)/shard_map/all_to_all | solution.py:308
  9.2 3.7 %shard_map.127 = (bf16[4,128,1280]{2,1,0:T(8,128)(2,1)S(1)}, bf16[4,128,1280]{2,1,0:T(8,128)(2,1)}) custom-call(bf16[128,8192]{1,0:T(8,128)(2,1)} %dy_ref.1, bf16[128,2048]{1,0:T(8,128)(2,1)S(1)} %copy-done.9), custom_call_target="tpu_custom_call" | custom-call | flops 128 | bytes 5242880 | tf_op jit(solution)/shard_map/pallas_call | solution.py:365
  13.8 2.7 %collective-permute-done.swapped_ref = bf16[4,128,1280]{2,1,0:T(8,128)(2,1)} collective-permute-done((bf16[4,128,1280]{2,1,0:T(8,128)(2,1)}, bf16[4,128,1280]{2,1,0:T(8,128)(2,1)}, u32[]{:S(2)}, u32[]{:S(2)}) %collective-permute-start) | collective-permute-done | bytes 1310752 | tf_op jit(solution)/shard_map/ppermute | solution.py:314
  16.4 2.5 %shard_map.128 = (bf16[256,1280]{1,0:T(8,128)(2,1)S(1)}, bf16[256,1280]{1,0:T(8,128)(2,1)}, bf16[256,1280]{1,0:T(8,128)(2,1)S(1)}, bf16[256,1280]{1,0:T(8,128)(2,1)}) custom-call(bf16[4,128,1280]{2,1,0:T(8,128)(2,1)S(1)} %get-tuple-element.61.own_ref, bf16[4,128,1280]{2,1,0:T(8,128)(2,1)} %collective-permute-done.swapped_ref), custom_call_target="tpu_custom_call" | custom-call | flops 128 | bytes 10485760 | tf_op jit(solution)/shard_map/pallas_call | solution.py:315
  19.8 25.1 %all-to-all-done = bf16[8,128,1408]{2,1,0:T(8,128)(2,1)} async-done(((bf16[8,128,1408]{2,1,0:T(8,128)(2,1)}), bf16[8,128,1408]{2,1,0:T(8,128)(2,1)}, u32[]{:S(2)}, u32[]{:S(2)}) %all-to-all-start) | async-done | bytes 2883616 | tf_op jit(solution)/shard_map/all_to_all | solution.py:308
  45.5 2.7 %collective-permute-start.2 = (bf16[256,1280]{1,0:T(8,128)(2,1)}, bf16[256,1280]{1,0:T(8,128)(2,1)}, u32[]{:S(2)}, u32[]{:S(2)}) collective-permute-start(bf16[256,1280]{1,0:T(8,128)(2,1)} %get-tuple-element.72), channel_id=1, source_target_pairs={{0,6},{1,7},{2,0},{3,1},{4,2},{5,3},{6,4},{7,5},{8,14},{9,15},{10,... | collective-permute-start | bytes 1966088 | tf_op jit(solution)/shard_map/ppermute | solution.py:327
  48.1 7.0 %shard_map.129 = (f32[256,1152]{1,0:T(8,128)}, bf16[1024,128]{1,0:T(8,128)(2,1)S(1)}, bf16[1024,128]{1,0:T(8,128)(2,1)S(1)}, bf16[1024,1024]{1,0:T(8,128)(2,1)S(...) custom-call(bf16[1024,1408]{1,0:T(8,128)(2,1)} %bitcast.refs_0_.refs_1_.refs_2_.x_ref.b_ref.dt_re, ...), custom_call_target="tpu_custom_call" | custom-call | flops 3221225472 | bytes 4194304 | tf_op jit(solution)/shard_map/pallas_call | solution.py:414
  56.5 7.0 %all-to-all-start.1 = ((f32[16,16,1152]{2,1,0:T(8,128)}), f32[16,16,1152]{2,1,0:T(8,128)S(1)}, u32[]{:S(2)}, u32[]{:S(2)}) async-start(f32[16,16,1152]{2,1,0:T(8,128)} %bitcast.1), calls=%async_computation.1 | async-start | bytes 2359296 | tf_op jit(solution)/shard_map/all_to_all | solution.py:296
  64.2 17.6 %all-to-all-done.1.refs_0_ = f32[16,16,1152]{2,1,0:T(8,128)S(1)} async-done(((f32[16,16,1152]{2,1,0:T(8,128)}), f32[16,16,1152]{2,1,0:T(8,128)S(1)}, u32[]{:S(2)}, u32[]{:S(2)}) %all-to-all-start.1) | async-done | bytes 1179680 | tf_op jit(solution)/shard_map/all_to_all | solution.py:296
  83.0 4.8 %all-to-all-start.2 = ((f32[16,16,1024]{2,1,0:T(8,128)}), f32[16,16,1024]{2,1,0:T(8,128)S(1)}, u32[]{:S(2)}, u32[]{:S(2)}) async-start(f32[16,16,1024]{2,1,0:T(8,128)} %get-tuple-element.85), calls=%async_computation.2 | async-start | bytes 2097152 | tf_op jit(solution)/shard_map/all_to_all | solution.py:296
  87.8 6.7 %shard_map.130 = (f32[256,1024]{1,0:T(8,128)}, bf16[1024,1280]{1,0:T(8,128)(2,1)}, bf16[1024,1024]{1,0:T(8,128)(2,1)}, bf16[1024,1024]{1,0:T(8,128)(2,1)}, f32[4...) custom-call(bf16[1024,128]{1,0:T(8,128)(2,1)S(1)} %get-tuple-element.68.refs_0_.growth_ref, ...), custom_call_target="tpu_custom_call" | custom-call | flops 3221225472 | bytes 4194304 | tf_op jit(solution)/shard_map/pallas_call | solution.py:446
  94.6 9.5 %shard_map.131 = (f32[1024,1024]{1,0:T(8,128)}, f32[1024,256]{1,0:T(8,128)S(1)}, f32[1024,256]{1,0:T(8,128)S(1)}, f32[1,1024]{1,0:T(1,128)S(1)}) custom-call(bf16[1024,1408]{1,0:T(8,128)(2,1)} %bitcast.refs_0_.refs_1_.refs_2_.x_ref.b_ref.dt_ref, bf16[1024,1024]{1,0:T(8,128)(2,1)} %copy-done, bf16[1024,1024]{1,0:T(8,128)(2,1)} %get-tuple-element.76.x_low_ref, ...), custom_call_target="tpu_custom_call" | custom-call | flops 4294967296 | bytes 16777216 | tf_op jit(solution)/shard_map/pallas_call | solution.py:463
  106.1 7.3 %all-to-all-start.3 = ((f32[16,16,1024]{2,1,0:T(8,128)}), f32[16,16,1024]{2,1,0:T(8,128)S(1)}, u32[]{:S(2)}, u32[]{:S(2)}) async-start(f32[16,16,1024]{2,1,0:T(8,128)} %bitcast.20), calls=%async_computation.3 | async-start | bytes 2097152 | tf_op jit(solution)/shard_map/all_to_all | solution.py:296
  115.1 9.7 %shard_map.133 = (bf16[4,128,1280]{2,1,0:T(8,128)(2,1)}, bf16[4,128,1280]{2,1,0:T(8,128)(2,1)}, f32[1024,128]{1,0:T(8,128)S(1)}) custom-call(bf16[1024,1408]{1,0:T(8,128)(2,1)} %bitcast.refs_0_.refs_1_.refs_2_.x_ref.b_ref.dt_ref, bf16[1024,1280]{1,0:T(8,128)(2,1)} %get-tuple-element.74.dy_ref.c_ref, bf16[1024,1280]{1,0:T(8,128)(2,1)} %get-tuple-element.74.dy_ref.c_ref, ...), custom_call_target="tpu_custom_call" | custom-call | flops 4294967296 | bytes 16777216 | tf_op jit(solution)/shard_map/pallas_call | solution.py:482
  125.5 2.7 %all-to-all-done.3.pieces_ref = f32[16,16,1024]{2,1,0:T(8,128)S(1)} async-done(((f32[16,16,1024]{2,1,0:T(8,128)}), f32[16,16,1024]{2,1,0:T(8,128)S(1)}, u32[]{:S(2)}, u32[]{:S(2)}) %all-to-all-start.3) | async-done | bytes 1048608 | tf_op jit(solution)/shard_map/all_to_all | solution.py:296
  129.3 4.6 %all-to-all-start.4 = ((f32[16,16,1024]{2,1,0:T(8,128)}), f32[16,16,1024]{2,1,0:T(8,128)S(1)}, u32[]{:S(2)}, u32[]{:S(2)}) async-start(f32[16,16,1024]{2,1,0:T(8,128)} %shard_map.137), calls=%async_computation.4 | async-start | bytes 2097152 | tf_op jit(solution)/shard_map/all_to_all | solution.py:296
  135.2 2.8 %shard_map.134 = (bf16[256,1280]{1,0:T(8,128)(2,1)S(1)}, bf16[256,1280]{1,0:T(8,128)(2,1)}, bf16[256,1280]{1,0:T(8,128)(2,1)}, bf16[256,1280]{1,0:T(8,128)(2,1)}) custom-call(bf16[4,128,1280]{2,1,0:T(8,128)(2,1)S(1)} %copy-done.1, bf16[4,128,1280]{2,1,0:T(8,128)(2,1)} %collective-permute-done.4.swapped_ref), custom_call_target="tpu_custom_call" | custom-call | flops 128 | bytes 10485760 | tf_op jit(solution)/shard_map/pallas_call | solution.py:315
  138.0 3.2 %collective-permute-start.6 = (bf16[256,1280]{1,0:T(8,128)(2,1)}, bf16[256,1280]{1,0:T(8,128)(2,1)}, u32[]{:S(2)}, u32[]{:S(2)}) collective-permute-start(bf16[256,1280]{1,0:T(8,128)(2,1)} %get-tuple-element.95), channel_id=1, source_target_pairs={{0,6},{1,7},{2,0},{3,1},{4,2},{5,3},{6,4},{7,5},{8,14},{9,15},{10,... | collective-permute-start | bytes 1966088 | tf_op jit(solution)/shard_map/ppermute | solution.py:327
  142.0 6.7 %shard_map.135 = (f32[1024,1024]{1,0:T(8,128)}, f32[256,1024]{1,0:T(8,128)S(1)}) custom-call(bf16[1024,1408]{1,0:T(8,128)(2,1)} %bitcast.refs_0_.refs_1_.refs_2_.x_ref.b_ref.dt_ref, bf16[1024,1024]{1,0:T(8,128)(2,1)} %get-tuple-element.96.d_high_ref, bf16[1024,1024]{1,0:T(8,128)(2,1)} %get-tuple-element.78.d_low_ref, ...), custom_call_target="tpu_custom_call" | custom-call | flops 2147483648 | bytes 8388608 | tf_op jit(solution)/shard_map/pallas_call | solution.py:505
  149.6 6.7 %collective-permute-done.5.refs_1_ = bf16[256,1280]{1,0:T(8,128)(2,1)} collective-permute-done((bf16[256,1280]{1,0:T(8,128)(2,1)}, bf16[256,1280]{1,0:T(8,128)(2,1)}, u32[]{:S(2)}, u32[]{:S(2)}) %collective-permute-start.5) | collective-permute-done | bytes 655392 | tf_op jit(solution)/shard_map/ppermute | solution.py:327
  161.1 12.1 %shard_map.138 = (bf16[1024,1408]{1,0:T(8,128)(2,1)}, f32[1,128]{1,0:T(1,128)S(1)}) custom-call(bf16[1024,1408]{1,0:T(8,128)(2,1)} %bitcast.refs_0_.refs_1_.refs_2_.x_ref.b_ref.dt_ref, bf16[1024,1408]{1,0:T(8,128)(2,1)} %bitcast.refs_0_.refs_1_.refs_2_.x_ref.b_ref.dt_ref, bf16[1024,1408]{1,0:T(8,128)(2,1)} %bitcast.refs_0_.refs_1_.refs_2_.x_ref.b_ref.dt_ref, ...), custom_call_target="tpu_custom_call" | custom-call | flops 4294967296 | bytes 16777216 | tf_op jit(solution)/shard_map/pallas_call | solution.py:518
  175.0 3.9 %all-to-all-start.5 = ((bf16[8,128,1408]{2,1,0:T(8,128)(2,1)}), bf16[8,128,1408]{2,1,0:T(8,128)(2,1)S(1)}, u32[]{:S(2)}, u32[]{:S(2)}) async-start(bf16[8,128,1408]{2,1,0:T(8,128)(2,1)} %bitcast.19), calls=%async_computation.5 | async-start | bytes 5767168 | tf_op jit(solution)/shard_map/all_to_all | solution.py:308
  181.6 2.2 %collective-permute-done.8 = f32[1,128]{1,0:T(1,128)S(1)} collective-permute-done((f32[1,128]{1,0:T(1,128)S(1)}, f32[1,128]{1,0:T(1,128)S(1)}, u32[]{:S(2)}, u32[]{:S(2)}) %collective-permute-start.8) | collective-permute-done | bytes 544 | tf_op jit(solution)/shard_map/ppermute | solution.py:302
  183.9 2.8 %collective-permute-start.9 = (f32[1,128]{1,0:T(1,128)S(1)}, f32[1,128]{1,0:T(1,128)S(1)}, u32[]{:S(2)}, u32[]{:S(2)}) collective-permute-start(f32[1,128]{1,0:T(1,128)S(1)} %fusion.5), channel_id=1, source_target_pairs={{0,16},{8,24},{16,0},{24,8},{32,48},{40,56},{48,32},{56,40},{64,80... | collective-permute-start | bytes 1544 | tf_op jit(solution)/shard_map/ppermute | solution.py:302
  186.8 2.2 %collective-permute-done.9 = f32[1,128]{1,0:T(1,128)S(1)} collective-permute-done((f32[1,128]{1,0:T(1,128)S(1)}, f32[1,128]{1,0:T(1,128)S(1)}, u32[]{:S(2)}, u32[]{:S(2)}) %collective-permute-start.9) | collective-permute-done | bytes 544 | tf_op jit(solution)/shard_map/ppermute | solution.py:302
  190.3 2.2 %collective-permute-done.10 = f32[1,128]{1,0:T(1,128)S(1)} collective-permute-done((f32[1,128]{1,0:T(1,128)S(1)}, f32[1,128]{1,0:T(1,128)S(1)}, u32[]{:S(2)}, u32[]{:S(2)}) %collective-permute-start.10) | collective-permute-done | bytes 544 | tf_op jit(solution)/shard_map/ppermute | solution.py:302
  192.6 2.8 %collective-permute-start.11 = (f32[1,128]{1,0:T(1,128)S(1)}, f32[1,128]{1,0:T(1,128)S(1)}, u32[]{:S(2)}, u32[]{:S(2)}) collective-permute-start(f32[1,128]{1,0:T(1,128)S(1)} %add.53), channel_id=1, source_target_pairs={{0,64},{8,72},{16,80},{24,88},{32,96},{40,104},{48,112},{56,120},{... | collective-permute-start | bytes 1544 | tf_op jit(solution)/shard_map/ppermute | solution.py:302
  195.4 2.2 %collective-permute-done.11 = f32[1,128]{1,0:T(1,128)S(1)} collective-permute-done((f32[1,128]{1,0:T(1,128)S(1)}, f32[1,128]{1,0:T(1,128)S(1)}, u32[]{:S(2)}, u32[]{:S(2)}) %collective-permute-start.11) | collective-permute-done | bytes 544 | tf_op jit(solution)/shard_map/ppermute | solution.py:302
  199.3 3.0 %shard_map.136 = (bf16[128,8192]{1,0:T(8,128)(2,1)}, bf16[128,2048]{1,0:T(8,128)(2,1)}) custom-call(bf16[256,1280]{1,0:T(8,128)(2,1)S(1)} %get-tuple-element.92.refs_0_, bf16[256,1280]{1,0:T(8,128)(2,1)} %collective-permute-done.5.refs_1_, bf16[256,1280]{1,0:T(8,128)(2,1)S(1)} %copy-done.8, bf16[256,1280]{1,0:T(8,128)(2,1)} %collective-permute-done.6.refs_3_), custom_call_target="tpu_custom_call" | custom-call | flops 128 | bytes 5242880 | tf_op jit(solution)/shard_map/pallas_call | solution.py:562
  202.2 12.3 %all-to-all-done.5.refs_0_ = bf16[8,128,1408]{2,1,0:T(8,128)(2,1)S(1)} async-done(((bf16[8,128,1408]{2,1,0:T(8,128)(2,1)}), bf16[8,128,1408]{2,1,0:T(8,128)(2,1)S(1)}, u32[]{:S(2)}, u32[]{:S(2)}) %all-to-all-start.5) | async-done | bytes 2883616 | tf_op jit(solution)/shard_map/all_to_all | solution.py:308
  214.5 2.0 shard_map.139
  (78 shorter events, 26.3 us)
Async XLA Ops:
  3.6 5.5 %copy-start.9 = (bf16[128,2048]{1,0:T(8,128)(2,1)S(1)}, bf16[128,2048]{1,0:T(8,128)(2,1)}, u32[]{:S(2)}) copy-start(bf16[128,2048]{1,0:T(8,128)(2,1)} %c_ref.1) | copy-start | bytes 1572868
  3.6 41.3 %all-to-all-start = ((bf16[8,128,1408]{2,1,0:T(8,128)(2,1)}), bf16[8,128,1408]{2,1,0:T(8,128)(2,1)}, u32[]{:S(2)}, u32[]{:S(2)}) async-start(bf16[8,128,1408]{2,1,0:T(8,128)(2,1)} %shard_map.126), calls=%async_computation | async-start | bytes 5767168 | tf_op jit(solution)/shard_map/all_to_all | solution.py:308
  9.2 4.3 %copy-start.16 = (f32[128]{0:T(128)S(1)}, f32[128]{0:T(128)}, u32[]{:S(2)}) copy-start(f32[128]{0:T(128)} %param.11) | copy-start | bytes 1540
  12.9 3.5 %collective-permute-start = (bf16[4,128,1280]{2,1,0:T(8,128)(2,1)}, bf16[4,128,1280]{2,1,0:T(8,128)(2,1)}, u32[]{:S(2)}, u32[]{:S(2)}) collective-permute-start(bf16[4,128,1280]{2,1,0:T(8,128)(2,1)} %get-tuple-element.62), channel_id=1, source_target_pairs={{0,1},{1,0},{2,3},{3,2},{4,5},{5,4},{6,7},{7,6},{8,9},{9,8},{10,11... | collective-permute-start | bytes 3932168 | tf_op jit(solution)/shard_map/ppermute | solution.py:314
  44.9 18.6 %collective-permute-start.1 = (bf16[256,1280]{1,0:T(8,128)(2,1)}, bf16[256,1280]{1,0:T(8,128)(2,1)}, u32[]{:S(2)}, u32[]{:S(2)}) collective-permute-start(bf16[256,1280]{1,0:T(8,128)(2,1)} %get-tuple-element.70), channel_id=1, source_target_pairs={{0,2},{1,3},{2,4},{3,5},{4,6},{5,7},{6,0},{7,1},{8,10},{9,11},{10,... | collective-permute-start | bytes 1966088 | tf_op jit(solution)/shard_map/ppermute | solution.py:327
  45.5 18.1 %collective-permute-start.2 = (bf16[256,1280]{1,0:T(8,128)(2,1)}, bf16[256,1280]{1,0:T(8,128)(2,1)}, u32[]{:S(2)}, u32[]{:S(2)}) collective-permute-start(bf16[256,1280]{1,0:T(8,128)(2,1)} %get-tuple-element.72), channel_id=1, source_target_pairs={{0,6},{1,7},{2,0},{3,1},{4,2},{5,3},{6,4},{7,5},{8,14},{9,15},{10,... | collective-permute-start | bytes 1966088 | tf_op jit(solution)/shard_map/ppermute | solution.py:327
  55.2 1.3 copy-start
  56.5 25.3 %all-to-all-start.1 = ((f32[16,16,1152]{2,1,0:T(8,128)}), f32[16,16,1152]{2,1,0:T(8,128)S(1)}, u32[]{:S(2)}, u32[]{:S(2)}) async-start(f32[16,16,1152]{2,1,0:T(8,128)} %bitcast.1), calls=%async_computation.1 | async-start | bytes 2359296 | tf_op jit(solution)/shard_map/all_to_all | solution.py:296
  63.6 19.5 %collective-permute-start.3 = (bf16[256,1280]{1,0:T(8,128)(2,1)}, bf16[256,1280]{1,0:T(8,128)(2,1)}, u32[]{:S(2)}, u32[]{:S(2)}) collective-permute-start(bf16[256,1280]{1,0:T(8,128)(2,1)} %copy-done.15), channel_id=1, source_target_pairs={{0,4},{1,5},{2,6},{3,7},{4,0},{5,1},{6,2},{7,3},{8,12},{9,13},{10,... | collective-permute-start | bytes 1966088 | tf_op jit(solution)/shard_map/ppermute | solution.py:327
  83.0 45.2 %copy-start.12 = (f32[16,1024]{1,0:T(8,128)}, f32[16,1024]{1,0:T(8,128)S(1)}, u32[]{:S(2)}) copy-start(f32[16,1024]{1,0:T(8,128)S(1)} %get-tuple-element.97.decay_ref) | copy-start | bytes 196612
  83.0 23.1 %all-to-all-start.2 = ((f32[16,16,1024]{2,1,0:T(8,128)}), f32[16,16,1024]{2,1,0:T(8,128)S(1)}, u32[]{:S(2)}, u32[]{:S(2)}) async-start(f32[16,16,1024]{2,1,0:T(8,128)} %get-tuple-element.85), calls=%async_computation.2 | async-start | bytes 2097152 | tf_op jit(solution)/shard_map/all_to_all | solution.py:296
  94.6 9.5 %copy-start.13 = (f32[4,1,1024]{2,1,0:T(1,128)}, f32[4,1,1024]{2,1,0:T(1,128)S(1)}, u32[]{:S(2)}) copy-start(f32[4,1,1024]{2,1,0:T(1,128)S(1)} %get-tuple-element.104.decay_ref) | copy-start | bytes 49156
  104.1 1.0 copy-start.2
  105.1 1.0 copy-start.5
  106.1 7.4 %copy-start.17 = (f32[128]{0:T(128)S(1)}, f32[128]{0:T(128)}, u32[]{:S(2)}) copy-start(f32[128]{0:T(128)} %param.12) | copy-start | bytes 1540
  106.1 22.1 %all-to-all-start.3 = ((f32[16,16,1024]{2,1,0:T(8,128)}), f32[16,16,1024]{2,1,0:T(8,128)S(1)}, u32[]{:S(2)}, u32[]{:S(2)}) async-start(f32[16,16,1024]{2,1,0:T(8,128)} %bitcast.20), calls=%async_computation.3 | async-start | bytes 2097152 | tf_op jit(solution)/shard_map/all_to_all | solution.py:296
  113.9 1.2 copy-start.6
  128.2 5.6 %collective-permute-start.4 = (bf16[4,128,1280]{2,1,0:T(8,128)(2,1)}, bf16[4,128,1280]{2,1,0:T(8,128)(2,1)}, u32[]{:S(2)}, u32[]{:S(2)}) collective-permute-start(bf16[4,128,1280]{2,1,0:T(8,128)(2,1)} %get-tuple-element.91), channel_id=1, source_target_pairs={{0,1},{1,0},{2,3},{3,2},{4,5},{5,4},{6,7},{7,6},{8,9},{9,8},{10,11... | collective-permute-start | bytes 3932168 | tf_op jit(solution)/shard_map/ppermute | solution.py:314
  129.3 28.8 %all-to-all-start.4 = ((f32[16,16,1024]{2,1,0:T(8,128)}), f32[16,16,1024]{2,1,0:T(8,128)S(1)}, u32[]{:S(2)}, u32[]{:S(2)}) async-start(f32[16,16,1024]{2,1,0:T(8,128)} %shard_map.137), calls=%async_computation.4 | async-start | bytes 2097152 | tf_op jit(solution)/shard_map/all_to_all | solution.py:296
  133.8 1.3 copy-start.1
  138.0 18.4 %collective-permute-start.5 = (bf16[256,1280]{1,0:T(8,128)(2,1)}, bf16[256,1280]{1,0:T(8,128)(2,1)}, u32[]{:S(2)}, u32[]{:S(2)}) collective-permute-start(bf16[256,1280]{1,0:T(8,128)(2,1)} %get-tuple-element.93), channel_id=1, source_target_pairs={{0,2},{1,3},{2,4},{3,5},{4,6},{5,7},{6,0},{7,1},{8,10},{9,11},{10,... | collective-permute-start | bytes 1966088 | tf_op jit(solution)/shard_map/ppermute | solution.py:327
  138.0 18.4 %collective-permute-start.6 = (bf16[256,1280]{1,0:T(8,128)(2,1)}, bf16[256,1280]{1,0:T(8,128)(2,1)}, u32[]{:S(2)}, u32[]{:S(2)}) collective-permute-start(bf16[256,1280]{1,0:T(8,128)(2,1)} %get-tuple-element.95), channel_id=1, source_target_pairs={{0,6},{1,7},{2,0},{3,1},{4,2},{5,3},{6,4},{7,5},{8,14},{9,15},{10,... | collective-permute-start | bytes 1966088 | tf_op jit(solution)/shard_map/ppermute | solution.py:327
  148.7 1.0 copy-start.4
  156.4 17.8 %collective-permute-start.7 = (bf16[256,1280]{1,0:T(8,128)(2,1)}, bf16[256,1280]{1,0:T(8,128)(2,1)S(1)}, u32[]{:S(2)}, u32[]{:S(2)}) collective-permute-start(bf16[256,1280]{1,0:T(8,128)(2,1)} %get-tuple-element.99), channel_id=1, source_target_pairs={{0,4},{1,5},{2,6},{3,7},{4,0},{5,1},{6,2},{7,3},{8,12},{9,13},{10,... | collective-permute-start | bytes 1966088 | tf_op jit(solution)/shard_map/ppermute | solution.py:327
  158.1 1.2 copy-start.3
  159.3 1.0 copy-start.11
  175.0 39.5 %all-to-all-start.5 = ((bf16[8,128,1408]{2,1,0:T(8,128)(2,1)}), bf16[8,128,1408]{2,1,0:T(8,128)(2,1)S(1)}, u32[]{:S(2)}, u32[]{:S(2)}) async-start(bf16[8,128,1408]{2,1,0:T(8,128)(2,1)} %bitcast.19), calls=%async_computation.5 | async-start | bytes 5767168 | tf_op jit(solution)/shard_map/all_to_all | solution.py:308
  180.3 3.6 %collective-permute-start.8 = (f32[1,128]{1,0:T(1,128)S(1)}, f32[1,128]{1,0:T(1,128)S(1)}, u32[]{:S(2)}, u32[]{:S(2)}) collective-permute-start(f32[1,128]{1,0:T(1,128)S(1)} %fusion.4), channel_id=1, source_target_pairs={{0,8},{8,0},{16,24},{24,16},{32,40},{40,32},{48,56},{56,48},{64,72... | collective-permute-start | bytes 1544 | tf_op jit(solution)/shard_map/ppermute | solution.py:302
  183.9 5.1 %collective-permute-start.9 = (f32[1,128]{1,0:T(1,128)S(1)}, f32[1,128]{1,0:T(1,128)S(1)}, u32[]{:S(2)}, u32[]{:S(2)}) collective-permute-start(f32[1,128]{1,0:T(1,128)S(1)} %fusion.5), channel_id=1, source_target_pairs={{0,16},{8,24},{16,0},{24,8},{32,48},{40,56},{48,32},{56,40},{64,80... | collective-permute-start | bytes 1544 | tf_op jit(solution)/shard_map/ppermute | solution.py:302
  189.0 3.5 %collective-permute-start.10 = (f32[1,128]{1,0:T(1,128)S(1)}, f32[1,128]{1,0:T(1,128)S(1)}, u32[]{:S(2)}, u32[]{:S(2)}) collective-permute-start(f32[1,128]{1,0:T(1,128)S(1)} %add.52), channel_id=1, source_target_pairs={{0,32},{8,40},{16,48},{24,56},{32,0},{40,8},{48,16},{56,24},{64,96... | collective-permute-start | bytes 1544 | tf_op jit(solution)/shard_map/ppermute | solution.py:302
  192.6 5.0 %collective-permute-start.11 = (f32[1,128]{1,0:T(1,128)S(1)}, f32[1,128]{1,0:T(1,128)S(1)}, u32[]{:S(2)}, u32[]{:S(2)}) collective-permute-start(f32[1,128]{1,0:T(1,128)S(1)} %add.53), channel_id=1, source_target_pairs={{0,64},{8,72},{16,80},{24,88},{32,96},{40,104},{48,112},{56,120},{... | collective-permute-start | bytes 1544 | tf_op jit(solution)/shard_map/ppermute | solution.py:302
  198.2 1.1 copy-start.8
  (4 other events, 3.2 us)

commit v5 on v4

--- a/solution.py
+++ b/solution.py
@@ -473,7 +473,7 @@
             jax.ShapeDtypeStruct((length, width), F32), jax.ShapeDtypeStruct((length, width), F32),
             jax.ShapeDtypeStruct((1, channels), F32),
         ],
-        compiler_params=params(),
+        compiler_params=params(61),
         cost_estimate=cost(8 * unit, 16 * length * channels),
     )(xbd, x_high, x_low, xbd, dyc, d_high, d_low, dyc)
 
@@ -533,7 +533,7 @@
             jax.ShapeDtypeStruct((1, LANES), F32),
         ],
         scratch_shapes=[pltpu.VMEM((8, LANES), F32)],
-        compiler_params=params(),
+        compiler_params=params(61),
         cost_estimate=cost(8 * unit, 16 * length * channels),
     )(
         xbd, xbd, xbd, dyc, weight, grad_inner, inside_b, later, decay_after,

time: 218 us -> 216 us (level)
  local copies, waits for them, and re-layouts: 15.7 us -> 12.4 us
    unnamed x36 -> x48, local copies, waits for them, and re-layouts: 13.3 us -> 10.1 us
    ppermute x6, waiting for transfers between devices: 7.69 us -> 9.95 us  [permute(): lax.ppermute(value, 'head', [(i, (i + 2 * hop) % count) for i in range(co...]
  transfers between devices with their start and end apart: 18 -> 18, of which waited for: 11 -> 11; matrix products, arithmetic and copies ran while one was open for 2% -> 2% of each run, Pallas kernels for 30% -> 31%
where the time goes in v5:
time: 216 us; the launch traced here: 215 us
  waiting for transfers between devices  78.8 us (36%)
  Pallas kernels  71.3 us (33%)
  starting transfers between devices  49.9 us (23%)
  local copies, waits for them, and re-layouts  12.4 us (6%)
    all_to_all x2, waiting for transfers between devices, exchange(): return lax.all_to_all(value, 'head', 0, 0)  36.5 us
    all_to_all x4, starting transfers between devices, seg_exchange(): lax.all_to_all(state.reshape(count, -1, state.shape[-1]), 'seg', 0, 0)  23.9 us
    all_to_all x4, waiting for transfers between devices, seg_exchange(): lax.all_to_all(state.reshape(count, -1, state.shape[-1]), 'seg', 0, 0)  20.7 us
    pallas_call x1, Pallas kernels, on_device(): pl.pallas_call(backward_kernel, grid=(blocks,), in_specs=[back['main'], b...  13.2 us
    unnamed x48, local copies, waits for them, and re-layouts  10.1 us
    pallas_call x1, Pallas kernels, on_device(): pl.pallas_call(inside_kernel, grid=(blocks,), in_specs=[onward[name] for...  10 us
    ppermute x6, waiting for transfers between devices, permute(): lax.ppermute(value, 'head', [(i, (i + 2 * hop) % count) for i in range(co...  9.95 us
    pallas_call x1, Pallas kernels, on_device(): pl.pallas_call(forward_kernel, grid=(blocks,), in_specs=[onward['main'],...  9.65 us
  transfers between devices with their start and end apart: 18, of which 11 were waited for; matrix products, arithmetic and copies ran while one was open for 2% of the time, Pallas kernels for 31%

profile of v5, /device:TPU:0, one launch (start us, length us, event | category | flops | bytes accessed | tf_op | source)
XLA Modules:
  0.0 214.7 jit_solution(11805709414144358249)
XLA Ops:
  0.6 3.0 %shard_map.126 = bf16[8,128,1408]{2,1,0:T(8,128)(2,1)} custom-call(bf16[128,8192]{1,0:T(8,128)(2,1)} %refs_0_.1, bf16[128,2048]{1,0:T(8,128)(2,1)} %refs_1_.1, bf16[128,128]{1,0:T(8,128)(2,1)} %refs_2_.1), custom_call_target="tpu_custom_call" | custom-call | flops 128 | bytes 5767168 | tf_op jit(solution)/shard_map/pallas_call | solution.py:349
  3.6 5.5 %all-to-all-start = ((bf16[8,128,1408]{2,1,0:T(8,128)(2,1)}), bf16[8,128,1408]{2,1,0:T(8,128)(2,1)}, u32[]{:S(2)}, u32[]{:S(2)}) async-start(bf16[8,128,1408]{2,1,0:T(8,128)(2,1)} %shard_map.126), calls=%async_computation | async-start | bytes 5767168 | tf_op jit(solution)/shard_map/all_to_all | solution.py:308
  9.2 3.7 %shard_map.127 = (bf16[4,128,1280]{2,1,0:T(8,128)(2,1)S(1)}, bf16[4,128,1280]{2,1,0:T(8,128)(2,1)}) custom-call(bf16[128,8192]{1,0:T(8,128)(2,1)} %dy_ref.1, bf16[128,2048]{1,0:T(8,128)(2,1)S(1)} %copy-done.12), custom_call_target="tpu_custom_call" | custom-call | flops 128 | bytes 5242880 | tf_op jit(solution)/shard_map/pallas_call | solution.py:365
  13.8 2.6 %collective-permute-done.swapped_ref = bf16[4,128,1280]{2,1,0:T(8,128)(2,1)} collective-permute-done((bf16[4,128,1280]{2,1,0:T(8,128)(2,1)}, bf16[4,128,1280]{2,1,0:T(8,128)(2,1)}, u32[]{:S(2)}, u32[]{:S(2)}) %collective-permute-start) | collective-permute-done | bytes 1310752 | tf_op jit(solution)/shard_map/ppermute | solution.py:314
  16.4 2.5 %shard_map.128 = (bf16[256,1280]{1,0:T(8,128)(2,1)S(1)}, bf16[256,1280]{1,0:T(8,128)(2,1)}, bf16[256,1280]{1,0:T(8,128)(2,1)S(1)}, bf16[256,1280]{1,0:T(8,128)(2,1)}) custom-call(bf16[4,128,1280]{2,1,0:T(8,128)(2,1)S(1)} %get-tuple-element.61.own_ref, bf16[4,128,1280]{2,1,0:T(8,128)(2,1)} %collective-permute-done.swapped_ref), custom_call_target="tpu_custom_call" | custom-call | flops 128 | bytes 10485760 | tf_op jit(solution)/shard_map/pallas_call | solution.py:315
  19.8 25.1 %all-to-all-done = bf16[8,128,1408]{2,1,0:T(8,128)(2,1)} async-done(((bf16[8,128,1408]{2,1,0:T(8,128)(2,1)}), bf16[8,128,1408]{2,1,0:T(8,128)(2,1)}, u32[]{:S(2)}, u32[]{:S(2)}) %all-to-all-start) | async-done | bytes 2883616 | tf_op jit(solution)/shard_map/all_to_all | solution.py:308
  45.5 2.7 %collective-permute-start.2 = (bf16[256,1280]{1,0:T(8,128)(2,1)}, bf16[256,1280]{1,0:T(8,128)(2,1)}, u32[]{:S(2)}, u32[]{:S(2)}) collective-permute-start(bf16[256,1280]{1,0:T(8,128)(2,1)} %get-tuple-element.72), channel_id=1, source_target_pairs={{0,6},{1,7},{2,0},{3,1},{4,2},{5,3},{6,4},{7,5},{8,14},{9,15},{10,... | collective-permute-start | bytes 1966088 | tf_op jit(solution)/shard_map/ppermute | solution.py:327
  48.1 7.0 %shard_map.129 = (f32[256,1152]{1,0:T(8,128)}, bf16[1024,128]{1,0:T(8,128)(2,1)S(1)}, bf16[1024,128]{1,0:T(8,128)(2,1)S(1)}, bf16[1024,1024]{1,0:T(8,128)(2,1)S(...) custom-call(bf16[1024,1408]{1,0:T(8,128)(2,1)} %bitcast.refs_0_.refs_1_.refs_2_.x_ref.b_ref.dt_re, ...), custom_call_target="tpu_custom_call" | custom-call | flops 3221225472 | bytes 4194304 | tf_op jit(solution)/shard_map/pallas_call | solution.py:414
  57.2 7.0 %all-to-all-start.1 = ((f32[16,16,1152]{2,1,0:T(8,128)}), f32[16,16,1152]{2,1,0:T(8,128)S(1)}, u32[]{:S(2)}, u32[]{:S(2)}) async-start(f32[16,16,1152]{2,1,0:T(8,128)} %bitcast.1), calls=%async_computation.1 | async-start | bytes 2359296 | tf_op jit(solution)/shard_map/all_to_all | solution.py:296
  64.4 18.1 %all-to-all-done.1.refs_0_ = f32[16,16,1152]{2,1,0:T(8,128)S(1)} async-done(((f32[16,16,1152]{2,1,0:T(8,128)}), f32[16,16,1152]{2,1,0:T(8,128)S(1)}, u32[]{:S(2)}, u32[]{:S(2)}) %all-to-all-start.1) | async-done | bytes 1179680 | tf_op jit(solution)/shard_map/all_to_all | solution.py:296
  83.8 4.8 %all-to-all-start.2 = ((f32[16,16,1024]{2,1,0:T(8,128)}), f32[16,16,1024]{2,1,0:T(8,128)S(1)}, u32[]{:S(2)}, u32[]{:S(2)}) async-start(f32[16,16,1024]{2,1,0:T(8,128)} %get-tuple-element.85), calls=%async_computation.2 | async-start | bytes 2097152 | tf_op jit(solution)/shard_map/all_to_all | solution.py:296
  88.6 6.7 %shard_map.130 = (f32[256,1024]{1,0:T(8,128)}, bf16[1024,1280]{1,0:T(8,128)(2,1)}, bf16[1024,1024]{1,0:T(8,128)(2,1)}, bf16[1024,1024]{1,0:T(8,128)(2,1)}, f32[4...) custom-call(bf16[1024,128]{1,0:T(8,128)(2,1)S(1)} %get-tuple-element.68.refs_0_.growth_ref, ...), custom_call_target="tpu_custom_call" | custom-call | flops 3221225472 | bytes 4194304 | tf_op jit(solution)/shard_map/pallas_call | solution.py:446
  95.3 10.0 %shard_map.131 = (f32[1024,1024]{1,0:T(8,128)}, f32[1024,256]{1,0:T(8,128)}, f32[1024,256]{1,0:T(8,128)}, f32[1,1024]{1,0:T(1,128)}) custom-call(bf16[1024,1408]{1,0:T(8,128)(2,1)} %bitcast.refs_0_.refs_1_.refs_2_.x_ref.b_ref.dt_ref, bf16[1024,1024]{1,0:T(8,128)(2,1)} %copy-done.2, bf16[1024,1024]{1,0:T(8,128)(2,1)} %get-tuple-element.76.x_low_ref, ...), custom_call_target="tpu_custom_call" | custom-call | flops 4294967296 | bytes 16777216 | tf_op jit(solution)/shard_map/pallas_call | solution.py:463
  105.4 7.2 %all-to-all-start.3 = ((f32[16,16,1024]{2,1,0:T(8,128)}), f32[16,16,1024]{2,1,0:T(8,128)S(1)}, u32[]{:S(2)}, u32[]{:S(2)}) async-start(f32[16,16,1024]{2,1,0:T(8,128)} %bitcast.19), calls=%async_computation.3 | async-start | bytes 2097152 | tf_op jit(solution)/shard_map/all_to_all | solution.py:296
  114.4 9.6 %shard_map.133 = (bf16[4,128,1280]{2,1,0:T(8,128)(2,1)}, bf16[4,128,1280]{2,1,0:T(8,128)(2,1)}, f32[1024,128]{1,0:T(8,128)S(1)}) custom-call(bf16[1024,1408]{1,0:T(8,128)(2,1)} %bitcast.refs_0_.refs_1_.refs_2_.x_ref.b_ref.dt_ref, bf16[1024,1280]{1,0:T(8,128)(2,1)} %get-tuple-element.74.dy_ref.c_ref, bf16[1024,1280]{1,0:T(8,128)(2,1)} %get-tuple-element.74.dy_ref.c_ref, ...), custom_call_target="tpu_custom_call" | custom-call | flops 4294967296 | bytes 16777216 | tf_op jit(solution)/shard_map/pallas_call | solution.py:482
  124.8 2.5 %all-to-all-done.3.pieces_ref = f32[16,16,1024]{2,1,0:T(8,128)S(1)} async-done(((f32[16,16,1024]{2,1,0:T(8,128)}), f32[16,16,1024]{2,1,0:T(8,128)S(1)}, u32[]{:S(2)}, u32[]{:S(2)}) %all-to-all-start.3) | async-done | bytes 1048608 | tf_op jit(solution)/shard_map/all_to_all | solution.py:296
  128.5 4.9 %all-to-all-start.4 = ((f32[16,16,1024]{2,1,0:T(8,128)}), f32[16,16,1024]{2,1,0:T(8,128)}, u32[]{:S(2)}, u32[]{:S(2)}) async-start(f32[16,16,1024]{2,1,0:T(8,128)} %shard_map.137), calls=%async_computation.4 | async-start | bytes 2097152 | tf_op jit(solution)/shard_map/all_to_all | solution.py:296
  133.3 2.8 %shard_map.134 = (bf16[256,1280]{1,0:T(8,128)(2,1)S(1)}, bf16[256,1280]{1,0:T(8,128)(2,1)}, bf16[256,1280]{1,0:T(8,128)(2,1)}, bf16[256,1280]{1,0:T(8,128)(2,1)}) custom-call(bf16[4,128,1280]{2,1,0:T(8,128)(2,1)S(1)} %copy-done.3, bf16[4,128,1280]{2,1,0:T(8,128)(2,1)} %collective-permute-done.4.swapped_ref), custom_call_target="tpu_custom_call" | custom-call | flops 128 | bytes 10485760 | tf_op jit(solution)/shard_map/pallas_call | solution.py:315
  136.1 3.2 %collective-permute-start.6 = (bf16[256,1280]{1,0:T(8,128)(2,1)}, bf16[256,1280]{1,0:T(8,128)(2,1)S(1)}, u32[]{:S(2)}, u32[]{:S(2)}) collective-permute-start(bf16[256,1280]{1,0:T(8,128)(2,1)} %get-tuple-element.95), channel_id=1, source_target_pairs={{0,6},{1,7},{2,0},{3,1},{4,2},{5,3},{6,4},{7,5},{8,14},{9,15},{10,... | collective-permute-start | bytes 1966088 | tf_op jit(solution)/shard_map/ppermute | solution.py:327
  140.1 6.7 %shard_map.135 = (f32[1024,1024]{1,0:T(8,128)}, f32[256,1024]{1,0:T(8,128)S(1)}) custom-call(bf16[1024,1408]{1,0:T(8,128)(2,1)} %bitcast.refs_0_.refs_1_.refs_2_.x_ref.b_ref.dt_ref, bf16[1024,1024]{1,0:T(8,128)(2,1)} %get-tuple-element.96.d_high_ref, bf16[1024,1024]{1,0:T(8,128)(2,1)} %get-tuple-element.78.d_low_ref, ...), custom_call_target="tpu_custom_call" | custom-call | flops 2147483648 | bytes 8388608 | tf_op jit(solution)/shard_map/pallas_call | solution.py:505
  147.8 6.6 %collective-permute-done.5.refs_1_ = bf16[256,1280]{1,0:T(8,128)(2,1)S(1)} collective-permute-done((bf16[256,1280]{1,0:T(8,128)(2,1)}, bf16[256,1280]{1,0:T(8,128)(2,1)S(1)}, u32[]{:S(2)}, u32[]{:S(2)}) %collective-permute-start.5) | collective-permute-done | bytes 655392 | tf_op jit(solution)/shard_map/ppermute | solution.py:327
  155.9 13.2 %shard_map.138 = (bf16[1024,1408]{1,0:T(8,128)(2,1)}, f32[1,128]{1,0:T(1,128)}) custom-call(bf16[1024,1408]{1,0:T(8,128)(2,1)} %bitcast.refs_0_.refs_1_.refs_2_.x_ref.b_ref.dt_ref, bf16[1024,1408]{1,0:T(8,128)(2,1)} %bitcast.refs_0_.refs_1_.refs_2_.x_ref.b_ref.dt_ref, bf16[1024,1408]{1,0:T(8,128)(2,1)} %bitcast.refs_0_.refs_1_.refs_2_.x_ref.b_ref.dt_ref, ...), custom_call_target="tpu_custom_call" | custom-call | flops 4294967296 | bytes 16777216 | tf_op jit(solution)/shard_map/pallas_call | solution.py:518
  169.1 3.3 %collective-permute-done.7.refs_2_ = bf16[256,1280]{1,0:T(8,128)(2,1)S(1)} collective-permute-done((bf16[256,1280]{1,0:T(8,128)(2,1)}, bf16[256,1280]{1,0:T(8,128)(2,1)S(1)}, u32[]{:S(2)}, u32[]{:S(2)}) %collective-permute-start.7) | collective-permute-done | bytes 655392 | tf_op jit(solution)/shard_map/ppermute | solution.py:327
  173.3 3.8 %all-to-all-start.5 = ((bf16[8,128,1408]{2,1,0:T(8,128)(2,1)}), bf16[8,128,1408]{2,1,0:T(8,128)(2,1)S(1)}, u32[]{:S(2)}, u32[]{:S(2)}) async-start(bf16[8,128,1408]{2,1,0:T(8,128)(2,1)} %bitcast.18), calls=%async_computation.5 | async-start | bytes 5767168 | tf_op jit(solution)/shard_map/all_to_all | solution.py:308
  179.8 2.3 %collective-permute-done.8 = f32[1,128]{1,0:T(1,128)S(1)} collective-permute-done((f32[1,128]{1,0:T(1,128)S(1)}, f32[1,128]{1,0:T(1,128)S(1)}, u32[]{:S(2)}, u32[]{:S(2)}) %collective-permute-start.8) | collective-permute-done | bytes 544 | tf_op jit(solution)/shard_map/ppermute | solution.py:302
  182.1 2.8 %collective-permute-start.9 = (f32[1,128]{1,0:T(1,128)S(1)}, f32[1,128]{1,0:T(1,128)S(1)}, u32[]{:S(2)}, u32[]{:S(2)}) collective-permute-start(f32[1,128]{1,0:T(1,128)S(1)} %fusion.5), channel_id=1, source_target_pairs={{0,16},{8,24},{16,0},{24,8},{32,48},{40,56},{48,32},{56,40},{64,80... | collective-permute-start | bytes 1544 | tf_op jit(solution)/shard_map/ppermute | solution.py:302
  184.9 2.3 %collective-permute-done.9 = f32[1,128]{1,0:T(1,128)S(1)} collective-permute-done((f32[1,128]{1,0:T(1,128)S(1)}, f32[1,128]{1,0:T(1,128)S(1)}, u32[]{:S(2)}, u32[]{:S(2)}) %collective-permute-start.9) | collective-permute-done | bytes 544 | tf_op jit(solution)/shard_map/ppermute | solution.py:302
  188.5 2.3 %collective-permute-done.10 = f32[1,128]{1,0:T(1,128)S(1)} collective-permute-done((f32[1,128]{1,0:T(1,128)S(1)}, f32[1,128]{1,0:T(1,128)S(1)}, u32[]{:S(2)}, u32[]{:S(2)}) %collective-permute-start.10) | collective-permute-done | bytes 544 | tf_op jit(solution)/shard_map/ppermute | solution.py:302
  190.7 2.8 %collective-permute-start.11 = (f32[1,128]{1,0:T(1,128)S(1)}, f32[1,128]{1,0:T(1,128)S(1)}, u32[]{:S(2)}, u32[]{:S(2)}) collective-permute-start(f32[1,128]{1,0:T(1,128)S(1)} %add.53), channel_id=1, source_target_pairs={{0,64},{8,72},{16,80},{24,88},{32,96},{40,104},{48,112},{56,120},{... | collective-permute-start | bytes 1544 | tf_op jit(solution)/shard_map/ppermute | solution.py:302
  193.5 2.3 %collective-permute-done.11 = f32[1,128]{1,0:T(1,128)S(1)} collective-permute-done((f32[1,128]{1,0:T(1,128)S(1)}, f32[1,128]{1,0:T(1,128)S(1)}, u32[]{:S(2)}, u32[]{:S(2)}) %collective-permute-start.11) | collective-permute-done | bytes 544 | tf_op jit(solution)/shard_map/ppermute | solution.py:302
  201.3 11.4 %all-to-all-done.5.refs_0_ = bf16[8,128,1408]{2,1,0:T(8,128)(2,1)S(1)} async-done(((bf16[8,128,1408]{2,1,0:T(8,128)(2,1)}), bf16[8,128,1408]{2,1,0:T(8,128)(2,1)S(1)}, u32[]{:S(2)}, u32[]{:S(2)}) %all-to-all-start.5) | async-done | bytes 2883616 | tf_op jit(solution)/shard_map/all_to_all | solution.py:308
  212.7 2.0 shard_map.139
  (90 shorter events, 22.9 us)
Async XLA Ops:
  3.6 5.5 %copy-start.12 = (bf16[128,2048]{1,0:T(8,128)(2,1)S(1)}, bf16[128,2048]{1,0:T(8,128)(2,1)}, u32[]{:S(2)}) copy-start(bf16[128,2048]{1,0:T(8,128)(2,1)} %c_ref.1) | copy-start | bytes 1572868
  3.6 41.3 %all-to-all-start = ((bf16[8,128,1408]{2,1,0:T(8,128)(2,1)}), bf16[8,128,1408]{2,1,0:T(8,128)(2,1)}, u32[]{:S(2)}, u32[]{:S(2)}) async-start(bf16[8,128,1408]{2,1,0:T(8,128)(2,1)} %shard_map.126), calls=%async_computation | async-start | bytes 5767168 | tf_op jit(solution)/shard_map/all_to_all | solution.py:308
  9.2 4.3 %copy-start.21 = (f32[128]{0:T(128)S(1)}, f32[128]{0:T(128)}, u32[]{:S(2)}) copy-start(f32[128]{0:T(128)} %param.11) | copy-start | bytes 1540
  12.9 3.5 %collective-permute-start = (bf16[4,128,1280]{2,1,0:T(8,128)(2,1)}, bf16[4,128,1280]{2,1,0:T(8,128)(2,1)}, u32[]{:S(2)}, u32[]{:S(2)}) collective-permute-start(bf16[4,128,1280]{2,1,0:T(8,128)(2,1)} %get-tuple-element.62), channel_id=1, source_target_pairs={{0,1},{1,0},{2,3},{3,2},{4,5},{5,4},{6,7},{7,6},{8,9},{9,8},{10,11... | collective-permute-start | bytes 3932168 | tf_op jit(solution)/shard_map/ppermute | solution.py:314
  13.6 41.6 %copy-start.18 = (f32[1,128]{1,0:T(1,128)}, f32[1,128]{1,0:T(1,128)S(1)}, u32[]{:S(2)}) copy-start(f32[1,128]{1,0:T(1,128)S(1)} %broadcast_in_dim_tile.3.refs_3_.rate_ref) | copy-start | bytes 1540
  13.8 99.3 %copy-start = (bf16[128,1024]{1,0:T(8,128)(2,1)}, bf16[128,1024]{1,0:T(8,128)(2,1)S(1)}, u32[]{:S(2)}) copy-start(bf16[128,1024]{1,0:T(8,128)(2,1)S(1)} %and_convert_fusion.refs_4_.refs_1_.expand_ref) | copy-start | bytes 786436
  44.9 19.4 %collective-permute-start.1 = (bf16[256,1280]{1,0:T(8,128)(2,1)}, bf16[256,1280]{1,0:T(8,128)(2,1)}, u32[]{:S(2)}, u32[]{:S(2)}) collective-permute-start(bf16[256,1280]{1,0:T(8,128)(2,1)} %get-tuple-element.70), channel_id=1, source_target_pairs={{0,2},{1,3},{2,4},{3,5},{4,6},{5,7},{6,0},{7,1},{8,10},{9,11},{10,... | collective-permute-start | bytes 1966088 | tf_op jit(solution)/shard_map/ppermute | solution.py:327
  45.5 18.8 %collective-permute-start.2 = (bf16[256,1280]{1,0:T(8,128)(2,1)}, bf16[256,1280]{1,0:T(8,128)(2,1)}, u32[]{:S(2)}, u32[]{:S(2)}) collective-permute-start(bf16[256,1280]{1,0:T(8,128)(2,1)} %get-tuple-element.72), channel_id=1, source_target_pairs={{0,6},{1,7},{2,0},{3,1},{4,2},{5,3},{6,4},{7,5},{8,14},{9,15},{10,... | collective-permute-start | bytes 1966088 | tf_op jit(solution)/shard_map/ppermute | solution.py:327
  57.2 25.3 %all-to-all-start.1 = ((f32[16,16,1152]{2,1,0:T(8,128)}), f32[16,16,1152]{2,1,0:T(8,128)S(1)}, u32[]{:S(2)}, u32[]{:S(2)}) async-start(f32[16,16,1152]{2,1,0:T(8,128)} %bitcast.1), calls=%async_computation.1 | async-start | bytes 2359296 | tf_op jit(solution)/shard_map/all_to_all | solution.py:296
  64.3 19.5 %collective-permute-start.3 = (bf16[256,1280]{1,0:T(8,128)(2,1)}, bf16[256,1280]{1,0:T(8,128)(2,1)}, u32[]{:S(2)}, u32[]{:S(2)}) collective-permute-start(bf16[256,1280]{1,0:T(8,128)(2,1)} %copy-done.19), channel_id=1, source_target_pairs={{0,4},{1,5},{2,6},{3,7},{4,0},{5,1},{6,2},{7,3},{8,12},{9,13},{10,... | collective-permute-start | bytes 1966088 | tf_op jit(solution)/shard_map/ppermute | solution.py:327
  83.7 43.7 %copy-start.15 = (f32[16,1024]{1,0:T(8,128)}, f32[16,1024]{1,0:T(8,128)S(1)}, u32[]{:S(2)}) copy-start(f32[16,1024]{1,0:T(8,128)S(1)} %get-tuple-element.97.decay_ref) | copy-start | bytes 196612
  83.8 21.6 %all-to-all-start.2 = ((f32[16,16,1024]{2,1,0:T(8,128)}), f32[16,16,1024]{2,1,0:T(8,128)S(1)}, u32[]{:S(2)}, u32[]{:S(2)}) async-start(f32[16,16,1024]{2,1,0:T(8,128)} %get-tuple-element.85), calls=%async_computation.2 | async-start | bytes 2097152 | tf_op jit(solution)/shard_map/all_to_all | solution.py:296
  95.3 10.0 %copy-start.17 = (f32[4,1,1024]{2,1,0:T(1,128)}, f32[4,1,1024]{2,1,0:T(1,128)S(1)}, u32[]{:S(2)}) copy-start(f32[4,1,1024]{2,1,0:T(1,128)S(1)} %get-tuple-element.104.decay_ref) | copy-start | bytes 49156
  105.4 7.2 %copy-start.22 = (f32[128]{0:T(128)S(1)}, f32[128]{0:T(128)}, u32[]{:S(2)}) copy-start(f32[128]{0:T(128)} %param.12) | copy-start | bytes 1540
  105.4 22.0 %all-to-all-start.3 = ((f32[16,16,1024]{2,1,0:T(8,128)}), f32[16,16,1024]{2,1,0:T(8,128)S(1)}, u32[]{:S(2)}, u32[]{:S(2)}) async-start(f32[16,16,1024]{2,1,0:T(8,128)} %bitcast.19), calls=%async_computation.3 | async-start | bytes 2097152 | tf_op jit(solution)/shard_map/all_to_all | solution.py:296
  112.8 11.2 %copy-start.16 = (f32[1,1024]{1,0:T(1,128)}, f32[1,1024]{1,0:T(1,128)S(1)}, u32[]{:S(2)}) copy-start(f32[1,1024]{1,0:T(1,128)S(1)} %broadcast_in_dim_reshape.3.skip_ref) | copy-start | bytes 12292
  113.1 11.0 %copy-start.1 = (bf16[1024,128]{1,0:T(8,128)(2,1)}, bf16[1024,128]{1,0:T(8,128)(2,1)S(1)}, u32[]{:S(2)}) copy-start(bf16[1024,128]{1,0:T(8,128)(2,1)S(1)} %compare_convert_fusion.collect_ref) | copy-start | bytes 786436
  127.4 5.9 %collective-permute-start.4 = (bf16[4,128,1280]{2,1,0:T(8,128)(2,1)}, bf16[4,128,1280]{2,1,0:T(8,128)(2,1)}, u32[]{:S(2)}, u32[]{:S(2)}) collective-permute-start(bf16[4,128,1280]{2,1,0:T(8,128)(2,1)} %get-tuple-element.91), channel_id=1, source_target_pairs={{0,1},{1,0},{2,3},{3,2},{4,5},{5,4},{6,7},{7,6},{8,9},{9,8},{10,11... | collective-permute-start | bytes 3932168 | tf_op jit(solution)/shard_map/ppermute | solution.py:314
  128.5 4.9 %copy-start.3 = (bf16[4,128,1280]{2,1,0:T(8,128)(2,1)S(1)}, bf16[4,128,1280]{2,1,0:T(8,128)(2,1)}, u32[]{:S(2)}) copy-start(bf16[4,128,1280]{2,1,0:T(8,128)(2,1)} %get-tuple-element.90.own_ref) | copy-start | bytes 3932164
  128.5 27.4 %all-to-all-start.4 = ((f32[16,16,1024]{2,1,0:T(8,128)}), f32[16,16,1024]{2,1,0:T(8,128)}, u32[]{:S(2)}, u32[]{:S(2)}) async-start(f32[16,16,1024]{2,1,0:T(8,128)} %shard_map.137), calls=%async_computation.4 | async-start | bytes 2097152 | tf_op jit(solution)/shard_map/all_to_all | solution.py:296
  136.1 18.3 %collective-permute-start.5 = (bf16[256,1280]{1,0:T(8,128)(2,1)}, bf16[256,1280]{1,0:T(8,128)(2,1)S(1)}, u32[]{:S(2)}, u32[]{:S(2)}) collective-permute-start(bf16[256,1280]{1,0:T(8,128)(2,1)} %get-tuple-element.93), channel_id=1, source_target_pairs={{0,2},{1,3},{2,4},{3,5},{4,6},{5,7},{6,0},{7,1},{8,10},{9,11},{10,... | collective-permute-start | bytes 1966088 | tf_op jit(solution)/shard_map/ppermute | solution.py:327
  136.1 18.3 %collective-permute-start.6 = (bf16[256,1280]{1,0:T(8,128)(2,1)}, bf16[256,1280]{1,0:T(8,128)(2,1)S(1)}, u32[]{:S(2)}, u32[]{:S(2)}) collective-permute-start(bf16[256,1280]{1,0:T(8,128)(2,1)} %get-tuple-element.95), channel_id=1, source_target_pairs={{0,6},{1,7},{2,0},{3,1},{4,2},{5,3},{6,4},{7,5},{8,14},{9,15},{10,... | collective-permute-start | bytes 1966088 | tf_op jit(solution)/shard_map/ppermute | solution.py:327
  154.4 14.7 %copy-start.6 = (bf16[256,1280]{1,0:T(8,128)(2,1)}, bf16[256,1280]{1,0:T(8,128)(2,1)S(1)}, u32[]{:S(2)}) copy-start(bf16[256,1280]{1,0:T(8,128)(2,1)S(1)} %collective-permute-done.5.refs_1_) | copy-start | bytes 1966084
  154.4 14.7 %copy-start.8 = (bf16[256,1280]{1,0:T(8,128)(2,1)}, bf16[256,1280]{1,0:T(8,128)(2,1)S(1)}, u32[]{:S(2)}) copy-start(bf16[256,1280]{1,0:T(8,128)(2,1)S(1)} %collective-permute-done.6.refs_3_) | copy-start | bytes 1966084
  154.4 18.0 %collective-permute-start.7 = (bf16[256,1280]{1,0:T(8,128)(2,1)}, bf16[256,1280]{1,0:T(8,128)(2,1)S(1)}, u32[]{:S(2)}, u32[]{:S(2)}) collective-permute-start(bf16[256,1280]{1,0:T(8,128)(2,1)} %get-tuple-element.99), channel_id=1, source_target_pairs={{0,4},{1,5},{2,6},{3,7},{4,0},{5,1},{6,2},{7,3},{8,12},{9,13},{10,... | collective-permute-start | bytes 1966088 | tf_op jit(solution)/shard_map/ppermute | solution.py:327
  173.2 4.3 %copy-start.20 = (f32[1,1024]{1,0:T(1,128)S(1)}, f32[1,1024]{1,0:T(1,128)}, u32[]{:S(2)}) copy-start(f32[1,1024]{1,0:T(1,128)} %get-tuple-element.114) | copy-start | bytes 12292
  173.3 5.2 %copy-start.23 = (f32[1,128]{1,0:T(1,128)S(1)}, f32[1,128]{1,0:T(1,128)}, u32[]{:S(2)}) copy-start(f32[1,128]{1,0:T(1,128)} %get-tuple-element.113) | copy-start | bytes 1540
  173.3 39.4 %all-to-all-start.5 = ((bf16[8,128,1408]{2,1,0:T(8,128)(2,1)}), bf16[8,128,1408]{2,1,0:T(8,128)(2,1)S(1)}, u32[]{:S(2)}, u32[]{:S(2)}) async-start(bf16[8,128,1408]{2,1,0:T(8,128)(2,1)} %bitcast.18), calls=%async_computation.5 | async-start | bytes 5767168 | tf_op jit(solution)/shard_map/all_to_all | solution.py:308
  178.5 3.6 %collective-permute-start.8 = (f32[1,128]{1,0:T(1,128)S(1)}, f32[1,128]{1,0:T(1,128)S(1)}, u32[]{:S(2)}, u32[]{:S(2)}) collective-permute-start(f32[1,128]{1,0:T(1,128)S(1)} %fusion.4), channel_id=1, source_target_pairs={{0,8},{8,0},{16,24},{24,16},{32,40},{40,32},{48,56},{56,48},{64,72... | collective-permute-start | bytes 1544 | tf_op jit(solution)/shard_map/ppermute | solution.py:302
  182.1 5.1 %collective-permute-start.9 = (f32[1,128]{1,0:T(1,128)S(1)}, f32[1,128]{1,0:T(1,128)S(1)}, u32[]{:S(2)}, u32[]{:S(2)}) collective-permute-start(f32[1,128]{1,0:T(1,128)S(1)} %fusion.5), channel_id=1, source_target_pairs={{0,16},{8,24},{16,0},{24,8},{32,48},{40,56},{48,32},{56,40},{64,80... | collective-permute-start | bytes 1544 | tf_op jit(solution)/shard_map/ppermute | solution.py:302
  187.2 3.5 %collective-permute-start.10 = (f32[1,128]{1,0:T(1,128)S(1)}, f32[1,128]{1,0:T(1,128)S(1)}, u32[]{:S(2)}, u32[]{:S(2)}) collective-permute-start(f32[1,128]{1,0:T(1,128)S(1)} %add.52), channel_id=1, source_target_pairs={{0,32},{8,40},{16,48},{24,56},{32,0},{40,8},{48,16},{56,24},{64,96... | collective-permute-start | bytes 1544 | tf_op jit(solution)/shard_map/ppermute | solution.py:302
  190.7 5.0 %collective-permute-start.11 = (f32[1,128]{1,0:T(1,128)S(1)}, f32[1,128]{1,0:T(1,128)S(1)}, u32[]{:S(2)}, u32[]{:S(2)}) collective-permute-start(f32[1,128]{1,0:T(1,128)S(1)} %add.53), channel_id=1, source_target_pairs={{0,64},{8,72},{16,80},{24,88},{32,96},{40,104},{48,112},{56,120},{... | collective-permute-start | bytes 1544 | tf_op jit(solution)/shard_map/ppermute | solution.py:302
  (10 other events, 10.0 us)

commit v6 on v5

--- a/solution.py
+++ b/solution.py
@@ -430,7 +430,7 @@
             terms_shape, terms_shape, main_shape, main_shape, states_shape, decays_shape,
         ],
         scratch_shapes=[row_scratch],
-        compiler_params=params(),
+        compiler_params=params(61),
         cost_estimate=cost(6 * unit, 4 * length * channels),
     )(xbd, xbd, xbd, rate_row, expand)
     piece = (segments, width // segments, channels)

time: 216 us -> 217 us (level)
  starting transfers between devices: 49.9 us -> 52.2 us
    all_to_all x2, waiting for transfers between devices: 36.5 us -> 38.7 us  [exchange(): return lax.all_to_all(value, 'head', 0, 0)]
    unnamed x48 -> x42, local copies, waits for them, and re-layouts: 10.1 us -> 8.15 us
where the time goes in v6:
time: 217 us; the launch traced here: 215 us
  waiting for transfers between devices  77.8 us (36%)
  Pallas kernels  70.9 us (33%)
  starting transfers between devices  52.2 us (24%)
  local copies, waits for them, and re-layouts  11 us (5%)
    all_to_all x2, waiting for transfers between devices, exchange(): return lax.all_to_all(value, 'head', 0, 0)  38.7 us
    all_to_all x4, starting transfers between devices, seg_exchange(): lax.all_to_all(state.reshape(count, -1, state.shape[-1]), 'seg', 0, 0)  24.1 us
    all_to_all x4, waiting for transfers between devices, seg_exchange(): lax.all_to_all(state.reshape(count, -1, state.shape[-1]), 'seg', 0, 0)  19.6 us
    pallas_call x1, Pallas kernels, on_device(): pl.pallas_call(backward_kernel, grid=(blocks,), in_specs=[back['main'], b...  13.2 us
    pallas_call x1, Pallas kernels, on_device(): pl.pallas_call(inside_kernel, grid=(blocks,), in_specs=[onward[name] for...  10 us
    ppermute x6, starting transfers between devices, permute(): lax.ppermute(value, 'head', [(i, (i + 2 * hop) % count) for i in range(co...  9.86 us
    pallas_call x1, Pallas kernels, on_device(): pl.pallas_call(forward_kernel, grid=(blocks,), in_specs=[onward['main'],...  9.64 us
    all_to_all x2, starting transfers between devices, exchange(): return lax.all_to_all(value, 'head', 0, 0)  9.57 us
  transfers between devices with their start and end apart: 18, of which 11 were waited for; matrix products, arithmetic and copies ran while one was open for 2% of the time, Pallas kernels for 31%

profile of v6, /device:TPU:0, one launch (start us, length us, event | category | flops | bytes accessed | tf_op | source)
XLA Modules:
  0.0 214.9 jit_solution(6188457453035412239)
XLA Ops:
  0.6 3.0 %shard_map.126 = bf16[8,128,1408]{2,1,0:T(8,128)(2,1)} custom-call(bf16[128,8192]{1,0:T(8,128)(2,1)} %refs_0_.1, bf16[128,2048]{1,0:T(8,128)(2,1)} %refs_1_.1, bf16[128,128]{1,0:T(8,128)(2,1)} %refs_2_.1), custom_call_target="tpu_custom_call" | custom-call | flops 128 | bytes 5767168 | tf_op jit(solution)/shard_map/pallas_call | solution.py:349
  3.6 5.5 %all-to-all-start = ((bf16[8,128,1408]{2,1,0:T(8,128)(2,1)}), bf16[8,128,1408]{2,1,0:T(8,128)(2,1)}, u32[]{:S(2)}, u32[]{:S(2)}) async-start(bf16[8,128,1408]{2,1,0:T(8,128)(2,1)} %shard_map.126), calls=%async_computation | async-start | bytes 5767168 | tf_op jit(solution)/shard_map/all_to_all | solution.py:308
  9.2 2.5 %shard_map.127 = (bf16[4,128,1280]{2,1,0:T(8,128)(2,1)S(1)}, bf16[4,128,1280]{2,1,0:T(8,128)(2,1)S(1)}) custom-call(bf16[128,8192]{1,0:T(8,128)(2,1)} %dy_ref.1, bf16[128,2048]{1,0:T(8,128)(2,1)S(1)} %copy-done.9), custom_call_target="tpu_custom_call" | custom-call | flops 128 | bytes 5242880 | tf_op jit(solution)/shard_map/pallas_call | solution.py:365
  15.1 2.5 %shard_map.128 = (bf16[256,1280]{1,0:T(8,128)(2,1)S(1)}, bf16[256,1280]{1,0:T(8,128)(2,1)}, bf16[256,1280]{1,0:T(8,128)(2,1)S(1)}, bf16[256,1280]{1,0:T(8,128)(2,1)}) custom-call(bf16[4,128,1280]{2,1,0:T(8,128)(2,1)S(1)} %get-tuple-element.61.own_ref, bf16[4,128,1280]{2,1,0:T(8,128)(2,1)} %collective-permute-done.swapped_ref), custom_call_target="tpu_custom_call" | custom-call | flops 128 | bytes 10485760 | tf_op jit(solution)/shard_map/pallas_call | solution.py:315
  18.4 26.5 %all-to-all-done = bf16[8,128,1408]{2,1,0:T(8,128)(2,1)} async-done(((bf16[8,128,1408]{2,1,0:T(8,128)(2,1)}), bf16[8,128,1408]{2,1,0:T(8,128)(2,1)}, u32[]{:S(2)}, u32[]{:S(2)}) %all-to-all-start) | async-done | bytes 2883616 | tf_op jit(solution)/shard_map/all_to_all | solution.py:308
  45.5 2.7 %collective-permute-start.2 = (bf16[256,1280]{1,0:T(8,128)(2,1)}, bf16[256,1280]{1,0:T(8,128)(2,1)}, u32[]{:S(2)}, u32[]{:S(2)}) collective-permute-start(bf16[256,1280]{1,0:T(8,128)(2,1)} %get-tuple-element.72), channel_id=1, source_target_pairs={{0,6},{1,7},{2,0},{3,1},{4,2},{5,3},{6,4},{7,5},{8,14},{9,15},{10,... | collective-permute-start | bytes 1966088 | tf_op jit(solution)/shard_map/ppermute | solution.py:327
  48.1 7.6 %shard_map.129 = (f32[256,1152]{1,0:T(8,128)}, bf16[1024,128]{1,0:T(8,128)(2,1)}, bf16[1024,128]{1,0:T(8,128)(2,1)}, bf16[1024,1024]{1,0:T(8,128)(2,1)}, bf16[10...) custom-call(bf16[1024,1408]{1,0:T(8,128)(2,1)} %bitcast.refs_0_.refs_1_.refs_2_.x_ref.b_ref.dt_ref, ...), custom_call_target="tpu_custom_call" | custom-call | flops 3221225472 | bytes 4194304 | tf_op jit(solution)/shard_map/pallas_call | solution.py:414
  55.8 7.2 %all-to-all-start.1 = ((f32[16,16,1152]{2,1,0:T(8,128)}), f32[16,16,1152]{2,1,0:T(8,128)S(1)}, u32[]{:S(2)}, u32[]{:S(2)}) async-start(f32[16,16,1152]{2,1,0:T(8,128)} %bitcast.18), calls=%async_computation.1 | async-start | bytes 2359296 | tf_op jit(solution)/shard_map/all_to_all | solution.py:296
  64.2 17.1 %all-to-all-done.1.refs_0_ = f32[16,16,1152]{2,1,0:T(8,128)S(1)} async-done(((f32[16,16,1152]{2,1,0:T(8,128)}), f32[16,16,1152]{2,1,0:T(8,128)S(1)}, u32[]{:S(2)}, u32[]{:S(2)}) %all-to-all-start.1) | async-done | bytes 1179680 | tf_op jit(solution)/shard_map/all_to_all | solution.py:296
  82.5 4.8 %all-to-all-start.2 = ((f32[16,16,1024]{2,1,0:T(8,128)}), f32[16,16,1024]{2,1,0:T(8,128)S(1)}, u32[]{:S(2)}, u32[]{:S(2)}) async-start(f32[16,16,1024]{2,1,0:T(8,128)} %get-tuple-element.85), calls=%async_computation.2 | async-start | bytes 2097152 | tf_op jit(solution)/shard_map/all_to_all | solution.py:296
  87.3 6.8 %shard_map.130 = (f32[256,1024]{1,0:T(8,128)}, bf16[1024,1280]{1,0:T(8,128)(2,1)}, bf16[1024,1024]{1,0:T(8,128)(2,1)}, bf16[1024,1024]{1,0:T(8,128)(2,1)}, f32[4...) custom-call(bf16[1024,128]{1,0:T(8,128)(2,1)S(1)} %copy-done.11, bf16[128,1024]{1,0:T(8,128)(2,1)S(1)} %copy-done.2, ...), custom_call_target="tpu_custom_call" | custom-call | flops 3221225472 | bytes 4194304 | tf_op jit(solution)/shard_map/pallas_call | solution.py:446
  94.1 10.0 %shard_map.131 = (f32[1024,1024]{1,0:T(8,128)}, f32[1024,256]{1,0:T(8,128)}, f32[1024,256]{1,0:T(8,128)}, f32[1,1024]{1,0:T(1,128)}) custom-call(bf16[1024,1408]{1,0:T(8,128)(2,1)} %bitcast.refs_0_.refs_1_.refs_2_.x_ref.b_ref.dt_ref, bf16[1024,1024]{1,0:T(8,128)(2,1)} %get-tuple-element.75.x_high_ref, bf16[1024,1024]{1,0:T(8,128)(2,1)} %get-tuple-element.76.x_low_ref, ...), custom_call_target="tpu_custom_call" | custom-call | flops 4294967296 | bytes 16777216 | tf_op jit(solution)/shard_map/pallas_call | solution.py:463
  104.2 7.2 %all-to-all-start.3 = ((f32[16,16,1024]{2,1,0:T(8,128)}), f32[16,16,1024]{2,1,0:T(8,128)S(1)}, u32[]{:S(2)}, u32[]{:S(2)}) async-start(f32[16,16,1024]{2,1,0:T(8,128)} %bitcast.20), calls=%async_computation.3 | async-start | bytes 2097152 | tf_op jit(solution)/shard_map/all_to_all | solution.py:296
  113.2 9.6 %shard_map.133 = (bf16[4,128,1280]{2,1,0:T(8,128)(2,1)}, bf16[4,128,1280]{2,1,0:T(8,128)(2,1)}, f32[1024,128]{1,0:T(8,128)S(1)}) custom-call(bf16[1024,1408]{1,0:T(8,128)(2,1)} %bitcast.refs_0_.refs_1_.refs_2_.x_ref.b_ref.dt_ref, bf16[1024,1280]{1,0:T(8,128)(2,1)} %get-tuple-element.74.dy_ref.c_ref, bf16[1024,1280]{1,0:T(8,128)(2,1)} %get-tuple-element.74.dy_ref.c_ref, ...), custom_call_target="tpu_custom_call" | custom-call | flops 4294967296 | bytes 16777216 | tf_op jit(solution)/shard_map/pallas_call | solution.py:482
  123.6 2.5 %all-to-all-done.3.pieces_ref = f32[16,16,1024]{2,1,0:T(8,128)S(1)} async-done(((f32[16,16,1024]{2,1,0:T(8,128)}), f32[16,16,1024]{2,1,0:T(8,128)S(1)}, u32[]{:S(2)}, u32[]{:S(2)}) %all-to-all-start.3) | async-done | bytes 1048608 | tf_op jit(solution)/shard_map/all_to_all | solution.py:296
  127.3 4.9 %all-to-all-start.4 = ((f32[16,16,1024]{2,1,0:T(8,128)}), f32[16,16,1024]{2,1,0:T(8,128)}, u32[]{:S(2)}, u32[]{:S(2)}) async-start(f32[16,16,1024]{2,1,0:T(8,128)} %copy-done.1), calls=%async_computation.4 | async-start | bytes 2097152 | tf_op jit(solution)/shard_map/all_to_all | solution.py:296
  133.5 2.8 %shard_map.134 = (bf16[256,1280]{1,0:T(8,128)(2,1)S(1)}, bf16[256,1280]{1,0:T(8,128)(2,1)}, bf16[256,1280]{1,0:T(8,128)(2,1)}, bf16[256,1280]{1,0:T(8,128)(2,1)}) custom-call(bf16[4,128,1280]{2,1,0:T(8,128)(2,1)S(1)} %copy-done.4, bf16[4,128,1280]{2,1,0:T(8,128)(2,1)} %collective-permute-done.4.swapped_ref), custom_call_target="tpu_custom_call" | custom-call | flops 128 | bytes 10485760 | tf_op jit(solution)/shard_map/pallas_call | solution.py:315
  136.2 3.2 %collective-permute-start.6 = (bf16[256,1280]{1,0:T(8,128)(2,1)}, bf16[256,1280]{1,0:T(8,128)(2,1)}, u32[]{:S(2)}, u32[]{:S(2)}) collective-permute-start(bf16[256,1280]{1,0:T(8,128)(2,1)} %get-tuple-element.95), channel_id=1, source_target_pairs={{0,6},{1,7},{2,0},{3,1},{4,2},{5,3},{6,4},{7,5},{8,14},{9,15},{10,... | collective-permute-start | bytes 1966088 | tf_op jit(solution)/shard_map/ppermute | solution.py:327
  140.2 6.5 %shard_map.135 = (f32[1024,1024]{1,0:T(8,128)}, f32[256,1024]{1,0:T(8,128)S(1)}) custom-call(bf16[1024,1408]{1,0:T(8,128)(2,1)} %bitcast.refs_0_.refs_1_.refs_2_.x_ref.b_ref.dt_ref, bf16[1024,1024]{1,0:T(8,128)(2,1)} %get-tuple-element.96.d_high_ref, bf16[1024,1024]{1,0:T(8,128)(2,1)} %get-tuple-element.78.d_low_ref, ...), custom_call_target="tpu_custom_call" | custom-call | flops 2147483648 | bytes 8388608 | tf_op jit(solution)/shard_map/pallas_call | solution.py:505
  147.7 6.9 %collective-permute-done.5.refs_1_ = bf16[256,1280]{1,0:T(8,128)(2,1)} collective-permute-done((bf16[256,1280]{1,0:T(8,128)(2,1)}, bf16[256,1280]{1,0:T(8,128)(2,1)}, u32[]{:S(2)}, u32[]{:S(2)}) %collective-permute-start.5) | collective-permute-done | bytes 655392 | tf_op jit(solution)/shard_map/ppermute | solution.py:327
  154.6 2.2 %collective-permute-start.7 = (bf16[256,1280]{1,0:T(8,128)(2,1)}, bf16[256,1280]{1,0:T(8,128)(2,1)S(1)}, u32[]{:S(2)}, u32[]{:S(2)}) collective-permute-start(bf16[256,1280]{1,0:T(8,128)(2,1)} %get-tuple-element.99), channel_id=1, source_target_pairs={{0,4},{1,5},{2,6},{3,7},{4,0},{5,1},{6,2},{7,3},{8,12},{9,13},{10,... | collective-permute-start | bytes 1966088 | tf_op jit(solution)/shard_map/ppermute | solution.py:327
  156.9 13.2 %shard_map.138 = (bf16[1024,1408]{1,0:T(8,128)(2,1)}, f32[1,128]{1,0:T(1,128)}) custom-call(bf16[1024,1408]{1,0:T(8,128)(2,1)} %bitcast.refs_0_.refs_1_.refs_2_.x_ref.b_ref.dt_ref, bf16[1024,1408]{1,0:T(8,128)(2,1)} %bitcast.refs_0_.refs_1_.refs_2_.x_ref.b_ref.dt_ref, bf16[1024,1408]{1,0:T(8,128)(2,1)} %bitcast.refs_0_.refs_1_.refs_2_.x_ref.b_ref.dt_ref, ...), custom_call_target="tpu_custom_call" | custom-call | flops 4294967296 | bytes 16777216 | tf_op jit(solution)/shard_map/pallas_call | solution.py:518
  170.1 2.3 %collective-permute-done.7.refs_2_ = bf16[256,1280]{1,0:T(8,128)(2,1)S(1)} collective-permute-done((bf16[256,1280]{1,0:T(8,128)(2,1)}, bf16[256,1280]{1,0:T(8,128)(2,1)S(1)}, u32[]{:S(2)}, u32[]{:S(2)}) %collective-permute-start.7) | collective-permute-done | bytes 655392 | tf_op jit(solution)/shard_map/ppermute | solution.py:327
  173.2 4.0 %all-to-all-start.5 = ((bf16[8,128,1408]{2,1,0:T(8,128)(2,1)}), bf16[8,128,1408]{2,1,0:T(8,128)(2,1)S(1)}, u32[]{:S(2)}, u32[]{:S(2)}) async-start(bf16[8,128,1408]{2,1,0:T(8,128)(2,1)} %bitcast.19), calls=%async_computation.5 | async-start | bytes 5767168 | tf_op jit(solution)/shard_map/all_to_all | solution.py:308
  180.0 2.3 %collective-permute-done.8 = f32[1,128]{1,0:T(1,128)S(1)} collective-permute-done((f32[1,128]{1,0:T(1,128)S(1)}, f32[1,128]{1,0:T(1,128)S(1)}, u32[]{:S(2)}, u32[]{:S(2)}) %collective-permute-start.8) | collective-permute-done | bytes 544 | tf_op jit(solution)/shard_map/ppermute | solution.py:302
  182.3 2.8 %collective-permute-start.9 = (f32[1,128]{1,0:T(1,128)S(1)}, f32[1,128]{1,0:T(1,128)S(1)}, u32[]{:S(2)}, u32[]{:S(2)}) collective-permute-start(f32[1,128]{1,0:T(1,128)S(1)} %fusion.5), channel_id=1, source_target_pairs={{0,16},{8,24},{16,0},{24,8},{32,48},{40,56},{48,32},{56,40},{64,80... | collective-permute-start | bytes 1544 | tf_op jit(solution)/shard_map/ppermute | solution.py:302
  185.1 2.3 %collective-permute-done.9 = f32[1,128]{1,0:T(1,128)S(1)} collective-permute-done((f32[1,128]{1,0:T(1,128)S(1)}, f32[1,128]{1,0:T(1,128)S(1)}, u32[]{:S(2)}, u32[]{:S(2)}) %collective-permute-start.9) | collective-permute-done | bytes 544 | tf_op jit(solution)/shard_map/ppermute | solution.py:302
  188.7 2.3 %collective-permute-done.10 = f32[1,128]{1,0:T(1,128)S(1)} collective-permute-done((f32[1,128]{1,0:T(1,128)S(1)}, f32[1,128]{1,0:T(1,128)S(1)}, u32[]{:S(2)}, u32[]{:S(2)}) %collective-permute-start.10) | collective-permute-done | bytes 544 | tf_op jit(solution)/shard_map/ppermute | solution.py:302
  190.9 2.8 %collective-permute-start.11 = (f32[1,128]{1,0:T(1,128)S(1)}, f32[1,128]{1,0:T(1,128)S(1)}, u32[]{:S(2)}, u32[]{:S(2)}) collective-permute-start(f32[1,128]{1,0:T(1,128)S(1)} %add.53), channel_id=1, source_target_pairs={{0,64},{8,72},{16,80},{24,88},{32,96},{40,104},{48,112},{56,120},{... | collective-permute-start | bytes 1544 | tf_op jit(solution)/shard_map/ppermute | solution.py:302
  193.7 2.3 %collective-permute-done.11 = f32[1,128]{1,0:T(1,128)S(1)} collective-permute-done((f32[1,128]{1,0:T(1,128)S(1)}, f32[1,128]{1,0:T(1,128)S(1)}, u32[]{:S(2)}, u32[]{:S(2)}) %collective-permute-start.11) | collective-permute-done | bytes 544 | tf_op jit(solution)/shard_map/ppermute | solution.py:302
  197.7 3.0 %shard_map.136 = (bf16[128,8192]{1,0:T(8,128)(2,1)}, bf16[128,2048]{1,0:T(8,128)(2,1)}) custom-call(bf16[256,1280]{1,0:T(8,128)(2,1)S(1)} %get-tuple-element.92.refs_0_, bf16[256,1280]{1,0:T(8,128)(2,1)} %collective-permute-done.5.refs_1_, bf16[256,1280]{1,0:T(8,128)(2,1)S(1)} %copy-done.8, bf16[256,1280]{1,0:T(8,128)(2,1)} %collective-permute-done.6.refs_3_), custom_call_target="tpu_custom_call" | custom-call | flops 128 | bytes 5242880 | tf_op jit(solution)/shard_map/pallas_call | solution.py:562
  200.6 12.2 %all-to-all-done.5.refs_0_ = bf16[8,128,1408]{2,1,0:T(8,128)(2,1)S(1)} async-done(((bf16[8,128,1408]{2,1,0:T(8,128)(2,1)}), bf16[8,128,1408]{2,1,0:T(8,128)(2,1)S(1)}, u32[]{:S(2)}, u32[]{:S(2)}) %all-to-all-start.5) | async-done | bytes 2883616 | tf_op jit(solution)/shard_map/all_to_all | solution.py:308
  (84 shorter events, 22.4 us)
Async XLA Ops:
  3.6 5.5 %copy-start.9 = (bf16[128,2048]{1,0:T(8,128)(2,1)S(1)}, bf16[128,2048]{1,0:T(8,128)(2,1)}, u32[]{:S(2)}) copy-start(bf16[128,2048]{1,0:T(8,128)(2,1)} %c_ref.1) | copy-start | bytes 1572868
  3.6 41.3 %all-to-all-start = ((bf16[8,128,1408]{2,1,0:T(8,128)(2,1)}), bf16[8,128,1408]{2,1,0:T(8,128)(2,1)}, u32[]{:S(2)}, u32[]{:S(2)}) async-start(bf16[8,128,1408]{2,1,0:T(8,128)(2,1)} %shard_map.126), calls=%async_computation | async-start | bytes 5767168 | tf_op jit(solution)/shard_map/all_to_all | solution.py:308
  9.2 3.1 %copy-start.18 = (f32[128]{0:T(128)S(1)}, f32[128]{0:T(128)}, u32[]{:S(2)}) copy-start(f32[128]{0:T(128)} %param.11) | copy-start | bytes 1540
  11.7 3.4 %collective-permute-start = (bf16[4,128,1280]{2,1,0:T(8,128)(2,1)S(1)}, bf16[4,128,1280]{2,1,0:T(8,128)(2,1)}, u32[]{:S(2)}, u32[]{:S(2)}) collective-permute-start(bf16[4,128,1280]{2,1,0:T(8,128)(2,1)S(1)} %get-tuple-element.62), channel_id=1, source_target_pairs={{0,1},{1,0},{2,3},{3,2},{4,5},{5,4},{6,7},{7,6},{8,9},{9,8},{10,11... | collective-permute-start | bytes 3932168 | tf_op jit(solution)/shard_map/ppermute | solution.py:314
  44.9 18.1 %collective-permute-start.1 = (bf16[256,1280]{1,0:T(8,128)(2,1)}, bf16[256,1280]{1,0:T(8,128)(2,1)}, u32[]{:S(2)}, u32[]{:S(2)}) collective-permute-start(bf16[256,1280]{1,0:T(8,128)(2,1)} %get-tuple-element.70), channel_id=1, source_target_pairs={{0,2},{1,3},{2,4},{3,5},{4,6},{5,7},{6,0},{7,1},{8,10},{9,11},{10,... | collective-permute-start | bytes 1966088 | tf_op jit(solution)/shard_map/ppermute | solution.py:327
  45.5 17.6 %collective-permute-start.2 = (bf16[256,1280]{1,0:T(8,128)(2,1)}, bf16[256,1280]{1,0:T(8,128)(2,1)}, u32[]{:S(2)}, u32[]{:S(2)}) collective-permute-start(bf16[256,1280]{1,0:T(8,128)(2,1)} %get-tuple-element.72), channel_id=1, source_target_pairs={{0,6},{1,7},{2,0},{3,1},{4,2},{5,3},{6,4},{7,5},{8,14},{9,15},{10,... | collective-permute-start | bytes 1966088 | tf_op jit(solution)/shard_map/ppermute | solution.py:327
  55.8 25.4 %copy-start.2 = (bf16[128,1024]{1,0:T(8,128)(2,1)S(1)}, bf16[128,1024]{1,0:T(8,128)(2,1)}, u32[]{:S(2)}) copy-start(bf16[128,1024]{1,0:T(8,128)(2,1)} %and_convert_fusion.refs_4_.refs_1_.expand_ref) | copy-start | bytes 786436
  55.8 25.4 %all-to-all-start.1 = ((f32[16,16,1152]{2,1,0:T(8,128)}), f32[16,16,1152]{2,1,0:T(8,128)S(1)}, u32[]{:S(2)}, u32[]{:S(2)}) async-start(f32[16,16,1152]{2,1,0:T(8,128)} %bitcast.18), calls=%async_computation.1 | async-start | bytes 2359296 | tf_op jit(solution)/shard_map/all_to_all | solution.py:296
  63.0 24.3 %copy-start.11 = (bf16[1024,128]{1,0:T(8,128)(2,1)S(1)}, bf16[1024,128]{1,0:T(8,128)(2,1)}, u32[]{:S(2)}) copy-start(bf16[1024,128]{1,0:T(8,128)(2,1)} %get-tuple-element.68.refs_0_.growth_ref) | copy-start | bytes 786436
  63.0 19.5 %collective-permute-start.3 = (bf16[256,1280]{1,0:T(8,128)(2,1)}, bf16[256,1280]{1,0:T(8,128)(2,1)}, u32[]{:S(2)}, u32[]{:S(2)}) collective-permute-start(bf16[256,1280]{1,0:T(8,128)(2,1)} %copy-done.16), channel_id=1, source_target_pairs={{0,4},{1,5},{2,6},{3,7},{4,0},{5,1},{6,2},{7,3},{8,12},{9,13},{10,... | collective-permute-start | bytes 1966088 | tf_op jit(solution)/shard_map/ppermute | solution.py:327
  82.5 43.7 %copy-start.12 = (f32[16,1024]{1,0:T(8,128)}, f32[16,1024]{1,0:T(8,128)S(1)}, u32[]{:S(2)}) copy-start(f32[16,1024]{1,0:T(8,128)S(1)} %get-tuple-element.97.decay_ref) | copy-start | bytes 196612
  82.5 21.7 %all-to-all-start.2 = ((f32[16,16,1024]{2,1,0:T(8,128)}), f32[16,16,1024]{2,1,0:T(8,128)S(1)}, u32[]{:S(2)}, u32[]{:S(2)}) async-start(f32[16,16,1024]{2,1,0:T(8,128)} %get-tuple-element.85), calls=%async_computation.2 | async-start | bytes 2097152 | tf_op jit(solution)/shard_map/all_to_all | solution.py:296
  94.1 10.0 %copy-start.14 = (f32[4,1,1024]{2,1,0:T(1,128)}, f32[4,1,1024]{2,1,0:T(1,128)S(1)}, u32[]{:S(2)}) copy-start(f32[4,1,1024]{2,1,0:T(1,128)S(1)} %get-tuple-element.104.decay_ref) | copy-start | bytes 49156
  104.1 7.3 %copy-start.19 = (f32[128]{0:T(128)S(1)}, f32[128]{0:T(128)}, u32[]{:S(2)}) copy-start(f32[128]{0:T(128)} %param.12) | copy-start | bytes 1540
  104.1 7.7 %copy-start.15 = (f32[4,1,1024]{2,1,0:T(1,128)S(1)}, f32[4,1,1024]{2,1,0:T(1,128)}, u32[]{:S(2)}) copy-start(f32[4,1,1024]{2,1,0:T(1,128)} %get-tuple-element.82.decay_ref) | copy-start | bytes 49156
  104.2 22.0 %all-to-all-start.3 = ((f32[16,16,1024]{2,1,0:T(8,128)}), f32[16,16,1024]{2,1,0:T(8,128)S(1)}, u32[]{:S(2)}, u32[]{:S(2)}) async-start(f32[16,16,1024]{2,1,0:T(8,128)} %bitcast.20), calls=%async_computation.3 | async-start | bytes 2097152 | tf_op jit(solution)/shard_map/all_to_all | solution.py:296
  111.6 11.2 %copy-start.13 = (f32[1,1024]{1,0:T(1,128)}, f32[1,1024]{1,0:T(1,128)S(1)}, u32[]{:S(2)}) copy-start(f32[1,1024]{1,0:T(1,128)S(1)} %broadcast_in_dim_reshape.3.skip_ref) | copy-start | bytes 12292
  111.9 11.0 %copy-start.3 = (bf16[1024,128]{1,0:T(8,128)(2,1)}, bf16[1024,128]{1,0:T(8,128)(2,1)S(1)}, u32[]{:S(2)}) copy-start(bf16[1024,128]{1,0:T(8,128)(2,1)S(1)} %compare_convert_fusion.collect_ref) | copy-start | bytes 786436
  111.9 1.3 copy-start.6
  126.2 5.9 %collective-permute-start.4 = (bf16[4,128,1280]{2,1,0:T(8,128)(2,1)}, bf16[4,128,1280]{2,1,0:T(8,128)(2,1)}, u32[]{:S(2)}, u32[]{:S(2)}) collective-permute-start(bf16[4,128,1280]{2,1,0:T(8,128)(2,1)} %get-tuple-element.91), channel_id=1, source_target_pairs={{0,1},{1,0},{2,3},{3,2},{4,5},{5,4},{6,7},{7,6},{8,9},{9,8},{10,11... | collective-permute-start | bytes 3932168 | tf_op jit(solution)/shard_map/ppermute | solution.py:314
  127.2 13.0 %copy-start = (f32[256,1152]{1,0:T(8,128)S(1)}, f32[256,1152]{1,0:T(8,128)}, u32[]{:S(2)}) copy-start(f32[256,1152]{1,0:T(8,128)} %get-tuple-element.83.state_ref) | copy-start | bytes 3538948
  127.3 29.6 %all-to-all-start.4 = ((f32[16,16,1024]{2,1,0:T(8,128)}), f32[16,16,1024]{2,1,0:T(8,128)}, u32[]{:S(2)}, u32[]{:S(2)}) async-start(f32[16,16,1024]{2,1,0:T(8,128)} %copy-done.1), calls=%async_computation.4 | async-start | bytes 2097152 | tf_op jit(solution)/shard_map/all_to_all | solution.py:296
  136.2 18.4 %collective-permute-start.5 = (bf16[256,1280]{1,0:T(8,128)(2,1)}, bf16[256,1280]{1,0:T(8,128)(2,1)}, u32[]{:S(2)}, u32[]{:S(2)}) collective-permute-start(bf16[256,1280]{1,0:T(8,128)(2,1)} %get-tuple-element.93), channel_id=1, source_target_pairs={{0,2},{1,3},{2,4},{3,5},{4,6},{5,7},{6,0},{7,1},{8,10},{9,11},{10,... | collective-permute-start | bytes 1966088 | tf_op jit(solution)/shard_map/ppermute | solution.py:327
  136.2 18.4 %collective-permute-start.6 = (bf16[256,1280]{1,0:T(8,128)(2,1)}, bf16[256,1280]{1,0:T(8,128)(2,1)}, u32[]{:S(2)}, u32[]{:S(2)}) collective-permute-start(bf16[256,1280]{1,0:T(8,128)(2,1)} %get-tuple-element.95), channel_id=1, source_target_pairs={{0,6},{1,7},{2,0},{3,1},{4,2},{5,3},{6,4},{7,5},{8,14},{9,15},{10,... | collective-permute-start | bytes 1966088 | tf_op jit(solution)/shard_map/ppermute | solution.py:327
  154.6 17.8 %collective-permute-start.7 = (bf16[256,1280]{1,0:T(8,128)(2,1)}, bf16[256,1280]{1,0:T(8,128)(2,1)S(1)}, u32[]{:S(2)}, u32[]{:S(2)}) collective-permute-start(bf16[256,1280]{1,0:T(8,128)(2,1)} %get-tuple-element.99), channel_id=1, source_target_pairs={{0,4},{1,5},{2,6},{3,7},{4,0},{5,1},{6,2},{7,3},{8,12},{9,13},{10,... | collective-permute-start | bytes 1966088 | tf_op jit(solution)/shard_map/ppermute | solution.py:327
  173.2 4.6 %copy-start.17 = (f32[1,1024]{1,0:T(1,128)S(1)}, f32[1,1024]{1,0:T(1,128)}, u32[]{:S(2)}) copy-start(f32[1,1024]{1,0:T(1,128)} %get-tuple-element.114) | copy-start | bytes 12292
  173.2 5.4 %copy-start.20 = (f32[1,128]{1,0:T(1,128)S(1)}, f32[1,128]{1,0:T(1,128)}, u32[]{:S(2)}) copy-start(f32[1,128]{1,0:T(1,128)} %get-tuple-element.113) | copy-start | bytes 1540
  173.2 39.7 %all-to-all-start.5 = ((bf16[8,128,1408]{2,1,0:T(8,128)(2,1)}), bf16[8,128,1408]{2,1,0:T(8,128)(2,1)S(1)}, u32[]{:S(2)}, u32[]{:S(2)}) async-start(bf16[8,128,1408]{2,1,0:T(8,128)(2,1)} %bitcast.19), calls=%async_computation.5 | async-start | bytes 5767168 | tf_op jit(solution)/shard_map/all_to_all | solution.py:308
  178.7 3.6 %collective-permute-start.8 = (f32[1,128]{1,0:T(1,128)S(1)}, f32[1,128]{1,0:T(1,128)S(1)}, u32[]{:S(2)}, u32[]{:S(2)}) collective-permute-start(f32[1,128]{1,0:T(1,128)S(1)} %fusion.4), channel_id=1, source_target_pairs={{0,8},{8,0},{16,24},{24,16},{32,40},{40,32},{48,56},{56,48},{64,72... | collective-permute-start | bytes 1544 | tf_op jit(solution)/shard_map/ppermute | solution.py:302
  182.3 5.1 %collective-permute-start.9 = (f32[1,128]{1,0:T(1,128)S(1)}, f32[1,128]{1,0:T(1,128)S(1)}, u32[]{:S(2)}, u32[]{:S(2)}) collective-permute-start(f32[1,128]{1,0:T(1,128)S(1)} %fusion.5), channel_id=1, source_target_pairs={{0,16},{8,24},{16,0},{24,8},{32,48},{40,56},{48,32},{56,40},{64,80... | collective-permute-start | bytes 1544 | tf_op jit(solution)/shard_map/ppermute | solution.py:302
  187.4 3.5 %collective-permute-start.10 = (f32[1,128]{1,0:T(1,128)S(1)}, f32[1,128]{1,0:T(1,128)S(1)}, u32[]{:S(2)}, u32[]{:S(2)}) collective-permute-start(f32[1,128]{1,0:T(1,128)S(1)} %add.52), channel_id=1, source_target_pairs={{0,32},{8,40},{16,48},{24,56},{32,0},{40,8},{48,16},{56,24},{64,96... | collective-permute-start | bytes 1544 | tf_op jit(solution)/shard_map/ppermute | solution.py:302
  190.9 5.0 %collective-permute-start.11 = (f32[1,128]{1,0:T(1,128)S(1)}, f32[1,128]{1,0:T(1,128)S(1)}, u32[]{:S(2)}, u32[]{:S(2)}) collective-permute-start(f32[1,128]{1,0:T(1,128)S(1)} %add.53), channel_id=1, source_target_pairs={{0,64},{8,72},{16,80},{24,88},{32,96},{40,104},{48,112},{56,120},{... | collective-permute-start | bytes 1544 | tf_op jit(solution)/shard_map/ppermute | solution.py:302
  (7 other events, 6.8 us)
